TPU v7x, 32 devices: a whole 2x2x4 slice. The times are simulated.
32 devices in a mesh: dp: 4 (over x, core), mp: 8 (over z, y).
Axes of the slice: x: 2, y: 2, z: 4, core: 2. Of those that a mesh axis runs over, the one named last changes fastest.
Arguments:
- fast_in: bfloat16 [128, 8, 4, 256], P(None, 'mp', 'dp'), may hold values from -6 to 6
- slow_in: bfloat16 [1024, 2, 4, 256], P('mp', None, 'dp'), may hold values from -6 to 6
- fast_cot: bfloat16 [128, 8, 4, 256], P(None, 'mp', 'dp'), may hold values from -6 to 6
- slow_cot: bfloat16 [1024, 2, 4, 256], P('mp', None, 'dp'), may hold values from -6 to 6
- crop_tiles: int32 [4], P('dp'), may hold values from 10 to 16, as said below
- owner: int32 [7591], replicated, may hold values from 0 to 31, as said below
- master: float32 [15232, 128], P(('dp', 'mp')), as said below
- moment_one: float32 [15232, 128], P(('dp', 'mp')), as said below
- moment_two: float32 [15232, 128], P(('dp', 'mp')), as said below
Outputs:
- fast_out: float32 [128, 8, 4, 256], P(None, 'mp', 'dp')
- slow_out: float32 [1024, 2, 4, 256], P('mp', None, 'dp')
- fast_grad: float32 [128, 8, 4, 256], P(None, 'mp', 'dp')
- slow_grad: float32 [1024, 2, 4, 256], P('mp', None, 'dp')
- new_master: float32 [15232, 128], P(('dp', 'mp'))
- new_moment_one: float32 [15232, 128], P(('dp', 'mp'))
- new_moment_two: float32 [15232, 128], P(('dp', 'mp'))
- new_weights: bfloat16 [15232, 128], P(('dp', 'mp'))
Inputs may be any that keep to these rules, and one draw needn't show every extreme that they name: `crop_tiles`: each value is 10, 14 or 16. `owner`: blocks of 128 flattened parameters; each device owns one contiguous run of 1 to 476 blocks, one device exactly 476; runs follow a drawn order of devices. `master`: row j of device d's 476 rows holds the j-th block d owns; other rows are ignored. `moment_one`: rows laid out as master's. `moment_two`: positive; rows laid out as master's.
All inputs are finite; a program needn't handle non-finite values.
Results may differ from a plain program's by a relative error of at most 0.012.
The roundings to bfloat16 on the way count: a program that leaves them out, or rounds other values in their place, can miss the bound.
Values may be sent and summed in bfloat16 or wider, within the bound.
A program may use at most 128 MiB of HBM per device.

v0:
```python
import math

import jax
import jax.numpy as jnp
from jax import lax
from jax.sharding import PartitionSpec as P

C_FAST = 128
B_FAST = 32
C_SLOW = 1024
B_SLOW = 256
C_LAT = 256
TILE = 16
BLK = 128
STEP = 10
NBLK = 7591


norm_eps = 1e-05
beta_first = 0.5
beta_second = 0.5
adam_eps = 1e-08
decay_rate = 0.05


def from_behind(block, axis, distance):
    devices = range(lax.axis_size(axis))
    route = [(i - distance, i) for i in devices if i - distance in devices]
    return lax.ppermute(block, axis, route)


def for_sending(shard):

    def short(part):
        return part.astype(jnp.bfloat16) if part.dtype == jnp.float32 else part

    return jax.tree.map(short, shard)


def segment_list():
    mats = [
        ("fast_one", (B_FAST, 3 * C_FAST)),
        ("fast_two", (B_FAST, B_FAST)),
        ("fast_three", (C_FAST, B_FAST)),
        ("lateral", (C_LAT, 5 * C_FAST)),
        ("slow_one", (B_SLOW, C_SLOW + C_LAT)),
        ("slow_two", (B_SLOW, 3 * B_SLOW)),
        ("slow_three", (C_SLOW, B_SLOW)),
    ]
    norms = []
    for label, width in (
        ("fast_one", B_FAST),
        ("fast_two", B_FAST),
        ("fast_three", C_FAST),
        ("lateral", C_LAT),
        ("slow_one", B_SLOW),
        ("slow_two", B_SLOW),
        ("slow_three", C_SLOW),
    ):
        norms.append(("gain_" + label, (width,)))
        norms.append(("bias_" + label, (width,)))
    return mats + norms


def unpack(flat):
    result = {}
    offset = 0
    for label, shape in segment_list():
        size = math.prod(shape)
        result[label] = flat[offset : offset + size].reshape(shape)
        offset += size
    return result


def element_rates(element):
    rate = jnp.zeros(element.shape, jnp.float32)
    decay = jnp.zeros(element.shape, jnp.float32)
    offset = 0
    for label, shape in segment_list():
        size = math.prod(shape)
        inside = (element >= offset) & (element < offset + size)
        if len(shape) == 2:
            rate = jnp.where(inside, 0.5 / math.sqrt(shape[1]), rate)
            decay = jnp.where(inside, decay_rate, decay)
        else:
            rate = jnp.where(inside, 0.2, rate)
        offset += size
    return (rate, decay)


def block_positions(owner, devices, slots):
    onehot = (owner[:, None] == jnp.arange(devices, dtype=jnp.int32)[None, :]).astype(jnp.int32)
    before = jnp.cumsum(onehot, axis=0) - onehot
    return (owner * slots + jnp.sum(before * onehot, axis=1)).astype(jnp.int32)


def clip_mask(crop_tiles, times):
    spot = jnp.arange(TILE * TILE, dtype=jnp.int32)
    inside = ((spot // TILE)[None, :] < crop_tiles[:, None]) & (
        (spot % TILE)[None, :] < crop_tiles[:, None]
    )
    living = (times[:, None] >= 0) & (crop_tiles[None, :] > 0)
    return (living[:, :, None] & inside[None]).astype(jnp.float32)


def adam(weight, grad, first, second, rate, decay):
    first = beta_first * first + (1.0 - beta_first) * grad
    second = beta_second * second + (1.0 - beta_second) * grad * grad
    lift_one = 1.0 - beta_first**STEP
    lift_two = 1.0 - beta_second**STEP
    update = first / lift_one / (jnp.sqrt(second / lift_two) + adam_eps)
    return (first, second, weight - rate * (update + decay * weight))


def contract_last(left, right):
    return lax.dot_general(
        left, right, (((1,), (1,)), ((), ())), preferred_element_type=jnp.float32
    )


def contract_first(left, right):
    return lax.dot_general(
        left, right, (((0,), (0,)), ((), ())), preferred_element_type=jnp.float32
    )


def fast_total(parts):
    return lax.psum(parts, ("dp", "mp"))


def slow_total(parts):
    return lax.psum(parts, "dp")


def norm_forward(value, mask, gain, bias, extra, total):
    sums = total((jnp.sum(value * mask, 1), jnp.sum(value * value * mask, 1), jnp.sum(mask)))
    mean = sums[0] / sums[2]
    scale = lax.rsqrt(sums[1] / sums[2] - mean * mean + norm_eps)
    normed = (value - mean[:, None]) * scale[:, None]
    pre = gain[:, None] * normed + bias[:, None] + extra
    return (jax.nn.gelu(pre) * mask, (normed, scale, pre, sums[2]))


def norm_backward(incoming, mask, gain, kept, total):
    normed, scale, pre, count = kept
    pre_grad = jax.vjp(jax.nn.gelu, pre)[1](incoming * mask)[0]
    gain_part = jnp.sum(pre_grad * normed, 1)
    bias_part = jnp.sum(pre_grad, 1)
    sums = total((gain_part, bias_part))
    normed_grad = pre_grad * gain[:, None]
    shared = gain[:, None] * (sums[1][:, None] + normed * sums[0][:, None]) / count
    raw_grad = scale[:, None] * (normed_grad - mask * shared)
    return (raw_grad, pre_grad, gain_part, bias_part)


def frame_window(act, frames):
    shaped = act.reshape(act.shape[0], frames, -1)
    blank = jnp.zeros_like(shaped[:, :1])
    return jnp.concatenate(
        [
            jnp.concatenate([blank, shaped[:, :-1]], 1),
            shaped,
            jnp.concatenate([shaped[:, 1:], blank], 1),
        ],
        0,
    ).reshape(3 * act.shape[0], -1)


def window_return(grad, width, frames):
    taps = grad.reshape(3, width, frames, -1)
    zero_frame = jnp.zeros_like(taps[0][:, :1])
    summed = (
        taps[1]
        + jnp.concatenate([taps[0][:, 1:], zero_frame], 1)
        + jnp.concatenate([zero_frame, taps[2][:, :-1]], 1)
    )
    return summed.reshape(width, -1)


def spread_sum(weight, inputs):
    block = lax.slice_in_dim(
        weight, 0, weight.shape[0] // lax.axis_size("mp") * lax.axis_size("mp"), axis=0
    )
    return lax.psum_scatter(
        jnp.dot(block, inputs, preferred_element_type=jnp.float32),
        "mp",
        scatter_dimension=0,
        tiled=True,
    )


def fold_back(grad_rows, weight, inputs):
    piece = jax.tree.map(lambda a: lax.all_gather(a, "mp", axis=0, tiled=True), grad_rows)
    start = jnp.int32(0)
    weight_grad = jnp.zeros(weight.shape, jnp.float32)
    input_grad = jnp.zeros((weight.shape[1], inputs.shape[1]), jnp.float32)
    product = contract_last(piece, inputs)
    weight_grad = lax.dynamic_update_slice_in_dim(weight_grad, product, start, 0)
    block = lax.dynamic_slice_in_dim(weight, start, piece.shape[0], 0)
    input_grad = input_grad + contract_first(block, piece)
    return (weight_grad, input_grad)


def local(fast_in, slow_in, fast_cot, slow_cot, crop_tiles, owner, master, moment_one, moment_two):
    devices = lax.axis_size(("dp", "mp"))
    slots = master.shape[0]
    ranks = lax.axis_size("mp")
    mp_rank = lax.axis_index("mp")
    position = block_positions(owner, devices, slots)
    gathered = lax.all_gather(master.astype(jnp.bfloat16), ("dp", "mp"), axis=0, tiled=True)
    params = unpack(gathered[position].reshape(-1))
    gains = {label: value.astype(jnp.float32) for label, value in params.items() if value.ndim == 1}
    fast_width = fast_in.shape[0]
    columns = fast_in.shape[2] * fast_in.shape[3]
    slow_share = slow_in.shape[0]
    slow_frames = slow_in.shape[1]
    lat_share = C_LAT // ranks
    neck_share = B_SLOW // ranks

    def owned_part(vector, share):
        return lax.dynamic_slice_in_dim(vector, mp_rank * share, share)

    def place(vector, share, width):
        return lax.dynamic_update_slice_in_dim(
            jnp.zeros((width,), jnp.float32), vector, mp_rank * share, 0
        )

    fast_mask = clip_mask(crop_tiles, mp_rank[None]).reshape(-1)
    slow_mask = clip_mask(crop_tiles, 4 * jnp.arange(slow_frames, dtype=jnp.int32)).reshape(-1)
    fast_masked = (fast_in.reshape(fast_width, columns).astype(jnp.float32) * fast_mask).astype(
        jnp.bfloat16
    )
    offsets = (2, 1, -1, -2)
    rims = {}
    for offset in offsets:
        rims[offset] = from_behind(fast_masked, "mp", offset)
    window = jnp.concatenate([rims[1], fast_masked, rims[-1]], 0)
    first_raw = jnp.dot(params["fast_one"], window, preferred_element_type=jnp.float32)
    first_out, first_kept = norm_forward(
        first_raw, fast_mask, gains["gain_fast_one"], gains["bias_fast_one"], 0.0, fast_total
    )
    first_act = first_out.astype(jnp.bfloat16)
    second_raw = jnp.dot(params["fast_two"], first_act, preferred_element_type=jnp.float32)
    second_out, second_kept = norm_forward(
        second_raw, fast_mask, gains["gain_fast_two"], gains["bias_fast_two"], 0.0, fast_total
    )
    second_act = second_out.astype(jnp.bfloat16)
    third_raw = jnp.dot(params["fast_three"], second_act, preferred_element_type=jnp.float32)
    fast_out, third_kept = norm_forward(
        third_raw,
        fast_mask,
        gains["gain_fast_three"],
        gains["bias_fast_three"],
        fast_masked.astype(jnp.float32),
        fast_total,
    )
    lat_weight = params["lateral"]
    wide_window = jnp.concatenate([rims[2], rims[1], fast_masked, rims[-1], rims[-2]], 0)
    lateral_full = jnp.dot(lat_weight, wide_window, preferred_element_type=jnp.float32).astype(
        jnp.bfloat16
    )
    received = lax.all_to_all(lateral_full[:, None], "mp", split_axis=0, concat_axis=1, tiled=True)
    lateral_raw = received.reshape(lat_share, slow_frames, 4, columns)[:, :, 0].reshape(
        lat_share, -1
    )
    lat_out, lat_kept = norm_forward(
        lateral_raw.astype(jnp.float32),
        slow_mask,
        owned_part(gains["gain_lateral"], lat_share),
        owned_part(gains["bias_lateral"], lat_share),
        0.0,
        slow_total,
    )
    lat_act = lat_out.astype(jnp.bfloat16)
    slow_masked = (slow_in.reshape(slow_share, -1).astype(jnp.float32) * slow_mask).astype(
        jnp.bfloat16
    )
    joined = jnp.concatenate([slow_masked, lat_act], 0)
    one_weight = params["slow_one"]
    one_local = jnp.concatenate(
        [
            lax.dynamic_slice_in_dim(one_weight, mp_rank * slow_share, slow_share, 1),
            lax.dynamic_slice_in_dim(one_weight, C_SLOW + mp_rank * lat_share, lat_share, 1),
        ],
        1,
    )
    one_raw = spread_sum(one_local, joined)
    one_out, one_kept = norm_forward(
        one_raw,
        slow_mask,
        owned_part(gains["gain_slow_one"], neck_share),
        owned_part(gains["bias_slow_one"], neck_share),
        0.0,
        slow_total,
    )
    one_act = one_out.astype(jnp.bfloat16)
    slow_window = frame_window(one_act, slow_frames)
    two_local = lax.dynamic_slice_in_dim(
        params["slow_two"].reshape(B_SLOW, 3, B_SLOW), mp_rank * neck_share, neck_share, 2
    ).reshape(B_SLOW, 3 * neck_share)
    two_raw = spread_sum(two_local, slow_window)
    two_out, two_kept = norm_forward(
        two_raw,
        slow_mask,
        owned_part(gains["gain_slow_two"], neck_share),
        owned_part(gains["bias_slow_two"], neck_share),
        0.0,
        slow_total,
    )
    two_act = two_out.astype(jnp.bfloat16)
    three_local = lax.dynamic_slice_in_dim(
        params["slow_three"], mp_rank * neck_share, neck_share, 1
    )
    three_raw = spread_sum(three_local, two_act)
    three_gain = owned_part(gains["gain_slow_three"], slow_share)
    slow_out, three_kept = norm_forward(
        three_raw,
        slow_mask,
        three_gain,
        owned_part(gains["bias_slow_three"], slow_share),
        slow_masked.astype(jnp.float32),
        slow_total,
    )
    three_back, three_pre, gain_three, bias_three = norm_backward(
        slow_cot.reshape(slow_share, -1).astype(jnp.float32),
        slow_mask,
        three_gain,
        three_kept,
        slow_total,
    )
    three_wgrad, two_grad = fold_back(three_back.astype(jnp.bfloat16), three_local, two_act)
    three_full = lax.dynamic_update_slice_in_dim(
        jnp.zeros((C_SLOW, B_SLOW), jnp.float32), three_wgrad, mp_rank * neck_share, 1
    )
    two_back, two_pre, gain_two, bias_two = norm_backward(
        two_grad, slow_mask, owned_part(gains["gain_slow_two"], neck_share), two_kept, slow_total
    )
    two_wgrad, window_grad = fold_back(two_back.astype(jnp.bfloat16), two_local, slow_window)
    one_grad = window_return(window_grad, neck_share, slow_frames)
    one_back, one_pre, gain_one, bias_one = norm_backward(
        one_grad, slow_mask, owned_part(gains["gain_slow_one"], neck_share), one_kept, slow_total
    )
    one_wgrad, joined_grad = fold_back(one_back.astype(jnp.bfloat16), one_local, joined)
    slow_grad = slow_mask * (three_pre + joined_grad[:slow_share])
    lat_incoming = joined_grad[slow_share:]
    one_full = jnp.zeros((B_SLOW, C_SLOW + C_LAT), jnp.float32)
    one_full = lax.dynamic_update_slice_in_dim(
        one_full, one_wgrad[:, :slow_share], mp_rank * slow_share, 1
    )
    one_full = lax.dynamic_update_slice_in_dim(
        one_full, one_wgrad[:, slow_share:], C_SLOW + mp_rank * lat_share, 1
    )
    two_full = lax.dynamic_update_slice_in_dim(
        jnp.zeros((B_SLOW, 3, B_SLOW), jnp.float32),
        two_wgrad.reshape(B_SLOW, 3, neck_share),
        mp_rank * neck_share,
        2,
    )
    slow_grads = {
        "slow_one": one_full,
        "slow_two": two_full,
        "slow_three": three_full,
        "gain_slow_one": place(gain_one, neck_share, B_SLOW),
        "bias_slow_one": place(bias_one, neck_share, B_SLOW),
        "gain_slow_two": place(gain_two, neck_share, B_SLOW),
        "bias_slow_two": place(bias_two, neck_share, B_SLOW),
        "gain_slow_three": place(gain_three, slow_share, C_SLOW),
        "bias_slow_three": place(bias_three, slow_share, C_SLOW),
    }
    lat_back, lat_pre, gain_lat, bias_lat = norm_backward(
        lat_incoming, slow_mask, owned_part(gains["gain_lateral"], lat_share), lat_kept, slow_total
    )
    lat_back = lat_back.astype(jnp.bfloat16).reshape(lat_share, slow_frames, columns)
    tap_grads = {}
    padding = jnp.zeros((lat_share, slow_frames, 3, columns), jnp.bfloat16)
    send_full = jnp.concatenate([lat_back[:, :, None], padding], 2).reshape(
        lat_share, ranks, columns
    )
    back_full = lax.all_to_all(send_full, "mp", split_axis=1, concat_axis=0, tiled=True)[:, 0]
    lat_wgrad = contract_last(back_full, wide_window)
    wide_grad = contract_first(lat_weight, back_full).reshape(5, fast_width, columns)
    own_extra = wide_grad[2]
    tap_grads = {2: wide_grad[0], 1: wide_grad[1], -1: wide_grad[3], -2: wide_grad[4]}
    third_back, third_pre, gain_fast_three, bias_fast_three = norm_backward(
        fast_cot.reshape(fast_width, -1).astype(jnp.float32),
        fast_mask,
        gains["gain_fast_three"],
        third_kept,
        fast_total,
    )
    third_back = third_back.astype(jnp.bfloat16)
    third_wgrad = contract_last(third_back, second_act)
    second_grad = contract_first(params["fast_three"], third_back)
    second_back, second_pre, gain_fast_two, bias_fast_two = norm_backward(
        second_grad, fast_mask, gains["gain_fast_two"], second_kept, fast_total
    )
    second_back = second_back.astype(jnp.bfloat16)
    second_wgrad = contract_last(second_back, first_act)
    first_grad = contract_first(params["fast_two"], second_back)
    first_back, first_pre, gain_fast_one, bias_fast_one = norm_backward(
        first_grad, fast_mask, gains["gain_fast_one"], first_kept, fast_total
    )
    first_back = first_back.astype(jnp.bfloat16)
    first_wgrad = contract_last(first_back, window)
    window_back = contract_first(params["fast_one"], first_back).reshape(3, fast_width, columns)
    tap_grads[1] = tap_grads.get(1, 0.0) + window_back[0]
    tap_grads[-1] = tap_grads.get(-1, 0.0) + window_back[2]
    masked_grad = window_back[1] + own_extra + third_pre
    for offset in offsets:
        masked_grad = masked_grad + from_behind(for_sending(tap_grads[offset]), "mp", -offset)
    fast_grad = masked_grad * fast_mask
    grads = {
        "fast_one": first_wgrad,
        "fast_two": second_wgrad,
        "fast_three": third_wgrad,
        "lateral": lat_wgrad,
        "gain_fast_one": gain_fast_one,
        "bias_fast_one": bias_fast_one,
        "gain_fast_two": gain_fast_two,
        "bias_fast_two": bias_fast_two,
        "gain_fast_three": gain_fast_three,
        "bias_fast_three": bias_fast_three,
        "gain_lateral": place(gain_lat, lat_share, C_LAT),
        "bias_lateral": place(bias_lat, lat_share, C_LAT),
    }
    grads.update(slow_grads)
    flat_grad = jnp.concatenate([grads[label].reshape(-1) for label, shape in segment_list()])
    packed = (
        jnp.zeros((devices * slots, BLK), jnp.float32)
        .at[position]
        .set(flat_grad.reshape(NBLK, BLK))
    )
    owned = lax.psum_scatter(packed, ("dp", "mp"), scatter_dimension=0, tiled=True)
    device_rank = lax.axis_index(("dp", "mp"))
    block_of = (
        jnp.zeros((devices * slots,), jnp.int32).at[position].set(jnp.arange(NBLK, dtype=jnp.int32))
    )
    living = jnp.zeros((devices * slots,), jnp.float32).at[position].set(1.0)
    my_blocks = lax.dynamic_slice_in_dim(block_of, device_rank * slots, slots)
    my_living = lax.dynamic_slice_in_dim(living, device_rank * slots, slots)[:, None]
    element = my_blocks[:, None] * BLK + jnp.arange(BLK, dtype=jnp.int32)[None, :]
    rate, decay = element_rates(element)
    new_first, new_second, new_weight = adam(master, owned, moment_one, moment_two, rate, decay)
    new_weight = new_weight * my_living
    return (
        fast_out.reshape(fast_in.shape),
        slow_out.reshape(slow_in.shape),
        fast_grad.reshape(fast_in.shape),
        slow_grad.reshape(slow_in.shape),
        new_weight,
        new_first * my_living,
        new_second * my_living,
        new_weight.astype(jnp.bfloat16),
    )


def solution(mesh):
    return jax.shard_map(
        local,
        mesh=mesh,
        in_specs=(
            P(None, "mp", "dp", None),
            P("mp", None, "dp", None),
            P(None, "mp", "dp", None),
            P("mp", None, "dp", None),
            P("dp"),
            P(),
            P(("dp", "mp"), None),
            P(("dp", "mp"), None),
            P(("dp", "mp"), None),
        ),
        out_specs=(
            P(None, "mp", "dp", None),
            P("mp", None, "dp", None),
            P(None, "mp", "dp", None),
            P("mp", None, "dp", None),
            P(("dp", "mp"), None),
            P(("dp", "mp"), None),
            P(("dp", "mp"), None),
            P(("dp", "mp"), None),
        ),
        check_vma=False,
    )
```

profile of v0, /device:TPU:25, one launch (start us, length us, event | category | flops | bytes accessed | tf_op | source)
XLA Modules:
  0.0 1030.1 jit_solution(11775890240768970642)
XLA Ops:
  7.2 1.6 convert_bitcast_fusion
  10.4 3.0 collective-permute-start.1
  13.4 2.2 collective-permute-start
  17.0 4.0 collective-permute-start.3
  22.2 9.5 reduce-window.6
  35.5 37.5 %all-gather.6.cloned.1.call-done = bf16[32,476,128]{2,1,0:T(8,128)(2,1)} async-done(((bf16[1,476,128]{2,1,0:T(8,128)(2,1)}), bf16[32,476,128]{2,1,0:T(8,128)(2,1)}) %all-gather.6.cloned.1.call-update) | async-done | bytes 3899408 | tf_op jit(solution)/shard_map/all_gather | solution.py:210
  73.1 5.9 reshape.480
  78.9 15.1 %gather_fusion = bf16[7591,128]{1,0:T(8,128)(2,1)S(1)} fusion(bf16[15232,128]{1,0:T(8,128)(2,1)} %reshape.480, s32[8192]{0:T(1024)S(1)} %pad_clamp_fusion), kind=kCustom, calls=%fused_computation | custom fusion | bytes 3916956 | tf_op jit(solution)/shard_map/gather | solution.py:211
  96.5 5.4 all-to-all-start
  102.8 1.6 reshape.409
  106.5 6.5 all-reduce.21
  117.5 57.2 %reduce-scatter.6.cloned.1.call-done = f32[32,512]{1,0:T(8,128)} async-done(((f32[256,512]{1,0:T(8,128)}), f32[32,512]{1,0:T(8,128)}) %reduce-scatter.6.cloned.1.call-update) | async-done | bytes 65552 | tf_op jit(solution)/shard_map/reduce_scatter | solution.py:184
  175.7 7.7 all-reduce.20
  188.1 58.0 %reduce-scatter.8.cloned.1.call-done = f32[32,512]{1,0:T(8,128)} async-done(((f32[256,512]{1,0:T(8,128)}), f32[32,512]{1,0:T(8,128)}) %reduce-scatter.8.cloned.1.call-update) | async-done | bytes 65552 | tf_op jit(solution)/shard_map/reduce_scatter | solution.py:184
  247.1 7.6 all-reduce.19
  255.3 2.8 fusion.81
  258.3 35.9 %scatter_custom_fusion = s32[15232]{0:T(1024)S(1)} fusion(s32[7591]{0:T(1024)} %copy-done.26, s32[7591]{0:T(1024)S(1)} %iota.29, s32[]{:T(128)} %constant.61.clone.1), kind=kCustom, calls=%fused_computation.241 | custom fusion | bytes 61440 | tf_op jit(solution)/shard_map/scatter | solution.py:436
  294.3 36.1 %scatter_custom_fusion.2 = f32[15232]{0:T(1024)S(1)} fusion(s32[7591]{0:T(1024)} %copy-done.26, f32[7591]{0:T(1024)S(1)} %broadcast.510, f32[]{:T(128)} %constant.70.clone.1), kind=kCustom, calls=%fused_computation.239 | custom fusion | bytes 61440 | tf_op jit(solution)/shard_map/scatter | solution.py:438
  333.6 39.3 %all-reduce.13 = (f32[32]{0:T(128)S(1)}, f32[]{:T(128)}, f32[32]{0:T(128)S(1)}) all-reduce(f32[32]{0:T(128)S(1)} %get-tuple-element.71, f32[]{:T(128)} %fusion.166, f32[32]{0:T(128)S(1)} %get-tuple-element.70), channel_id=1, replica_groups=mesh['dp'=4,'mp'=8] {'dp','mp'}, use_global_device_ids=true, to_apply=%region_4.5 | all-reduce | flops 65 | bytes 520 | tf_op jit(solution)/shard_map/psum | solution.py:128
  374.1 39.8 %all-reduce.12 = (f32[32]{0:T(128)S(1)}, f32[32]{0:T(128)S(1)}) all-reduce(f32[32]{0:T(128)S(1)} %get-tuple-element.69, f32[32]{0:T(128)S(1)} %get-tuple-element.68), channel_id=1, replica_groups=mesh['dp'=4,'mp'=8] {'dp','mp'}, use_global_device_ids=true, to_apply=%region_10.11 | all-reduce | flops 64 | bytes 512 | tf_op jit(solution)/shard_map/psum | solution.py:128
  416.8 40.2 %all-reduce.11 = (f32[128]{0:T(128)S(1)}, f32[128]{0:T(128)S(1)}) all-reduce(f32[128]{0:T(128)S(1)} %get-tuple-element.55, f32[128]{0:T(128)S(1)} %get-tuple-element.54), channel_id=1, replica_groups=mesh['dp'=4,'mp'=8] {'dp','mp'}, use_global_device_ids=true, to_apply=%region_14.15 | all-reduce | flops 256 | bytes 2048 | tf_op jit(solution)/shard_map/psum | solution.py:128
  459.6 39.8 %all-reduce.10 = (f32[128]{0:T(128)S(1)}, f32[128]{0:T(128)S(1)}) all-reduce(f32[128]{0:T(128)S(1)} %get-tuple-element.57, f32[128]{0:T(128)S(1)} %get-tuple-element.56), channel_id=1, replica_groups=mesh['dp'=4,'mp'=8] {'dp','mp'}, use_global_device_ids=true, to_apply=%region_41.42 | all-reduce | flops 256 | bytes 2048 | tf_op jit(solution)/shard_map/psum | solution.py:128
  500.4 7.2 all-reduce.18
  509.7 5.8 all-reduce.17
  515.5 2.4 multiply_convert_fusion
  517.9 1.7 multiply_convert_fusion.2
  520.7 39.9 %all-reduce.9 = (f32[32]{0:T(128)S(1)}, f32[32]{0:T(128)S(1)}) all-reduce(f32[32]{0:T(128)S(1)} %get-tuple-element.75, f32[32]{0:T(128)S(1)} %get-tuple-element.74), channel_id=1, replica_groups=mesh['dp'=4,'mp'=8] {'dp','mp'}, use_global_device_ids=true, to_apply=%region_45.46 | all-reduce | flops 64 | bytes 512 | tf_op jit(solution)/shard_map/psum | solution.py:128
  563.2 39.3 %all-reduce.8 = (f32[32]{0:T(128)S(1)}, f32[32]{0:T(128)S(1)}) all-reduce(f32[32]{0:T(128)S(1)} %get-tuple-element.73, f32[32]{0:T(128)S(1)} %get-tuple-element.72), channel_id=1, replica_groups=mesh['dp'=4,'mp'=8] {'dp','mp'}, use_global_device_ids=true, to_apply=%region_49.50 | all-reduce | flops 64 | bytes 512 | tf_op jit(solution)/shard_map/psum | solution.py:128
  603.4 1.7 fusion.107
  606.9 1.7 fusion.170
  611.5 1.8 fusion.176
  613.3 7.2 all-reduce.16
  621.2 23.2 %all_gather.14 = bf16[256,512]{1,0:T(8,128)(2,1)S(1)} all-gather(bf16[32,512]{1,0:T(8,128)(2,1)S(1)} %multiply_convert_fusion.5), channel_id=1, replica_groups=mesh['dp'=4,'mp'=8] {'mp'}, dimensions={0}, use_global_device_ids=true | all-gather | bytes 294912 | tf_op jit(solution)/shard_map/all_gather | solution.py:193
  646.0 12.2 %all-reduce.15 = (f32[32]{0:T(128)S(1)}, f32[32]{0:T(128)S(1)}) all-reduce(f32[32]{0:T(128)S(1)} %get-tuple-element.65, f32[32]{0:T(128)S(1)} %get-tuple-element.64), channel_id=1, replica_groups=mesh['dp'=4,'mp'=8] {'dp'}, use_global_device_ids=true, to_apply=%region_61.62 | all-reduce | flops 64 | bytes 512 | tf_op jit(solution)/shard_map/psum | solution.py:132
  658.9 25.1 %all_gather.15 = bf16[256,512]{1,0:T(8,128)(2,1)S(1)} all-gather(bf16[32,512]{1,0:T(8,128)(2,1)S(1)} %multiply_convert_fusion.4), channel_id=1, replica_groups=mesh['dp'=4,'mp'=8] {'mp'}, dimensions={0}, use_global_device_ids=true | all-gather | bytes 294912 | tf_op jit(solution)/shard_map/all_gather | solution.py:193
  684.8 11.5 %all-reduce.14 = (f32[32]{0:T(128)S(1)}, f32[32]{0:T(128)S(1)}) all-reduce(f32[32]{0:T(128)S(1)} %get-tuple-element.63, f32[32]{0:T(128)S(1)} %get-tuple-element.62), channel_id=1, replica_groups=mesh['dp'=4,'mp'=8] {'dp'}, use_global_device_ids=true, to_apply=%region_65.66 | all-reduce | flops 64 | bytes 512 | tf_op jit(solution)/shard_map/psum | solution.py:132
  697.8 6.9 all-to-all-start.1
  709.6 43.4 %dynamic_update_slice.38 = f32[256,3,256]{2,1,0:T(4,128)S(1)} dynamic-update-slice(f32[256,3,256]{2,1,0:T(4,128)S(1)} %broadcast_in_dim.74, f32[256,3,32]{2,1,0:T(4,128)} %copy.66, s32[]{:T(128)} %constant.61.clone.1, s32[]{:T(128)} %constant.61.clone.1, s32[]{:T(128)S(6)} %select_n.173) | dynamic-update-slice | bytes 196612 | tf_op jit(solution)/shard_map/dynamic_update_slice | solution.py:353
  755.0 3.1 dynamic_update_slice.39
  760.0 2.1 fusion.187
  762.2 2.2 fusion.190
  766.8 35.7 %concatenate.50 = f32[971648]{0:T(1024)} concatenate(f32[12288]{0:T(1024)S(1)} %copy-done.23, f32[1024]{0:T(1024)S(1)} %reshape.419, f32[4096]{0:T(1024)S(1)} %copy-done.33, f32[163840]{0:T(1024)S(1)} %reshape.421, f32[327680]{0:T(1024)S(1)} %reshape.422, f32[196608]{0:T(1024)} %reshape.423, f32[262144]{0:T(1024)S(1)} %bitcast.158, f32[32]{0:T(128)} %copy-done.91, f32[32]{0:T(128)} %copy-done.90, ...), dimensions={0} | concatenate | bytes 7773184 | tf_op jit(solution)/shard_map/concatenate | solution.py:427
  802.5 31.5 %scatter_custom_fusion.1 = f32[15232,128]{1,0:T(8,128)} fusion(s32[7591]{0:T(1024)} %copy-done.26, f32[]{:T(128)} %constant.70.clone.1, f32[971648]{0:T(1024)} %concatenate.50), kind=kCustom, calls=%fused_computation.4 | custom fusion | bytes 11686400 | tf_op jit(solution)/shard_map/scatter | solution.py:431
  834.0 173.6 %fusion = f32[480,128]{1,0:T(8,128)S(1)} fusion(f32[15232,128]{1,0:T(8,128)} %scatter_custom_fusion.1), kind=kCustom, calls=%all-reduce-scatter | all-reduce-scatter fusion | flops 1966081 | bytes 8044544
  1007.7 4.1 collective-permute-start.8
  1011.8 5.0 collective-permute-start.6
  1016.8 1.9 collective-permute-start.5
  1020.8 1.9 fusion.179
  (395 shorter events, 64.8 us)
Async XLA Ops:
  7.2 65.9 %all-gather.6.cloned.1.call-start = ((), (), s32[]{:S(2)}) async-start(), calls=%async_computation.9 | async-start | bytes 4055040 | tf_op jit(solution)/shard_map/all_gather | solution.py:210
  10.4 24.7 %collective-permute-start.1 = (bf16[128,256]{1,0:T(8,128)(2,1)S(1)}, bf16[128,256]{1,0:T(8,128)(2,1)S(1)}, u32[]{:S(2)}, u32[]{:S(2)}) collective-permute-start(bf16[128,256]{1,0:T(8,128)(2,1)S(1)} %fusion.103), channel_id=1, source_target_pairs={{1,0},{2,1},{3,2},{4,3},{5,4},{6,5},{7,6},{9,8},{10,9},{11,10},{12... | collective-permute-start | bytes 196616 | tf_op jit(solution)/shard_map/ppermute | solution.py:29
  13.4 21.6 %collective-permute-start = (bf16[128,256]{1,0:T(8,128)(2,1)S(1)}, bf16[128,256]{1,0:T(8,128)(2,1)S(1)}, u32[]{:S(2)}, u32[]{:S(2)}) collective-permute-start(bf16[128,256]{1,0:T(8,128)(2,1)S(1)} %fusion.103), channel_id=1, source_target_pairs={{0,1},{1,2},{2,3},{3,4},{4,5},{5,6},{6,7},{8,9},{9,10},{10,11},{11... | collective-permute-start | bytes 196616 | tf_op jit(solution)/shard_map/ppermute | solution.py:29
  15.7 19.3 %collective-permute-start.2 = (bf16[128,256]{1,0:T(8,128)(2,1)S(1)}, bf16[128,256]{1,0:T(8,128)(2,1)S(1)}, u32[]{:S(2)}, u32[]{:S(2)}) collective-permute-start(bf16[128,256]{1,0:T(8,128)(2,1)S(1)} %fusion.103), channel_id=1, source_target_pairs={{0,2},{1,3},{2,4},{3,5},{4,6},{5,7},{8,10},{9,11},{10,12},{11,13},... | collective-permute-start | bytes 196616 | tf_op jit(solution)/shard_map/ppermute | solution.py:29
  17.0 18.5 %collective-permute-start.3 = (bf16[128,256]{1,0:T(8,128)(2,1)S(1)}, bf16[128,256]{1,0:T(8,128)(2,1)S(1)}, u32[]{:S(2)}, u32[]{:S(2)}) collective-permute-start(bf16[128,256]{1,0:T(8,128)(2,1)S(1)} %fusion.103), channel_id=1, source_target_pairs={{2,0},{3,1},{4,2},{5,3},{6,4},{7,5},{10,8},{11,9},{12,10},{13,11},... | collective-permute-start | bytes 196616 | tf_op jit(solution)/shard_map/ppermute | solution.py:29
  96.5 9.6 all-to-all-start
  102.0 72.7 %reduce-scatter.6.cloned.1.call-start = ((), (), s32[]{:S(2)}) async-start(), calls=%async_computation.5 | async-start | bytes 589824 | tf_op jit(solution)/shard_map/reduce_scatter | solution.py:184
  114.9 131.2 %reduce-scatter.8.cloned.1.call-start = ((), (), s32[]{:S(2)}) async-start(), calls=%async_computation.6 | async-start | bytes 589824 | tf_op jit(solution)/shard_map/reduce_scatter | solution.py:184
  117.4 140.8 %copy-start.14 = (bf16[256,3,32]{0,2,1:T(8,128)(2,1)}, bf16[256,3,32]{0,2,1:T(8,128)(2,1)S(1)}, u32[]{:S(2)}) copy-start(bf16[256,3,32]{0,2,1:T(8,128)(2,1)S(1)} %copy.59) | copy-start | bytes 147460
  186.8 312.5 %reduce-scatter.10.cloned.1.call-start = ((), (), s32[]{:S(2)}) async-start(), calls=%async_computation.7 | async-start | bytes 2359296 | tf_op jit(solution)/shard_map/reduce_scatter | solution.py:184
  258.2 353.2 %all-gather.4.cloned.1.call-start = ((), (), s32[]{:S(2)}) async-start(), calls=%async_computation.8 | async-start | bytes 1179648 | tf_op jit(solution)/shard_map/all_gather | solution.py:193
  332.3 125.5 %copy-start.31 = (bf16[32,384]{1,0:T(8,128)(2,1)}, bf16[32,384]{1,0:T(8,128)(2,1)S(1)}, u32[]{:S(2)}) copy-start(bf16[32,384]{1,0:T(8,128)(2,1)S(1)} %reshape.405) | copy-start | bytes 73732
  332.3 279.1 %copy-start.3 = (bf16[1024,256]{1,0:T(8,128)(2,1)S(1)}, bf16[1024,256]{1,0:T(8,128)(2,1)}, u32[]{:S(2)}) copy-start(bf16[1024,256]{1,0:T(8,128)(2,1)} %reshape.407) | copy-start | bytes 1572868
  332.3 279.1 %copy-start.5 = (f32[32,512]{1,0:T(8,128)S(1)}, f32[32,512]{1,0:T(8,128)}, u32[]{:S(2)}) copy-start(f32[32,512]{1,0:T(8,128)} %reduce-scatter.8.cloned.1.call-done) | copy-start | bytes 196612
  332.3 279.1 %copy-start.41 = (f32[32]{0:T(128)S(1)}, f32[32]{0:T(128)}, u32[]{:S(2)}) copy-start(f32[32]{0:T(128)} %copy-done.40) | copy-start | bytes 388
  457.7 145.6 %copy-start.30 = (f32[32,256]{1,0:T(8,128)S(1)}, f32[32,256]{1,0:T(8,128)}, u32[]{:S(2)}) copy-start(f32[32,256]{1,0:T(8,128)} %copy-done.29) | copy-start | bytes 98308
  457.7 145.6 %copy-start.64 = (f32[32]{0:T(128)S(1)}, f32[32]{0:T(128)}, u32[]{:S(2)}) copy-start(f32[32]{0:T(128)} %copy-done.63) | copy-start | bytes 388
  457.8 145.6 %copy-start.66 = (f32[32]{0:T(128)S(1)}, f32[32]{0:T(128)}, u32[]{:S(2)}) copy-start(f32[32]{0:T(128)} %copy-done.65) | copy-start | bytes 388
  457.8 145.6 %copy-start.71 = (f32[32]{0:T(128)S(1)}, f32[32]{0:T(128)}, u32[]{:S(2)}) copy-start(f32[32]{0:T(128)} %copy-done.70) | copy-start | bytes 388
  458.3 147.7 %copy-start.28 = (f32[32,256]{1,0:T(8,128)S(1)}, f32[32,256]{1,0:T(8,128)}, u32[]{:S(2)}) copy-start(f32[32,256]{1,0:T(8,128)} %copy-done.27) | copy-start | bytes 98308
  458.3 147.7 %copy-start.79 = (f32[32]{0:T(128)S(1)}, f32[32]{0:T(128)}, u32[]{:S(2)}) copy-start(f32[32]{0:T(128)} %copy-done.78) | copy-start | bytes 388
  458.3 147.7 %copy-start.81 = (f32[32]{0:T(128)S(1)}, f32[32]{0:T(128)}, u32[]{:S(2)}) copy-start(f32[32]{0:T(128)} %copy-done.80) | copy-start | bytes 388
  458.3 147.7 %copy-start.83 = (f32[32]{0:T(128)S(1)}, f32[32]{0:T(128)}, u32[]{:S(2)}) copy-start(f32[32]{0:T(128)} %copy-done.82) | copy-start | bytes 388
  458.3 147.7 %copy-start.101 = (f32[32]{0:T(128)S(1)}, f32[32]{0:T(128)}, u32[]{:S(2)}) copy-start(f32[32]{0:T(128)} %copy-done.100) | copy-start | bytes 388
  458.3 148.6 %copy-start.32 = (bf16[32,384]{1,0:T(8,128)(2,1)S(1)}, bf16[32,384]{1,0:T(8,128)(2,1)}, u32[]{:S(2)}) copy-start(bf16[32,384]{1,0:T(8,128)(2,1)} %copy-done.31) | copy-start | bytes 73732
  459.6 161.6 %copy-start.8 = (f32[128,256]{1,0:T(8,128)}, f32[128,256]{1,0:T(8,128)S(1)}, u32[]{:S(2)}) copy-start(f32[128,256]{1,0:T(8,128)S(1)} %get-tuple-element.108) | copy-start | bytes 393220
  459.6 160.9 %copy-start.44 = (f32[32]{0:T(128)S(1)}, f32[32]{0:T(128)}, u32[]{:S(2)}) copy-start(f32[32]{0:T(128)} %copy-done.43) | copy-start | bytes 388
  459.6 160.8 %copy-start.57 = (f32[32]{0:T(128)S(1)}, f32[32]{0:T(128)}, u32[]{:S(2)}) copy-start(f32[32]{0:T(128)} %copy-done.56) | copy-start | bytes 388
  508.3 136.9 %copy-start.15 = (bf16[256,3,32]{0,2,1:T(8,128)(2,1)S(1)}, bf16[256,3,32]{0,2,1:T(8,128)(2,1)}, u32[]{:S(2)}) copy-start(bf16[256,3,32]{0,2,1:T(8,128)(2,1)} %copy-done.14) | copy-start | bytes 147460
  517.9 127.8 %copy-start.10 = (f32[32,512]{1,0:T(8,128)S(1)}, f32[32,512]{1,0:T(8,128)}, u32[]{:S(2)}) copy-start(f32[32,512]{1,0:T(8,128)} %reduce-scatter.6.cloned.1.call-done) | copy-start | bytes 196612
  517.9 127.8 %copy-start.51 = (f32[32]{0:T(128)S(1)}, f32[32]{0:T(128)}, u32[]{:S(2)}) copy-start(f32[32]{0:T(128)} %copy-done.50) | copy-start | bytes 388
  517.9 127.8 %copy-start.53 = (f32[32]{0:T(128)S(1)}, f32[32]{0:T(128)}, u32[]{:S(2)}) copy-start(f32[32]{0:T(128)} %copy-done.52) | copy-start | bytes 388
  517.9 127.8 %copy-start.62 = (f32[32]{0:T(128)S(1)}, f32[32]{0:T(128)}, u32[]{:S(2)}) copy-start(f32[32]{0:T(128)} %copy-done.61) | copy-start | bytes 388
  517.9 127.8 %copy-start.77 = (f32[32]{0:T(128)S(1)}, f32[32]{0:T(128)}, u32[]{:S(2)}) copy-start(f32[32]{0:T(128)} %copy-done.76) | copy-start | bytes 388
  697.8 62.2 %all-to-all-start.1 = ((bf16[32,8,256]{2,0,1:T(8,128)(2,1)}), bf16[32,8,256]{2,0,1:T(8,128)(2,1)}, u32[]{:S(2)}, u32[]{:S(2)}) async-start(bf16[32,8,256]{2,0,1:T(8,128)(2,1)} %bitcast.25), calls=%async_computation.4 | async-start | bytes 262144 | tf_op jit(solution)/shard_map/all_to_all | solution.py:379
  764.4 258.3 %collective-permute-start.7 = (bf16[128,256]{1,0:T(8,128)(2,1)S(1)}, bf16[128,256]{1,0:T(8,128)(2,1)S(1)}, u32[]{:S(2)}, u32[]{:S(2)}) collective-permute-start(bf16[128,256]{1,0:T(8,128)(2,1)S(1)} %get-tuple-element.147), channel_id=1, source_target_pairs={{0,2},{1,3},{2,4},{3,5},{4,6},{5,7},{8,10},{9,11},{10,12},{11,13},... | collective-permute-start | bytes 196616 | tf_op jit(solution)/shard_map/ppermute | solution.py:29
  834.0 177.8 %copy-start.4 = (f32[640,256]{1,0:T(8,128)S(1)}, f32[640,256]{1,0:T(8,128)}, u32[]{:S(2)}) copy-start(f32[640,256]{1,0:T(8,128)} %get-tuple-element.161) | copy-start | bytes 1966084
  834.0 177.8 %copy-start.7 = (f32[384,256]{1,0:T(8,128)S(1)}, f32[384,256]{1,0:T(8,128)}, u32[]{:S(2)}) copy-start(f32[384,256]{1,0:T(8,128)} %fusion.170) | copy-start | bytes 1179652
  834.0 186.7 %copy-start.11 = (f32[476,128]{1,0:T(8,128)S(1)}, f32[476,128]{1,0:T(8,128)}, u32[]{:S(2)}) copy-start(f32[476,128]{1,0:T(8,128)} %param.15) | copy-start | bytes 731140
  834.0 186.7 %copy-start.21 = (f32[476,128]{1,0:T(8,128)S(1)}, f32[476,128]{1,0:T(8,128)}, u32[]{:S(2)}) copy-start(f32[476,128]{1,0:T(8,128)} %param.17) | copy-start | bytes 731140
  834.0 186.8 %copy-start.22 = (f32[476,128]{1,0:T(8,128)S(1)}, f32[476,128]{1,0:T(8,128)}, u32[]{:S(2)}) copy-start(f32[476,128]{1,0:T(8,128)} %param.16) | copy-start | bytes 731140
  834.0 186.7 %copy-start.54 = (f32[476]{0:T(512)S(1)}, f32[476]{0:T(512)}, u32[]{:S(2)}) copy-start(f32[476]{0:T(512)} %dynamic_slice.58) | copy-start | bytes 5716
  834.0 186.7 %copy-start.55 = (s32[476]{0:T(512)S(1)}, s32[476]{0:T(512)}, u32[]{:S(2)}) copy-start(s32[476]{0:T(512)} %dynamic-slice_multiply_fusion) | copy-start | bytes 5716
  834.0 188.7 %copy-start.9 = (f32[128,256]{1,0:T(8,128)S(1)}, f32[128,256]{1,0:T(8,128)}, u32[]{:S(2)}) copy-start(f32[128,256]{1,0:T(8,128)} %copy-done.8) | copy-start | bytes 393220
  1007.7 12.4 %collective-permute-start.8 = (f32[124,128]{1,0:T(8,128)S(1)}, f32[124,128]{1,0:T(8,128)S(1)}, u32[]{:S(2)}, u32[]{:S(2)}) collective-permute-start(f32[124,128]{1,0:T(8,128)S(1)} %slice.252), channel_id=1, source_target_pairs={{0,1},{1,2},{2,3},{3,4},{4,5},{5,6},{6,7},{7,8},{8,9},{9,10},{10,1... | collective-permute-start | bytes 190472
  1011.8 10.8 %collective-permute-start.6 = (bf16[128,256]{1,0:T(8,128)(2,1)S(1)}, bf16[128,256]{1,0:T(8,128)(2,1)S(1)}, u32[]{:S(2)}, u32[]{:S(2)}) collective-permute-start(bf16[128,256]{1,0:T(8,128)(2,1)S(1)} %get-tuple-element.142), channel_id=1, source_target_pairs={{0,1},{1,2},{2,3},{3,4},{4,5},{5,6},{6,7},{8,9},{9,10},{10,11},{11... | collective-permute-start | bytes 196616 | tf_op jit(solution)/shard_map/ppermute | solution.py:29
  1016.8 5.9 collective-permute-start.5
  1018.8 4.0 collective-permute-start.4
  (70 other events, 3146.4 us)
Sparse Core Ops, SparseCore 0:
  11.5 61.5 all-gather.5
  115.0 59.6 reduce-scatter.5
  186.9 59.0 reduce-scatter.7
  258.3 65.2 reduce-scatter.9
  518.0 38.3 all-gather.3
where the time goes:
time: 1040 us; the launch traced here: 1030 us
  blocking collectives  526 us (51%)
  local copies, waits for them, and re-layouts  236 us (23%)
  waiting for transfers between devices  153 us (15%)
  other arithmetic  40.5 us (4%)
  starting transfers between devices  36.7 us (4%)
  matrix products  21.9 us (2%)
  between operations  16.4 us (2%)
    psum x6, blocking collectives, fast_total(): return lax.psum(parts, ('dp', 'mp'))  238 us
    unnamed x1, blocking collectives  174 us
    reduce_scatter x3, waiting for transfers between devices, spread_sum(): lax.psum_scatter(jnp.dot(block, inputs, preferred_element_type=jnp.float3...  115 us
    psum x8, blocking collectives, slow_total(): return lax.psum(parts, 'dp')  65.6 us
    all_gather x2, blocking collectives, fold_back(): lax.all_gather(a, 'mp', axis=0, tiled=True)  48.3 us
    dynamic_update_slice x1, local copies, waits for them, and re-layouts, local(): lax.dynamic_update_slice_in_dim(jnp.zeros((B_SLOW, 3, B_SLOW), jnp.float3...  43.4 us
    all_gather x1, waiting for transfers between devices, local(): lax.all_gather(master.astype(jnp.bfloat16), ('dp', 'mp'), axis=0, tiled=T...  37.5 us
    scatter x1, local copies, waits for them, and re-layouts, local(): living = jnp.zeros((devices * slots,), jnp.float32).at[position].set(1.0)  36.1 us
  transfers between devices with their start and end apart: 16, of which 4 were waited for; matrix products, arithmetic and copies ran while one was open for 41% of the time, Pallas kernels for 0%

commit v1 on v0

v1 whole, which is shorter than its diff:
```python
import functools
import math

import jax
import jax.numpy as jnp
from jax import lax
from jax.experimental import pallas as pl
from jax.experimental.pallas import tpu as pltpu
from jax.sharding import PartitionSpec as P

C_FAST = 128
B_FAST = 32
C_SLOW = 1024
B_SLOW = 256
C_LAT = 256
TILE = 16
POS = TILE * TILE
BLK = 128
STEP = 10
NBLK = 7591

norm_eps = 1e-05
beta_first = 0.5
beta_second = 0.5
adam_eps = 1e-08
decay_rate = 0.05

MESH = pl.DeviceIdType.MESH
f32 = jnp.float32
bf16 = jnp.bfloat16
RC = 32
GROUPS = BLK // B_FAST

AT_F1 = 0
AT_F2 = AT_F1 + B_FAST * 3 * C_FAST // BLK
AT_F3 = AT_F2 + B_FAST * B_FAST // BLK
AT_LAT = AT_F3 + C_FAST * B_FAST // BLK
AT_S1 = AT_LAT + C_LAT * 5 * C_FAST // BLK
AT_S2 = AT_S1 + B_SLOW * (C_SLOW + C_LAT) // BLK
AT_S3 = AT_S2 + B_SLOW * 3 * B_SLOW // BLK
AT_VEC = AT_S3 + C_SLOW * B_SLOW // BLK
VECS = NBLK - AT_VEC
V_F3 = (1, 2, 1)
V_LAT = (3, 5, 2)
V_S1 = (7, 9, 2)
V_S2 = (11, 13, 2)
V_S3 = (15, 23, 8)


def up(n, m):
    return (n + m - 1) // m * m


def dot_nt(a, b):
    return lax.dot_general(a, b, (((1,), (1,)), ((), ())), preferred_element_type=f32)


def dot_tn(a, b):
    return lax.dot_general(a, b, (((0,), (0,)), ((), ())), preferred_element_type=f32)


def dot_nn(a, b):
    return lax.dot_general(a, b, (((1,), (0,)), ((), ())), preferred_element_type=f32)


G0 = math.sqrt(2.0 / math.pi)
G1 = 0.044715


def gelu(x):
    t = jnp.tanh(x * (G0 + (G0 * G1) * (x * x)))
    return 0.5 * x * (1.0 + t)


def gelu_slope(x):
    xx = x * x
    t = jnp.tanh(x * (G0 + (G0 * G1) * xx))
    return 0.5 * (1.0 + t) + (0.5 * x) * (1.0 - t * t) * (G0 + (3.0 * G0 * G1) * xx)


def position_mask(crop):
    spot = lax.broadcasted_iota(jnp.int32, (POS, BLK), 0)
    inside = (spot // TILE < crop) & (lax.rem(spot, TILE) < crop)
    return jnp.where(inside, 1.0, 0.0).astype(f32)


class Sender:
    def __init__(self, sems):
        self.sems = sems
        self.copies = []

    def send(self, view, recv_sem, device):
        copy = pltpu.make_async_remote_copy(
            src_ref=view,
            dst_ref=view,
            send_sem=self.sems.at[len(self.copies)],
            recv_sem=recv_sem,
            device_id=device,
            device_id_type=MESH,
        )
        copy.start()
        self.copies.append(copy)

    def drain(self):
        for copy in self.copies:
            copy.wait_send()
        self.copies = []


def arrived(view, sem):
    pltpu.make_async_copy(view, view, sem).wait()


class Place:
    def __init__(self, nd, nm):
        self.nd, self.nm = nd, nm
        self.nc = 2
        self.nx = nd // 2
        self.nb = 2 if nm % 2 == 0 else 1
        self.na = nm // self.nb
        self.dp = lax.axis_index("dp")
        self.mp = lax.axis_index("mp")
        self.x, self.c = self.dp // 2, lax.rem(self.dp, 2)
        self.a, self.b = self.mp // self.nb, lax.rem(self.mp, self.nb)

    def off_a(self, i):
        return lax.rem(self.a + i, self.na)

    def off_b(self, i):
        return lax.rem(self.b + i, self.nb)

    def off_x(self, i):
        return lax.rem(self.x + i, self.nx)

    def dev(self, x, c, a, b):
        return (x * 2 + c, a * self.nb + b)

    def slot(self, x, c, a, b):
        return (x * 2 + c) * self.nm + a * self.nb + b


class Gather:
    def __init__(self, place, view, sender, recv):
        self.p, self.view, self.sender, self.recv = place, view, sender, recv

    def rank(self, a, b):
        return a * self.p.nb + b

    def forward(self, a):
        p = self.p
        r = self.rank(a, p.b)
        for i in range(1, p.nb):
            self.sender.send(self.view(r), self.recv.at[r], (p.dp, self.rank(p.a, p.off_b(i))))

    def start(self):
        p = self.p
        for i in range(1, p.na):
            self.sender.send(
                self.view(p.mp), self.recv.at[p.mp], (p.dp, self.rank(p.off_a(i), p.b))
            )
        self.forward(p.a)

    def relay(self):
        p = self.p
        for i in range(1, p.na):
            a = p.off_a(p.na - i)
            arrived(self.view(self.rank(a, p.b)), self.recv.at[self.rank(a, p.b)])
            self.forward(a)

    def finish(self):
        p = self.p
        for j in range(1, p.nb):
            for i in range(p.na):
                r = self.rank(p.off_a(p.na - i), p.off_b(j))
                arrived(self.view(r), self.recv.at[r])


def signal_all(devices):
    barrier = pltpu.get_barrier_semaphore()
    for device in devices:
        pl.semaphore_signal(barrier, inc=1, device_id=device, device_id_type=MESH)


def gather_sizes(nd, nm):
    nb = 2 if nm % 2 == 0 else 1
    na, nx = nm // nb, nd // 2
    params = (na - 1) + (nb - 1) + (nx - 1) + 1
    params += (na - 1) * ((nb - 1) + (nx - 1) + 1)
    params += na * (nb - 1) * (1 + nx - 1) + na * (nx - 1) * (1 + nb - 1)
    params += na * (nb - 1) * (nx - 1)
    arrays = nm - 1
    return params, arrays


def gather_kernel(
    cfg, start_ref, count_ref, crop_ref, master_ref, fast_ref, slow_ref,
    p_ref, xt_ref, xs_ref, shift_ref, natural_ref, p_recv, f_recv, s_recv, send_sems
):
    nd, nm, frames, slow_frames, share, slots = cfg
    rows = up(slots + 15, 16)
    p = Place(nd, nm)
    peers = [p.dev(p.x, p.c, p.off_a(i), p.b) for i in range(1, p.na)]
    peers += [p.dev(p.x, p.c, p.a, p.off_b(i)) for i in range(1, p.nb)]
    peers += [p.dev(p.off_x(i), p.c, p.a, p.b) for i in range(1, p.nx)]
    peers += [p.dev(p.x, 1 - p.c, p.a, p.b)]
    signal_all(peers)

    me = p.dp * nm + p.mp
    start = start_ref[me]
    shift = lax.rem(start, 16)
    shift_ref[...] = jnp.zeros_like(shift_ref)
    shift_ref[16 : 16 + slots] = master_ref[...]
    moved = shift_ref[pl.ds(16 - shift, rows), :]
    row = lax.broadcasted_iota(jnp.int32, (rows, BLK), 0)
    own = (row >= shift) & (row < shift + count_ref[me])
    p_ref[me] = jnp.where(own, moved, 0.0).astype(bf16)

    pl.semaphore_wait(pltpu.get_barrier_semaphore(), len(peers))

    out = Sender(send_sems)

    def view(x, c, a, b):
        return p_ref.at[p.slot(x, c, a, b)]

    def pass_on(source, along_a=False, along_b=False, along_x=False, along_c=False):
        piece, sem = view(*source), p_recv.at[p.slot(*source)]
        if along_a:
            for i in range(1, p.na):
                out.send(piece, sem, p.dev(p.x, p.c, p.off_a(i), p.b))
        if along_x:
            for i in range(1, p.nx):
                out.send(piece, sem, p.dev(p.off_x(i), p.c, p.a, p.b))
        if along_b:
            for i in range(1, p.nb):
                out.send(piece, sem, p.dev(p.x, p.c, p.a, p.off_b(i)))
        if along_c:
            out.send(piece, sem, p.dev(p.x, 1 - p.c, p.a, p.b))

    def take(source):
        arrived(view(*source), p_recv.at[p.slot(*source)])

    pass_on((p.x, p.c, p.a, p.b), along_a=True, along_b=True, along_x=True, along_c=True)

    mask = position_mask(crop_ref[0])
    xt_ref[: 2 * POS] = jnp.zeros((2 * POS, BLK), bf16)
    xt_ref[(frames + 2) * POS :] = jnp.zeros((2 * POS, BLK), bf16)

    def frame_view(r):
        return xt_ref.at[pl.ds(pl.multiple_of((r + 2) * POS, POS), POS)]

    frame_view(p.mp)[...] = (fast_ref[...].astype(f32).T * mask).astype(bf16)
    fast_gather = Gather(p, frame_view, out, f_recv)
    fast_gather.start()

    if share == BLK:

        def slow_view(r):
            return xs_ref.at[:, pl.ds(pl.multiple_of(r * BLK, BLK), BLK)]

        for s in range(slow_frames):
            piece = slow_ref[:, s * POS : (s + 1) * POS].astype(f32).T * mask
            slow_view(p.mp)[s * POS : (s + 1) * POS, :] = piece.astype(bf16)
    else:

        def slow_view(r):
            return natural_ref.at[pl.ds(pl.multiple_of(r * share, share), share)]

        slow_view(p.mp)[...] = slow_ref[...]
    slow_gather = Gather(p, slow_view, out, s_recv)
    slow_gather.start()

    for i in range(1, p.na):
        source = (p.x, p.c, p.off_a(p.na - i), p.b)
        take(source)
        pass_on(source, along_b=True, along_x=True, along_c=True)
    fast_gather.relay()
    across = p.na * 3 // 4
    for i in range(p.na):
        for j in range(1, p.nb):
            source = (p.x, p.c, p.off_a(p.na - i), p.off_b(j))
            take(source)
            pass_on(source, along_x=i < across, along_c=True)
        for j in range(1, p.nx):
            source = (p.off_x(j), p.c, p.off_a(p.na - i), p.b)
            take(source)
            pass_on(source, along_b=i >= across, along_c=True)
    slow_gather.relay()
    for i in range(p.na):
        for j in range(1, p.nb):
            for k in range(1, p.nx):
                source = (p.off_x(k), p.c, p.off_a(p.na - i), p.off_b(j))
                take(source)
                pass_on(source, along_c=True)
    for i in range(p.na):
        for j in range(p.nb):
            for k in range(p.nx):
                take((p.off_x(k), 1 - p.c, p.off_a(i), p.off_b(j)))
    fast_gather.finish()
    slow_gather.finish()
    out.drain()
    if share != BLK:
        from_natural(natural_ref, xs_ref, mask, slow_frames)


def from_natural(natural_ref, wide_ref, mask, slow_frames):
    def block(i, _):
        s, j = i // (C_SLOW // BLK), lax.rem(i, C_SLOW // BLK)
        at_row = pl.ds(pl.multiple_of(s * POS, POS), POS)
        at_lane = pl.ds(pl.multiple_of(j * BLK, BLK), BLK)
        piece = natural_ref[at_lane, at_row].astype(f32).T * mask
        wide_ref[at_row, at_lane] = piece.astype(bf16)
        return 0

    lax.fori_loop(0, slow_frames * (C_SLOW // BLK), block, 0)


def call_gather(cfg, starts, counts, crop, master, fast, slow):
    nd, nm, frames, slow_frames, share, slots = cfg
    rows = up(slots + 15, 16)
    params, arrays = gather_sizes(nd, nm)
    smem = pl.BlockSpec(memory_space=pltpu.SMEM)
    vmem = pl.BlockSpec(memory_space=pltpu.VMEM)
    dma = pltpu.SemaphoreType.DMA
    natural = (C_SLOW, slow_frames * POS) if share != BLK else (16, BLK)
    return pl.pallas_call(
        functools.partial(gather_kernel, cfg),
        out_shape=(
            jax.ShapeDtypeStruct((nd * nm, rows, BLK), bf16),
            jax.ShapeDtypeStruct(((frames + 4) * POS, BLK), bf16),
            jax.ShapeDtypeStruct((slow_frames * POS, C_SLOW), bf16),
        ),
        in_specs=[smem, smem, smem, vmem, vmem, vmem],
        out_specs=(vmem, vmem, vmem),
        scratch_shapes=[
            pltpu.VMEM((rows + 16, BLK), f32),
            pltpu.VMEM(natural, bf16),
            dma((nd * nm,)),
            dma((nm,)),
            dma((nm,)),
            dma((params + 2 * arrays,)),
        ],
        compiler_params=pltpu.CompilerParams(
            collective_id=0, has_side_effects=True, vmem_limit_bytes=48 << 20
        ),
        name="gather",
    )(starts, counts, crop, master, fast, slow)


def lane_group():
    return lax.broadcasted_iota(jnp.int32, (1, BLK), 1) // B_FAST


def fold_lanes(v):
    v = v + pltpu.roll(v, B_FAST, 1)
    return v + pltpu.roll(v, 2 * B_FAST, 1)


def weights_kernel(
    cfg, start_ref, p_ref, lat_ref, s1_ref, s2_ref, s3_ref, f1_ref, f2_ref, f3_ref, vec_ref,
    flat_ref, square_ref
):
    nd, nm, frames, slow_frames, share, slots = cfg
    rows = up(slots + 15, 16)
    chunk = 64

    def clear(i, _):
        flat_ref[pl.ds(pl.multiple_of(i * chunk, chunk), chunk), :] = jnp.zeros((chunk, BLK), f32)
        return 0

    lax.fori_loop(0, flat_ref.shape[0] // chunk, clear, 0)

    def add(d, _):
        base = pl.multiple_of(start_ref[d] // 16 * 16, 16)
        flat_ref[pl.ds(base, rows), :] += p_ref[d].astype(f32)
        return 0

    lax.fori_loop(0, nd * nm, add, 0)

    def matrix(out_ref, at, tall, blocks):
        for j in range(blocks):
            for o in range(0, tall, 256):
                out_ref[o : o + 256, j * BLK : (j + 1) * BLK] = flat_ref[
                    pl.ds(at + o * blocks + j, 256, stride=blocks), :
                ].astype(bf16)

    matrix(lat_ref, AT_LAT, C_LAT, 5)
    matrix(s1_ref, AT_S1, B_SLOW, 10)
    matrix(s2_ref, AT_S2, B_SLOW, 6)
    matrix(s3_ref, AT_S3, C_SLOW, 2)
    for k in range(3):
        tap = flat_ref[pl.ds(AT_F1 + k, B_FAST, stride=3), :].astype(bf16)
        for g in range(GROUPS):
            f1_ref[g * B_FAST : (g + 1) * B_FAST, k * BLK : (k + 1) * BLK] = tap
    group = lane_group()

    def spread(at, tall):
        for r in range(GROUPS):
            part = jnp.where(group == r, flat_ref[at : at + tall // GROUPS, :], 0.0)
            square_ref[pl.ds(r, tall // GROUPS, stride=GROUPS), :] = fold_lanes(part)
        return square_ref[:tall, :]

    two = spread(AT_F2, B_FAST)
    for g in range(GROUPS):
        f2_ref[g * B_FAST : (g + 1) * B_FAST, :] = jnp.where(group == g, two, 0.0).astype(bf16)
    f3_ref[...] = spread(AT_F3, C_FAST).astype(bf16)
    vec_ref[...] = flat_ref[AT_VEC : AT_VEC + 32, :]


def call_weights(cfg, starts, gathered):
    nd, nm, frames, slow_frames, share, slots = cfg
    rows = up(slots + 15, 16)
    smem = pl.BlockSpec(memory_space=pltpu.SMEM)
    vmem = pl.BlockSpec(memory_space=pltpu.VMEM)
    shapes = [
        ((C_LAT, 5 * C_FAST), bf16),
        ((B_SLOW, C_SLOW + C_LAT), bf16),
        ((B_SLOW, 3 * B_SLOW), bf16),
        ((C_SLOW, B_SLOW), bf16),
        ((BLK, 3 * C_FAST), bf16),
        ((BLK, BLK), bf16),
        ((BLK, BLK), bf16),
        ((32, BLK), f32),
    ]
    return pl.pallas_call(
        functools.partial(weights_kernel, cfg),
        out_shape=tuple(jax.ShapeDtypeStruct(s, t) for s, t in shapes),
        in_specs=[smem, vmem],
        out_specs=tuple(vmem for _ in shapes),
        scratch_shapes=[
            pltpu.VMEM((up(NBLK + rows, 64), BLK), f32),
            pltpu.VMEM((BLK, BLK), f32),
        ],
        compiler_params=pltpu.CompilerParams(vmem_limit_bytes=48 << 20),
        name="weights",
    )(starts, gathered)


EX_LAT, EX_S1, EX_S2, EX_B2, EX_B1, EX_BLAT = range(6)
EX_F1, EX_F2, EX_F3, EX_BF3, EX_BF2, EX_BF1 = range(6, 12)
EX_S3, EX_BS3 = 12, 13
EXCHANGES = 14


def main_kernel(
    cfg, start_ref, crop_ref, xt_ref, xs_ref, lat_w, s1_w, s2_w, s3_w, f1_w, f2_w, f3_w, vec_ref,
    fcot_ref, scot_ref,
    fast_out, slow_out, fast_grad, slow_grad, grad_out,
    mask_ref, fc_ref, sc_ref, natural_ref, zb, latb, s1b, s2b, dz, da1, da2, c1, c2, c3, e, e3,
    a1p, a2p, h1p, h2p, d1p, d2p, ep, a3, e3f, square_ref, flat_ref, own3_ref, win_ref,
    st_ref, st16_ref, f_recv, s_recv, gather_sems, ex_send, ex_recv, g_send, g_recv
):
    nd, nm, frames, slow_frames, share, slots = cfg
    p = Place(nd, nm)
    slow_rows, fast_rows = slow_frames * POS, frames * POS
    per_group = frames // GROUPS
    group_rows = per_group * POS
    keep = share == BLK
    da3, da3f = sc_ref, fc_ref

    peers = [(lax.rem(p.dp + i, nd), p.mp) for i in range(1, nd)]
    near = [p.dev(p.x, p.c, p.off_a(i), p.b) for i in range(1, p.na)]
    near += [p.dev(p.x, p.c, p.a, p.off_b(i)) for i in range(1, p.nb)]
    signal_all(peers + near)

    crop = crop_ref[0]
    mask_ref[...] = position_mask(crop)
    tall = crop.astype(f32)
    area = tall * tall

    mask = mask_ref[...]

    def frame_view(r):
        return fc_ref.at[pl.ds(pl.multiple_of(r * POS, POS), POS)]

    frame_view(p.mp)[...] = (fcot_ref[...].astype(f32).T * mask).astype(bf16)
    if keep:

        def slow_view(r):
            return sc_ref.at[:, pl.ds(pl.multiple_of(r * BLK, BLK), BLK)]

        for s in range(slow_frames):
            piece = scot_ref[:, s * POS : (s + 1) * POS].astype(f32).T * mask
            slow_view(p.mp)[s * POS : (s + 1) * POS, :] = piece.astype(bf16)
    else:

        def slow_view(r):
            return natural_ref.at[pl.ds(pl.multiple_of(r * share, share), share)]

        slow_view(p.mp)[...] = scot_ref[...]

    pl.semaphore_wait(pltpu.get_barrier_semaphore(), len(peers) + len(near))
    out = Sender(gather_sems)
    slow_gather = Gather(p, slow_view, out, s_recv)
    fast_gather = Gather(p, frame_view, out, f_recv)
    fast_gather.start()
    slow_gather.start()

    ex_copies = []

    def stat(which):
        return st_ref.at[which] if which < 12 else st16_ref.at[which - 12]

    def exchange(which):
        own = stat(which).at[p.dp]
        for i in range(1, nd):
            copy = pltpu.make_async_remote_copy(
                src_ref=own,
                dst_ref=own,
                send_sem=ex_send.at[which, i - 1],
                recv_sem=ex_recv.at[which, i - 1],
                device_id=peers[i - 1],
                device_id_type=MESH,
            )
            copy.start()
            ex_copies.append(copy)

    def exchanged(which):
        buffer = stat(which)
        for i in range(1, nd):
            arrived(buffer.at[lax.rem(p.dp + nd - i, nd)], ex_recv.at[which, i - 1])
        total = buffer[0]
        for i in range(1, nd):
            total = total + buffer[i]
        return total

    def put(which, at, vector):
        ref = stat(which)
        for j in range(vector.shape[1] // BLK):
            ref[p.dp, at + j : at + j + 1, :] = vector[:, j * BLK : (j + 1) * BLK]

    def row_of(block, at, n):
        return jnp.concatenate([block[at + j : at + j + 1, :] for j in range(n)], 1)

    def vectors(place):
        g, b, n = place
        return row_of(vec_ref[...], g, n), row_of(vec_ref[...], b, n)

    def rows_at(i, size):
        return pl.ds(pl.multiple_of(i * size, size), size)

    def mask_at(i, width):
        part = mask_ref[pl.ds(pl.multiple_of(lax.rem(i * RC, POS), RC), RC), :]
        return jnp.concatenate([part] * (width // BLK), 1) if width > BLK else part

    def eights(v):
        return jnp.sum(v.reshape(v.shape[0] // 8, 8, v.shape[1]), 0)

    def total_row(v):
        return jnp.sum(v, 0, keepdims=True)

    def affine(sums, squares, count, gain, bias):
        mean = sums / count
        scale = lax.rsqrt(squares / count - mean * mean + norm_eps)
        grow = gain * scale
        return mean, scale, grow, bias - mean * grow

    def sums_of(ref, n_rows, width):
        def body(i, acc):
            v = ref[rows_at(i, RC), :].astype(f32)
            return acc[0] + eights(v), acc[1] + eights(v * v)

        zero = jnp.zeros((8, width), f32)
        one, two = lax.fori_loop(0, n_rows // RC, body, (zero, zero))
        return total_row(one), total_row(two)

    def activate(src, dst, n_rows, width, grow, base):
        def body(i, _):
            at = rows_at(i, RC)
            pre = src[at, :].astype(f32) * grow + base
            dst[at, :] = (gelu(pre) * mask_at(i, width)).astype(bf16)
            return 0

        lax.fori_loop(0, n_rows // RC, body, 0)

    def slopes(src, incoming, n_rows, width, norm):
        mean, scale, grow, base = norm

        def body(i, acc):
            at = rows_at(i, RC)
            a = src[at, :].astype(f32)
            d = gelu_slope(a * grow + base) * incoming[at, :] * mask_at(i, width)
            incoming[at, :] = d
            return acc[0] + eights(d), acc[1] + eights(d * ((a - mean) * scale))

        zero = jnp.zeros((8, width), f32)
        one, two = lax.fori_loop(0, n_rows // RC, body, (zero, zero))
        return total_row(one), total_row(two)

    def back_vectors(bias_sum, gain_sum, count, norm):
        mean, scale, grow, base = norm
        k1 = grow * gain_sum / count
        return grow * bias_sum / count - k1 * (mean * scale), k1 * scale

    def raw_grads(src, pres, dst, n_rows, width, norm, q0, q1):
        grow = norm[2]

        def body(i, _):
            at = rows_at(i, RC)
            a = src[at, :].astype(f32)
            da = grow * pres[at, :] - mask_at(i, width) * (q0 + a * q1)
            dst[at, :] = da.astype(bf16)
            return 0

        lax.fori_loop(0, n_rows // RC, body, 0)

    def put_vector(row, vector):
        for j in range(vector.shape[1] // BLK):
            at = AT_VEC + row + j
            flat_ref[at : at + 1, :] = vector[:, j * BLK : (j + 1) * BLK]

    def frame(ref, s):
        return ref[s * POS : (s + 1) * POS, :]

    group = lane_group()

    for s in range(slow_frames):
        window = jnp.concatenate([frame(xt_ref, 4 * s + k) for k in range(5)], 1)
        zb[s * POS : (s + 1) * POS, :] = dot_nt(window, lat_w[...]).astype(bf16)
    one, two = sums_of(zb, slow_rows, C_LAT)
    put(EX_LAT, 0, one)
    put(EX_LAT, 2, two)
    st_ref[EX_LAT, p.dp, 4:8, :] = jnp.full((4, BLK), area, f32)
    exchange(EX_LAT)

    def first(j, _):
        total = jnp.zeros((POS, BLK), f32)
        for g in range(GROUPS):
            at = (g * per_group + j + 1) * POS
            window = jnp.concatenate(
                [xt_ref[pl.ds(pl.multiple_of(at + k * POS, POS), POS), :] for k in range(3)], 1
            )
            total = total + jnp.where(group == g, dot_nt(window, f1_w[...]), 0.0)
        a1p[rows_at(j, POS), :] = total
        return 0

    lax.fori_loop(0, per_group, first, 0)
    one, two = sums_of(a1p, group_rows, BLK)
    put(EX_F1, 0, fold_lanes(one))
    put(EX_F1, 1, fold_lanes(two))
    st_ref[EX_F1, p.dp, 2:8, :] = jnp.full((6, BLK), area, f32)
    exchange(EX_F1)

    for s in range(slow_frames):
        c1[s * POS : (s + 1) * POS, :] = dot_nt(frame(xs_ref, s), s1_w[:, :C_SLOW])

    total = exchanged(EX_LAT)
    area_all = total[4:5, :]
    slow_count = jnp.concatenate([area_all * float(slow_frames)] * 2, 1)
    slow_count8 = jnp.concatenate([slow_count] * 4, 1)
    fast_count = area_all * float(frames)
    lat_norm = affine(row_of(total, 0, 2), row_of(total, 2, 2), slow_count, *vectors(V_LAT))
    activate(zb, latb, slow_rows, C_LAT, lat_norm[2], lat_norm[3])
    for s in range(slow_frames):
        at = slice(s * POS, (s + 1) * POS)
        c1[at, :] = c1[at, :] + dot_nt(latb[at, :], s1_w[:, C_SLOW:])
    one, two = sums_of(c1, slow_rows, B_SLOW)
    put(EX_S1, 0, one)
    put(EX_S1, 2, two)
    st_ref[EX_S1, p.dp, 4:8, :] = jnp.zeros((4, BLK), f32)
    exchange(EX_S1)

    packed = vec_ref[0:1, :]

    def spread(which):
        return fold_lanes(jnp.where(group == which, packed, 0.0))

    def exchanged_two(which):
        total = exchanged(which)
        return total[0:1, :], total[1:2, :]

    f1_norm = affine(*exchanged_two(EX_F1), fast_count, spread(0), spread(1))
    activate(a1p, h1p, group_rows, BLK, f1_norm[2], f1_norm[3])
    for j in range(per_group):
        a2p[j * POS : (j + 1) * POS, :] = dot_nt(frame(h1p, j), f2_w[...])
    one, two = sums_of(a2p, group_rows, BLK)
    put(EX_F2, 0, fold_lanes(one))
    put(EX_F2, 1, fold_lanes(two))
    st_ref[EX_F2, p.dp, 2:8, :] = jnp.zeros((6, BLK), f32)
    exchange(EX_F2)
    fast_gather.relay()

    total = exchanged(EX_S1)
    s1_norm = affine(row_of(total, 0, 2), row_of(total, 2, 2), slow_count, *vectors(V_S1))
    activate(c1, s1b, slow_rows, B_SLOW, s1_norm[2], s1_norm[3])
    for s in range(slow_frames):
        low, high = max(0, 1 - s), min(3, slow_frames - s + 1)
        window = jnp.concatenate([frame(s1b, s + k - 1) for k in range(low, high)], 1)
        c2[s * POS : (s + 1) * POS, :] = dot_nt(window, s2_w[:, low * B_SLOW : high * B_SLOW])
    one, two = sums_of(c2, slow_rows, B_SLOW)
    put(EX_S2, 0, one)
    put(EX_S2, 2, two)
    st_ref[EX_S2, p.dp, 4:8, :] = jnp.zeros((4, BLK), f32)
    exchange(EX_S2)

    f2_norm = affine(*exchanged_two(EX_F2), fast_count, spread(2), spread(3))
    activate(a2p, h2p, group_rows, BLK, f2_norm[2], f2_norm[3])
    for g in range(GROUPS):

        def third(j, _, g=g):
            part = jnp.where(group == g, h2p[rows_at(j, POS), :], 0.0).astype(bf16)
            a3[rows_at(g * per_group + j, POS), :] = dot_nt(part, f3_w[...])
            return 0

        lax.fori_loop(0, per_group, third, 0)
    one, two = sums_of(a3, fast_rows, BLK)
    put(EX_F3, 0, one)
    put(EX_F3, 1, two)
    st_ref[EX_F3, p.dp, 2:8, :] = jnp.zeros((6, BLK), f32)
    exchange(EX_F3)
    slow_gather.relay()

    total = exchanged(EX_S2)
    s2_norm = affine(row_of(total, 0, 2), row_of(total, 2, 2), slow_count, *vectors(V_S2))
    activate(c2, s2b, slow_rows, B_SLOW, s2_norm[2], s2_norm[3])
    quarter = C_SLOW // 4
    for n in range(4):
        lanes = slice(n * quarter, (n + 1) * quarter)
        for s in range(slow_frames):
            c3[s * POS : (s + 1) * POS, lanes] = dot_nt(frame(s2b, s), s3_w[lanes, :])
        one, two = sums_of(c3.at[:, lanes], slow_rows, quarter)
        put(EX_S3, 2 * n, one)
        put(EX_S3, 8 + 2 * n, two)
    exchange(EX_S3)

    f3_norm = affine(*exchanged_two(EX_F3), fast_count, *vectors(V_F3))
    fast_gather.finish()
    own = a3[rows_at(p.mp, POS), :] * f3_norm[2] + f3_norm[3]
    own = own + xt_ref[rows_at(p.mp + 2, POS), :].astype(f32)
    fast_out[...] = (gelu(own) * mask_ref[...]).T

    def fast_slopes(i, acc):
        mean, scale, grow, base = f3_norm
        at = rows_at(i, RC)
        a = a3[at, :]
        x = xt_ref[pl.ds(pl.multiple_of(i * RC + 2 * POS, RC), RC), :].astype(f32)
        d = gelu_slope(a * grow + base + x) * fc_ref[at, :].astype(f32)
        e3f[at, :] = d
        return acc[0] + eights(d), acc[1] + eights(d * ((a - mean) * scale))

    zero = jnp.zeros((8, BLK), f32)
    one, two = lax.fori_loop(0, fast_rows // RC, fast_slopes, (zero, zero))
    one, two = total_row(one), total_row(two)
    put(EX_BF3, 0, one)
    put(EX_BF3, 1, two)
    st_ref[EX_BF3, p.dp, 2:8, :] = jnp.zeros((6, BLK), f32)
    exchange(EX_BF3)
    put_vector(V_F3[0], two)
    put_vector(V_F3[1], one)

    slow_gather.finish()
    out.drain()
    if not keep:
        from_natural(natural_ref, sc_ref, mask_ref[...], slow_frames)
    total = exchanged(EX_S3)
    s3_norm = affine(row_of(total, 0, 8), row_of(total, 8, 8), slow_count8, *vectors(V_S3))

    def slope_three(at, lanes, norm):
        a = c3[at, lanes]
        pre = a * norm[2] + norm[3] + xs_ref[at, lanes].astype(f32)
        return a, gelu_slope(pre) * sc_ref[at, lanes].astype(f32)

    for n in range(4):
        lanes = slice(n * quarter, (n + 1) * quarter)
        norm = [v[:, lanes] for v in s3_norm]

        def slow_slopes(i, acc, lanes=lanes, norm=norm):
            at = rows_at(i, RC)
            a, d = slope_three(at, lanes, norm)
            if keep:
                e3[at, lanes] = d
            return acc[0] + eights(d), acc[1] + eights(d * ((a - norm[0]) * norm[1]))

        zero = jnp.zeros((8, quarter), f32)
        one, two = lax.fori_loop(0, slow_rows // RC, slow_slopes, (zero, zero))
        one, two = total_row(one), total_row(two)
        put(EX_BS3, 2 * n, one)
        put(EX_BS3, 8 + 2 * n, two)
        put_vector(V_S3[0] + 2 * n, two)
        put_vector(V_S3[1] + 2 * n, one)
    exchange(EX_BS3)

    first_channel = p.mp * share
    at_lane = pl.ds(pl.multiple_of(first_channel // BLK * BLK, BLK), BLK)
    lane_shift = lax.rem(first_channel, BLK)
    own_rows = first_channel // BLK
    own_norm = [
        sum(
            jnp.where(own_rows == j, v[:, j * BLK : (j + 1) * BLK], 0.0)
            for j in range(C_SLOW // BLK)
        )
        for v in s3_norm
    ]

    def to_channels(block):
        turned = block.T
        if share == BLK:
            return turned
        return sum(
            jnp.where(lane_shift == k * share, turned[k * share : (k + 1) * share, :], 0.0)
            for k in range(BLK // share)
        )

    for s in range(slow_frames):
        at = slice(s * POS, (s + 1) * POS)
        pre = c3[at, at_lane] * own_norm[2] + own_norm[3] + xs_ref[at, at_lane].astype(f32)
        slow_out[:, at] = to_channels(gelu(pre) * mask_ref[...])
        own3_ref[at, :] = gelu_slope(pre) * sc_ref[at, at_lane].astype(f32)

    q0, q1 = back_vectors(*exchanged_two(EX_BF3), fast_count, f3_norm)
    raw_grads(a3, e3f, da3f, fast_rows, BLK, f3_norm, q0, q1)
    for j in range(per_group):
        total = jnp.zeros((POS, BLK), f32)
        for g in range(GROUPS):
            part = dot_nn(frame(da3f, g * per_group + j), f3_w[...])
            total = total + jnp.where(group == g, part, 0.0)
        ep[j * POS : (j + 1) * POS, :] = total
    one, two = slopes(a2p, ep, group_rows, BLK, f2_norm)
    put(EX_BF2, 0, fold_lanes(one))
    put(EX_BF2, 1, fold_lanes(two))
    st_ref[EX_BF2, p.dp, 2:8, :] = jnp.zeros((6, BLK), f32)
    exchange(EX_BF2)
    vec_two = jnp.where(group == 2, fold_lanes(two), 0.0)
    vec_two = vec_two + jnp.where(group == 3, fold_lanes(one), 0.0)

    total = exchanged(EX_BS3)
    q0, q1 = back_vectors(row_of(total, 0, 8), row_of(total, 8, 8), slow_count8, s3_norm)
    for n in range(4):
        lanes = slice(n * quarter, (n + 1) * quarter)
        norm = [v[:, lanes] for v in s3_norm]
        q0n, q1n = q0[:, lanes], q1[:, lanes]

        def raw_three(i, _, lanes=lanes, norm=norm, q0n=q0n, q1n=q1n):
            at = rows_at(i, RC)
            if keep:
                a, d = c3[at, lanes], e3[at, lanes]
            else:
                a, d = slope_three(at, lanes, norm)
            da = norm[2] * d - mask_at(i, quarter) * (q0n + a * q1n)
            da3[at, lanes] = da.astype(bf16)
            return 0

        lax.fori_loop(0, slow_rows // RC, raw_three, 0)
    for s in range(slow_frames):
        at = slice(s * POS, (s + 1) * POS)
        e[at, :] = dot_nn(da3[at, :], s3_w[...])
    one, two = slopes(c2, e, slow_rows, B_SLOW, s2_norm)
    put(EX_B2, 0, one)
    put(EX_B2, 2, two)
    st_ref[EX_B2, p.dp, 4:8, :] = jnp.zeros((4, BLK), f32)
    exchange(EX_B2)
    put_vector(V_S2[0], two)
    put_vector(V_S2[1], one)

    def to_flat(at, blocks, offset, tall, lane, value):
        flat_ref[pl.ds(at + offset * blocks + lane, tall, stride=blocks), :] = value

    for n in range(4):
        part = dot_tn(da3[:, n * quarter : (n + 1) * quarter], s2b[...])
        for j in range(2):
            to_flat(AT_S3, 2, n * quarter, quarter, j, part[:, j * BLK : (j + 1) * BLK])

    q0, q1 = back_vectors(*exchanged_two(EX_BF2), fast_count, f2_norm)
    raw_grads(a2p, ep, d2p, group_rows, BLK, f2_norm, q0, q1)
    for j in range(per_group):
        ep[j * POS : (j + 1) * POS, :] = dot_nn(frame(d2p, j), f2_w[...])
    one, two = slopes(a1p, ep, group_rows, BLK, f1_norm)
    put(EX_BF1, 0, fold_lanes(one))
    put(EX_BF1, 1, fold_lanes(two))
    st_ref[EX_BF1, p.dp, 2:8, :] = jnp.zeros((6, BLK), f32)
    exchange(EX_BF1)
    vec_one = jnp.where(group == 0, fold_lanes(two), 0.0)
    vec_one = vec_one + jnp.where(group == 1, fold_lanes(one), 0.0)
    put_vector(0, vec_one + vec_two)

    total = exchanged(EX_B2)
    q0, q1 = back_vectors(row_of(total, 0, 2), row_of(total, 2, 2), slow_count, s2_norm)
    raw_grads(c2, e, da2, slow_rows, B_SLOW, s2_norm, q0, q1)
    for s in range(slow_frames):
        parts = [
            dot_nn(frame(da2, s - k + 1), s2_w[:, k * B_SLOW : (k + 1) * B_SLOW])
            for k in range(3)
            if 0 <= s - k + 1 < slow_frames
        ]
        e[s * POS : (s + 1) * POS, :] = functools.reduce(lambda u, v: u + v, parts)
    one, two = slopes(c1, e, slow_rows, B_SLOW, s1_norm)
    put(EX_B1, 0, one)
    put(EX_B1, 2, two)
    st_ref[EX_B1, p.dp, 4:8, :] = jnp.zeros((4, BLK), f32)
    exchange(EX_B1)
    put_vector(V_S1[0], two)
    put_vector(V_S1[1], one)

    for k in range(3):
        low, high = max(0, 1 - k), min(slow_frames, slow_frames + 1 - k)
        part = dot_tn(
            da2[low * POS : high * POS, :], s1b[(low + k - 1) * POS : (high + k - 1) * POS, :]
        )
        for j in range(2):
            to_flat(AT_S2, 6, 0, B_SLOW, 2 * k + j, part[:, j * BLK : (j + 1) * BLK])

    total = jnp.zeros((BLK, BLK), f32)
    for g in range(GROUPS):
        at = slice(g * group_rows, (g + 1) * group_rows)
        total = total + jnp.where(group == g, dot_tn(da3f[at, :], h2p[...]), 0.0)

    def to_blocks(value, at):
        n = value.shape[0] // GROUPS
        square_ref[: value.shape[0], :] = fold_lanes(value)
        flat_ref[at : at + n, :] = sum(
            jnp.where(group == r, square_ref[pl.ds(r, n, stride=GROUPS), :], 0.0)
            for r in range(GROUPS)
        )

    to_blocks(total, AT_F3)
    square = dot_tn(d2p[...], h1p[...])
    to_blocks(
        sum(
            jnp.where(group == g, square[g * B_FAST : (g + 1) * B_FAST, :], 0.0)
            for g in range(GROUPS)
        ),
        AT_F2,
    )

    total = exchanged(EX_B1)
    q0, q1 = back_vectors(row_of(total, 0, 2), row_of(total, 2, 2), slow_count, s1_norm)
    raw_grads(c1, e, da1, slow_rows, B_SLOW, s1_norm, q0, q1)
    for s in range(slow_frames):
        at = slice(s * POS, (s + 1) * POS)
        e[at, :] = dot_nn(da1[at, :], s1_w[:, C_SLOW:])
    one, two = slopes(zb, e, slow_rows, C_LAT, lat_norm)
    put(EX_BLAT, 0, one)
    put(EX_BLAT, 2, two)
    st_ref[EX_BLAT, p.dp, 4:8, :] = jnp.zeros((4, BLK), f32)
    exchange(EX_BLAT)
    put_vector(V_LAT[0], two)
    put_vector(V_LAT[1], one)

    for s in range(slow_frames):
        at = slice(s * POS, (s + 1) * POS)
        value = own3_ref[at, :] + dot_nn(da1[at, :], s1_w[:, at_lane])
        slow_grad[:, at] = to_channels(value * mask_ref[...])

    q0, q1 = back_vectors(*exchanged_two(EX_BF1), fast_count, f1_norm)
    raw_grads(a1p, ep, d1p, group_rows, BLK, f1_norm, q0, q1)
    for k in range(3):
        tap = jnp.zeros((B_FAST, BLK), f32)
        for g in range(GROUPS):
            at = (g * per_group + k + 1) * POS
            part = dot_tn(d1p[...], xt_ref[at : at + group_rows, :])
            tap = tap + part[g * B_FAST : (g + 1) * B_FAST, :]
        to_flat(AT_F1, 3, 0, B_FAST, k, tap)

    for n in range((C_SLOW + C_LAT) // quarter):
        if n < 4:
            right = xs_ref[:, n * quarter : (n + 1) * quarter]
        else:
            right = latb[...]
        part = dot_tn(da1[...], right)
        for j in range(2):
            to_flat(AT_S1, 10, 0, B_SLOW, 2 * n + j, part[:, j * BLK : (j + 1) * BLK])

    near_grad = e3f[rows_at(p.mp, POS), :]
    for k in range(3):
        f = p.mp - k + 1
        there = (f >= 0) & (f < frames)
        g, j = f // per_group, lax.rem(f, per_group)
        g, j = jnp.where(there, g, 0), jnp.where(there, j, 0)
        left = jnp.where((group == g) & there, d1p[rows_at(j, POS), :], 0.0).astype(bf16)
        near_grad = near_grad + dot_nn(left, f1_w[:, k * BLK : (k + 1) * BLK])

    total = exchanged(EX_BLAT)
    q0, q1 = back_vectors(row_of(total, 0, 2), row_of(total, 2, 2), slow_count, lat_norm)
    raw_grads(zb, e, dz, slow_rows, C_LAT, lat_norm, q0, q1)
    for k in range(5):
        tap = functools.reduce(
            lambda u, v: u + v,
            [dot_tn(frame(dz, s), frame(xt_ref, 4 * s + k)) for s in range(slow_frames)],
        )
        to_flat(AT_LAT, 5, 0, C_LAT, k, tap)

    height = up(slots, 16)
    g_copies = []

    def window_of(device):
        return flat_ref[pl.ds(start_ref[device], height), :]

    for i in range(1, nd):
        peer = lax.rem(p.dp + i, nd)
        win_ref[0, i - 1] = window_of(peer * nm + p.mp).astype(bf16)
        copy = pltpu.make_async_remote_copy(
            src_ref=win_ref.at[0, i - 1],
            dst_ref=win_ref.at[1, i - 1],
            send_sem=g_send.at[i - 1],
            recv_sem=g_recv.at[i - 1],
            device_id=peers[i - 1],
            device_id_type=MESH,
        )
        copy.start()
        g_copies.append(copy)

    later = lax.rem(p.mp + 2, 4)
    s = (p.mp + 2) // 4
    for tap, at, there in (
        (later, s, s < slow_frames),
        (later + 4, s - 1, (later == 0) & (s > 0)),
    ):
        tap, at = jnp.where(there, tap, 0), jnp.where(there, at, 0)
        left = jnp.where(there, dz[rows_at(at, POS), :], 0.0).astype(bf16)
        weight = lat_w[:, pl.ds(pl.multiple_of(tap * BLK, BLK), BLK)]
        near_grad = near_grad + dot_nn(left, weight)
    fast_grad[...] = (near_grad * mask_ref[...]).T

    total = window_of(p.dp * nm + p.mp)
    for i in range(1, nd):
        arrived(win_ref.at[1, i - 1], g_recv.at[i - 1])
        total = total + win_ref[1, i - 1].astype(f32)
    grad_out[...] = total
    for copy in ex_copies + g_copies:
        copy.wait_send()


def call_main(cfg, starts, crop, xt, xs, weights, fcot, scot):
    nd, nm, frames, slow_frames, share, slots = cfg
    height = up(slots, 16)
    slow_rows, fast_rows = slow_frames * POS, frames * POS
    group_rows = fast_rows // GROUPS
    keep = share == BLK
    smem = pl.BlockSpec(memory_space=pltpu.SMEM)
    vmem = pl.BlockSpec(memory_space=pltpu.VMEM)
    dma = pltpu.SemaphoreType.DMA
    out_shapes = (
        (C_FAST, POS), (share, slow_rows), (C_FAST, POS), (share, slow_rows), (height, BLK)
    )
    scratch = [
        ((POS, BLK), f32),
        ((fast_rows, BLK), bf16),
        ((slow_rows, C_SLOW), bf16),
        ((16, BLK) if keep else (C_SLOW, slow_rows), bf16),
    ]
    scratch += [((slow_rows, 256), bf16)] * 7
    scratch += [
        ((slow_rows, 256), f32),
        ((slow_rows, 256), f32),
        ((slow_rows, C_SLOW), f32),
        ((slow_rows, 256), f32),
        ((slow_rows, C_SLOW) if keep else (8, BLK), f32),
        ((group_rows, BLK), f32),
        ((group_rows, BLK), f32),
        ((group_rows, BLK), bf16),
        ((group_rows, BLK), bf16),
        ((group_rows, BLK), bf16),
        ((group_rows, BLK), bf16),
        ((group_rows, BLK), f32),
        ((fast_rows, BLK), f32),
        ((fast_rows, BLK), f32),
        ((BLK, BLK), f32),
        ((up(NBLK + height, 64), BLK), f32),
        ((slow_rows, BLK), f32),
        ((2, nd - 1, height, BLK), bf16),
        ((12, nd, 8, BLK), f32),
        ((2, nd, 16, BLK), f32),
    ]
    return pl.pallas_call(
        functools.partial(main_kernel, cfg),
        out_shape=tuple(jax.ShapeDtypeStruct(s, f32) for s in out_shapes),
        in_specs=[smem, smem] + [vmem] * 12,
        out_specs=tuple(vmem for _ in out_shapes),
        scratch_shapes=[pltpu.VMEM(s, t) for s, t in scratch]
        + [
            dma((nm,)),
            dma((nm,)),
            dma((2 * (nm - 1),)),
            dma((EXCHANGES, nd - 1)),
            dma((EXCHANGES, nd - 1)),
            dma((nd - 1,)),
            dma((nd - 1,)),
        ],
        compiler_params=pltpu.CompilerParams(
            collective_id=1, has_side_effects=True, vmem_limit_bytes=60 << 20
        ),
        name="block",
    )(starts, crop, xt, xs, *weights, fcot, scot)


def adam_kernel(cfg, start_ref, count_ref, grad, master, one, two, w_out, one_out, two_out, low_out):
    nd, nm, frames, slow_frames, share, slots = cfg
    me = lax.axis_index("dp") * nm + lax.axis_index("mp")
    row = lax.broadcasted_iota(jnp.int32, (slots, BLK), 0)
    living = row < count_ref[me]
    block = row + start_ref[me]
    rate = jnp.full((slots, BLK), 0.2, f32)
    for at, width in (
        (AT_VEC, B_SLOW),
        (AT_S3, 3 * B_SLOW),
        (AT_S2, C_SLOW + C_LAT),
        (AT_S1, 5 * C_FAST),
        (AT_LAT, B_FAST),
        (AT_F2, 3 * C_FAST),
    ):
        rate = jnp.where(block < at, 0.5 / math.sqrt(width), rate)
    decay = jnp.where(block < AT_VEC, decay_rate, 0.0)
    g = grad[:slots, :]
    first = beta_first * one[...] + (1.0 - beta_first) * g
    second = beta_second * two[...] + (1.0 - beta_second) * g * g
    lift_one = 1.0 - beta_first**STEP
    lift_two = 1.0 - beta_second**STEP
    update = first / lift_one / (jnp.sqrt(second / lift_two) + adam_eps)
    weight = master[...]
    weight = jnp.where(living, weight - rate * (update + decay * weight), 0.0)
    w_out[...] = weight
    one_out[...] = jnp.where(living, first, 0.0)
    two_out[...] = jnp.where(living, second, 0.0)
    low_out[...] = weight.astype(bf16)


def call_adam(cfg, starts, counts, grad, master, one, two):
    shape = master.shape
    smem = pl.BlockSpec(memory_space=pltpu.SMEM)
    vmem = pl.BlockSpec(memory_space=pltpu.VMEM)
    return pl.pallas_call(
        functools.partial(adam_kernel, cfg),
        out_shape=tuple(jax.ShapeDtypeStruct(shape, t) for t in (f32, f32, f32, bf16)),
        in_specs=[smem, smem] + [vmem] * 4,
        out_specs=(vmem,) * 4,
        compiler_params=pltpu.CompilerParams(vmem_limit_bytes=32 << 20),
        name="adam",
    )(starts, counts, grad, master, one, two)


def solution(mesh):
    nd, nm = mesh.shape["dp"], mesh.shape["mp"]

    def local(fast_in, slow_in, fast_cot, slow_cot, crop, owner, master, one, two):
        cfg = (nd, nm, fast_in.shape[1] * nm, slow_in.shape[1], slow_in.shape[0], master.shape[0])
        devices = jnp.arange(nd * nm, dtype=jnp.int32)[:, None]
        mine = owner[None, :] == devices
        spot = jnp.arange(NBLK, dtype=jnp.int32)[None, :]
        starts = jnp.min(jnp.where(mine, spot, NBLK), 1)
        counts = jnp.sum(mine.astype(jnp.int32), 1)
        fast = fast_in.reshape(C_FAST, -1)
        slow = slow_in.reshape(slow_in.shape[0], -1)
        fcot = fast_cot.reshape(C_FAST, -1)
        scot = slow_cot.reshape(slow_in.shape[0], -1)
        gathered, xt, xs = call_gather(cfg, starts, counts, crop, master, fast, slow)
        weights = call_weights(cfg, starts, gathered)
        fast_out, slow_out, fast_grad, slow_grad, grad = call_main(
            cfg, starts, crop, xt, xs, weights, fcot, scot
        )
        new = call_adam(cfg, starts, counts, grad, master, one, two)
        return (
            fast_out.reshape(fast_in.shape),
            slow_out.reshape(slow_in.shape),
            fast_grad.reshape(fast_in.shape),
            slow_grad.reshape(slow_in.shape),
            *new,
        )

    return jax.shard_map(
        local,
        mesh=mesh,
        in_specs=(
            P(None, "mp", "dp", None),
            P("mp", None, "dp", None),
            P(None, "mp", "dp", None),
            P("mp", None, "dp", None),
            P("dp"),
            P(),
            P(("dp", "mp"), None),
            P(("dp", "mp"), None),
            P(("dp", "mp"), None),
        ),
        out_specs=(
            P(None, "mp", "dp", None),
            P("mp", None, "dp", None),
            P(None, "mp", "dp", None),
            P("mp", None, "dp", None),
            P(("dp", "mp"), None),
            P(("dp", "mp"), None),
            P(("dp", "mp"), None),
            P(("dp", "mp"), None),
        ),
        check_vma=False,
    )
```

time: 1040 us -> 130 us (0.12)
  blocking collectives: 526 us -> 0 us
  local copies, waits for them, and re-layouts: 236 us -> 21.9 us
  waiting for transfers between devices: 153 us -> 0 us
  Pallas kernels: 0 us -> 104 us
  other arithmetic: 40.5 us -> 1.1 us
  starting transfers between devices: 36.7 us -> 0 us
  matrix products: 21.9 us -> 0 us
  between operations: 16.4 us -> 1.38 us
    psum x14 -> x0, blocking collectives: 304 us -> none  [the longest x6 238 us: fast_total(): return lax.psum(parts, ('dp', 'mp'))]
    unnamed x1 -> x0, blocking collectives: 174 us -> none
    reduce_scatter x3 -> x0, waiting for transfers between devices: 115 us -> none  [spread_sum(): lax.psum_scatter(jnp.dot(block, inputs, preferred_element_type=jnp.float3...]
    pallas_call x0 -> x4, Pallas kernels: none -> 104 us  [the longest x1 58.1 us: call_main(): pl.pallas_call(functools.partial(main_kernel, cfg), out_shape=tuple((jax....]
    scatter x3 -> x0, local copies, waits for them, and re-layouts: 103 us -> none  [the longest x1 36.1 us: local(): living = jnp.zeros((devices * slots,), jnp.float32).at[position].set(1.0)]
    dynamic_update_slice x12 -> x0, local copies, waits for them, and re-layouts: 49.1 us -> none  [the longest x1 43.4 us: local(): lax.dynamic_update_slice_in_dim(jnp.zeros((B_SLOW, 3, B_SLOW), jnp.float3...]
    all_gather x2 -> x0, blocking collectives: 48.3 us -> none  [fold_back(): lax.all_gather(a, 'mp', axis=0, tiled=True)]
    all_gather x2 -> x0, waiting for transfers between devices: 37.5 us -> none  [the longest x1 37.5 us: local(): lax.all_gather(master.astype(jnp.bfloat16), ('dp', 'mp'), axis=0, tiled=T...]
  transfers between devices with their start and end apart: 16 -> 0, of which waited for: 4 -> 0; matrix products, arithmetic and copies ran while one was open for 41% -> 0% of each run, Pallas kernels for 0% -> 0%
where the time goes in v1:
time: 130 us; the launch traced here: 129 us
  Pallas kernels  104 us (80%)
  local copies, waits for them, and re-layouts  21.9 us (17%)
  between operations  1.38 us (1%)
    pallas_call x1, Pallas kernels, call_main(): pl.pallas_call(functools.partial(main_kernel, cfg), out_shape=tuple((jax....  58.1 us
    pallas_call x1, Pallas kernels, call_gather(): pl.pallas_call(functools.partial(gather_kernel, cfg), out_shape=(jax.Shap...  41.8 us
    unnamed x44, local copies, waits for them, and re-layouts  18 us
    pallas_call x1, Pallas kernels, call_weights(): pl.pallas_call(functools.partial(weights_kernel, cfg), out_shape=tuple((j...  2.62 us

profile of v1, /device:TPU:25, one launch (start us, length us, event | category | flops | bytes accessed | tf_op | source)
XLA Modules:
  0.0 128.7 jit_solution(7760821616278807834)
XLA Ops:
  0.6 0.0 copy-start.19
  0.6 1.1 convert_reduce_fusion
  1.7 0.0 copy-start.17
  2.4 0.9 copy.25
  3.3 0.0 copy-start.2
  3.3 0.9 copy-done.2
  4.3 0.0 copy-start.13
  4.3 0.8 copy-done.13
  5.1 41.8 %gather.1 = (bf16[32,496,128]{2,1,0:T(8,128)(2,1)}, bf16[3072,128]{1,0:T(8,128)(2,1)S(1)}, bf16[512,1024]{1,0:T(8,128)(2,1)S(1)}) custom-call(s32[32]{0:T(128)S(1)} %get-tuple-element.65.start_ref, s32[32]{0:T(128)S(1)} %get-tuple-element.64.count_ref, s32[1]{0:T(128)S(6)} %copy.27.crop_ref, f32[476,128]{1,0:T(8,128)S(1)} %copy-done.2, ...), custom_call_target="tpu_custom_call" | custom-call | tf_op jit(solution)/shard_map/gather/pallas_call | solution.py:325
  46.9 0.0 copy-start.1
  46.9 1.0 copy-done.1
  47.9 0.0 copy-start.4
  47.9 0.9 copy-done.4
  48.8 0.0 copy-start
  48.8 2.1 %copy-done = bf16[32,496,128]{2,1,0:T(8,128)(2,1)S(1)} copy-done((bf16[32,496,128]{2,1,0:T(8,128)(2,1)S(1)}, bf16[32,496,128]{2,1,0:T(8,128)(2,1)}, u32[]{:S(2)}) %copy-start) | copy-done | bytes 4063256
  51.0 0.0 copy-start.3
  51.0 0.0 copy-start.9
  51.0 0.0 copy-start.10
  51.0 2.6 %weights.1 = (bf16[256,640]{1,0:T(8,128)(2,1)S(1)}, bf16[256,1280]{1,0:T(8,128)(2,1)S(1)}, bf16[256,768]{1,0:T(8,128)(2,1)S(1)}, bf16[1024,256]{1,0:T(8,128)(2,1...) custom-call(s32[32]{0:T(128)S(1)} %get-tuple-element.65.start_ref, ...), custom_call_target="tpu_custom_call" | custom-call | tf_op jit(solution)/shard_map/weights/pallas_call | solution.py:424
  53.6 0.0 copy-start.5
  53.6 0.8 copy-done.5
  54.5 0.0 copy-start.6
  54.5 0.8 copy-done.6
  55.3 0.0 copy-start.7
  55.3 0.7 copy-done.7
  56.0 0.0 copy-start.8
  56.0 0.7 copy-done.8
  56.7 0.0 copy-start.12
  56.7 0.6 copy-done.12
  57.4 0.0 copy-start.14
  57.4 0.6 copy-done.14
  58.0 0.6 copy-done.15
  58.6 0.6 copy-done.16
  59.2 0.0 copy-done.19
  59.2 0.7 copy.26
  59.9 0.0 copy-done.17
  59.9 58.1 %block.1 = (f32[128,256]{1,0:T(8,128)}, f32[128,512]{1,0:T(8,128)}, f32[128,256]{1,0:T(8,128)}, f32[128,512]{1,0:T(8,128)}, f32[480,128]{1,0:T(8,128)}) custom-call(s32[32]{0:T(128)} %copy-done.17, s32[1]{0:T(128)S(6)} %copy.27.crop_ref, bf16[3072,128]{1,0:T(8,128)(2,1)} %copy-done.4, bf16[512,1024]{1,0:T(8,128)(2,1)} %copy-done.1, ...), custom_call_target="tpu_custom_call" | custom-call | tf_op jit(solution)/shard_map/block/pallas_call | solution.py:1063
  118.0 1.7 %copy.21 = f32[128,1,1,256]{3,2,1,0:T(1,128)} copy(f32[128,1,1,256]{3,0,2,1:T(8,128)} %bitcast.18) | data formatting | bytes 262144
  119.7 2.0 %reshape.49 = f32[128,2,1,256]{3,2,1,0:T(1,128)} reshape(f32[128,512]{1,0:T(8,128)} %get-tuple-element.40) | data formatting | bytes 524288 | tf_op jit(solution)/shard_map/reshape | solution.py:1152
  121.7 1.7 %copy.23 = f32[128,1,1,256]{3,2,1,0:T(1,128)} copy(f32[128,1,1,256]{3,0,2,1:T(8,128)} %bitcast.17) | data formatting | bytes 262144
  123.4 2.0 %reshape.50 = f32[128,2,1,256]{3,2,1,0:T(1,128)} reshape(f32[128,512]{1,0:T(8,128)} %get-tuple-element.42) | data formatting | bytes 524288 | tf_op jit(solution)/shard_map/reshape | solution.py:1154
  125.3 0.0 copy-done.3
  125.3 0.0 copy-done.9
  125.3 0.0 copy-done.10
  125.3 0.0 copy-start.11
  125.4 0.9 copy-done.11
  126.3 0.7 copy-done.18
  126.9 1.7 %adam.1 = (f32[476,128]{1,0:T(8,128)}, f32[476,128]{1,0:T(8,128)}, f32[476,128]{1,0:T(8,128)}, bf16[476,128]{1,0:T(8,128)(2,1)}) custom-call(s32[32]{0:T(128)S(1)} %copy-done.18, s32[32]{0:T(128)S(1)} %get-tuple-element.64.count_ref, f32[480,128]{1,0:T(8,128)S(1)} %copy-done.11, f32[476,128]{1,0:T(8,128)S(1)} %copy-done.3, f32[476,128]{1,0:T(8,128)S(1)} %copy-done.9, ...), custom_call_target="tpu_custom_call" | custom-call | tf_op jit(solution)/shard_map/adam/pallas_call | solution.py:1120
  (3 shorter events, 0.0 us)
Async XLA Ops:
  0.6 58.6 %copy-start.19 = (bf16[128,2,1,256]{3,1,2,0:T(2,128)(2,1)S(1)}, bf16[128,2,1,256]{3,1,2,0:T(2,128)(2,1)}, u32[]{:S(2)}) copy-start(bf16[128,2,1,256]{3,1,2,0:T(2,128)(2,1)} %param.12) | copy-start | bytes 393220
  1.7 58.1 %copy-start.17 = (s32[32]{0:T(128)}, s32[32]{0:T(128)S(1)}, u32[]{:S(2)}) copy-start(s32[32]{0:T(128)S(1)} %get-tuple-element.65.start_ref) | copy-start | bytes 388
  3.3 0.9 copy-start.2
  4.3 0.8 copy-start.13
  46.9 1.0 copy-start.1
  47.9 0.9 copy-start.4
  48.8 2.2 %copy-start = (bf16[32,496,128]{2,1,0:T(8,128)(2,1)S(1)}, bf16[32,496,128]{2,1,0:T(8,128)(2,1)}, u32[]{:S(2)}) copy-start(bf16[32,496,128]{2,1,0:T(8,128)(2,1)} %get-tuple-element.30.p_ref) | copy-start | bytes 12189700
  51.0 74.4 %copy-start.3 = (f32[476,128]{1,0:T(8,128)S(1)}, f32[476,128]{1,0:T(8,128)}, u32[]{:S(2)}) copy-start(f32[476,128]{1,0:T(8,128)} %master.1) | copy-start | bytes 731140
  51.0 74.4 %copy-start.9 = (f32[476,128]{1,0:T(8,128)S(1)}, f32[476,128]{1,0:T(8,128)}, u32[]{:S(2)}) copy-start(f32[476,128]{1,0:T(8,128)} %one.1) | copy-start | bytes 731140
  51.0 74.4 %copy-start.10 = (f32[476,128]{1,0:T(8,128)S(1)}, f32[476,128]{1,0:T(8,128)}, u32[]{:S(2)}) copy-start(f32[476,128]{1,0:T(8,128)} %two.1) | copy-start | bytes 731140
  53.6 0.9 copy-start.5
  54.5 0.8 copy-start.6
  55.3 0.7 copy-start.7
  56.0 0.7 copy-start.8
  56.7 0.6 copy-start.12
  57.4 0.6 copy-start.14
  58.0 0.6 copy-start.15
  58.6 0.6 copy-start.16
  125.3 0.9 copy-start.11
  126.3 0.7 copy-start.18

commit v2 on v1

--- a/solution.py
+++ b/solution.py
@@ -181,49 +181,219 @@
         pl.semaphore_signal(barrier, inc=1, device_id=device, device_id_type=MESH)
 
 
-def gather_sizes(nd, nm):
+def lane_group():
+    return lax.broadcasted_iota(jnp.int32, (1, BLK), 1) // B_FAST
+
+
+def fold_lanes(v):
+    v = v + pltpu.roll(v, B_FAST, 1)
+    return v + pltpu.roll(v, 2 * B_FAST, 1)
+
+
+EX_LAT, EX_S1, EX_S2, EX_B2, EX_B1, EX_BLAT = range(6)
+EX_F1, EX_F2, EX_F3, EX_BF3, EX_BF2, EX_BF1 = range(6, 12)
+EX_S3, EX_BS3 = 12, 13
+EXCHANGES = 14
+
+ARGS = ("crop", "owner", "owners", "master", "fast", "slow", "fcot", "scot")
+
+
+def sizes(cfg):
+    nd, nm, frames, slow_frames, share, slots = cfg
     nb = 2 if nm % 2 == 0 else 1
     na, nx = nm // nb, nd // 2
     params = (na - 1) + (nb - 1) + (nx - 1) + 1
     params += (na - 1) * ((nb - 1) + (nx - 1) + 1)
     params += na * (nb - 1) * (1 + nx - 1) + na * (nx - 1) * (1 + nb - 1)
     params += na * (nb - 1) * (nx - 1)
-    arrays = nm - 1
-    return params, arrays
-
-
-def gather_kernel(
-    cfg, start_ref, count_ref, crop_ref, master_ref, fast_ref, slow_ref,
-    p_ref, xt_ref, xs_ref, shift_ref, natural_ref, p_recv, f_recv, s_recv, send_sems
-):
+    return params + 4 * (nm - 1)
+
+
+def outputs(cfg):
     nd, nm, frames, slow_frames, share, slots = cfg
+    halves = POS // BLK
+    result = [
+        ("fast_out", (C_FAST * halves, BLK), f32),
+        ("slow_out", (share * slow_frames * halves, BLK), f32),
+        ("fast_grad", (C_FAST * halves, BLK), f32),
+        ("slow_grad", (share * slow_frames * halves, BLK), f32),
+        ("grad", (up(slots, 16), BLK), f32),
+    ]
+    if share != BLK:
+        result += [
+            ("natural_x", (C_SLOW, slow_frames * POS), bf16),
+            ("natural_c", (C_SLOW, slow_frames * POS), bf16),
+        ]
+    return result
+
+
+def scratch(cfg):
+    nd, nm, frames, slow_frames, share, slots = cfg
+    keep = share == BLK
+    devices = nd * nm
     rows = up(slots + 15, 16)
+    height = up(slots, 16)
+    halves = POS // BLK
+    slow_rows, fast_rows = slow_frames * POS, frames * POS
+    group_rows = fast_rows // GROUPS
+    vmem, smem, dma = pltpu.VMEM, pltpu.SMEM, pltpu.SemaphoreType.DMA
+    result = [
+        ("owner_v", vmem((up(NBLK, 1024) // BLK, BLK), jnp.int32)),
+        ("owner_s", smem((NBLK,), jnp.int32)),
+        ("run_device", smem((devices,), jnp.int32)),
+        ("run_start", smem((devices,), jnp.int32)),
+        ("run_count", smem((devices,), jnp.int32)),
+        ("table_v", vmem((8, BLK), jnp.int32)),
+        ("table_s", smem((8, BLK), jnp.int32)),
+        ("shift", vmem((rows + 16, BLK), f32)),
+        ("p", vmem((devices * (rows // 16), 16, BLK), bf16)),
+        ("q", vmem((devices, 16, BLK), bf16)),
+        ("fast_v", vmem((C_FAST, POS), bf16)),
+        ("slow_v", vmem((share * slow_frames * halves, BLK), bf16)),
+        ("fcot_v", vmem((C_FAST, POS), bf16)),
+        ("scot_v", vmem((share * slow_frames * halves, BLK), bf16)),
+        ("stage", vmem((share * slow_frames * halves, BLK), f32)),
+        ("xt", vmem(((frames + 4) * POS, BLK), bf16)),
+        ("xs", vmem((slow_rows, C_SLOW), bf16)),
+        ("fc", vmem((fast_rows, BLK), bf16)),
+        ("sc", vmem((slow_rows, C_SLOW), bf16)),
+        ("lat_w", vmem((C_LAT, 5 * C_FAST), bf16)),
+        ("s1_w", vmem((B_SLOW, C_SLOW + C_LAT), bf16)),
+        ("s2_w", vmem((B_SLOW, 3 * B_SLOW), bf16)),
+        ("s3_w", vmem((C_SLOW, B_SLOW), bf16)),
+        ("f1_w", vmem((BLK, 3 * C_FAST), bf16)),
+        ("f2_w", vmem((BLK, BLK), bf16)),
+        ("f3_w", vmem((BLK, BLK), bf16)),
+        ("vec", vmem((32, BLK), f32)),
+        ("mask", vmem((POS, BLK), f32)),
+    ]
+    if not keep:
+        result += [
+            ("piece", vmem((share, slow_rows), bf16)),
+            ("turn", vmem((BLK, POS), bf16)),
+        ]
+    result += [
+        (name, vmem((slow_rows, 256), bf16))
+        for name in ("zb", "latb", "s1b", "s2b", "da1", "da2")
+    ]
+    result += [
+        ("c1", vmem((slow_rows, 256), f32)),
+        ("c2", vmem((slow_rows, 256), f32)),
+        ("c3", vmem((slow_rows, C_SLOW), f32)),
+        ("e", vmem((slow_rows, 256), f32)),
+        ("e3", vmem((slow_rows, C_SLOW) if keep else (8, BLK), f32)),
+        ("a1p", vmem((group_rows, BLK), f32)),
+        ("a2p", vmem((group_rows, BLK), f32)),
+        ("h1p", vmem((group_rows, BLK), bf16)),
+        ("h2p", vmem((group_rows, BLK), bf16)),
+        ("d1p", vmem((group_rows, BLK), bf16)),
+        ("d2p", vmem((group_rows, BLK), bf16)),
+        ("ep", vmem((group_rows, BLK), f32)),
+        ("a3", vmem((fast_rows, BLK), f32)),
+        ("e3f", vmem((fast_rows, BLK), f32)),
+        ("square", vmem((BLK, BLK), f32)),
+        ("flat", vmem((up(NBLK + height, 64), BLK), f32)),
+        ("own3", vmem((slow_rows, BLK), f32)),
+        ("win", vmem((2, nd - 1, height, BLK), bf16)),
+        ("st", vmem((12, nd, 8, BLK), f32)),
+        ("st16", vmem((2, nd, 16, BLK), f32)),
+        ("out_fast", vmem((C_FAST * halves, BLK), f32)),
+        ("out_slow", vmem((share * slow_frames * halves, BLK), f32)),
+        ("out_fgrad", vmem((C_FAST * halves, BLK), f32)),
+        ("out_sgrad", vmem((share * slow_frames * halves, BLK), f32)),
+        ("out_grad", vmem((height, BLK), f32)),
+        ("p_recv", dma((devices,))),
+        ("x_recv", dma((nm,))),
+        ("xs_recv", dma((nm,))),
+        ("fc_recv", dma((nm,))),
+        ("sc_recv", dma((nm,))),
+        ("sends", dma((sizes(cfg),))),
+        ("ex_send", dma((EXCHANGES, nd - 1))),
+        ("ex_recv", dma((EXCHANGES, nd - 1))),
+        ("g_send", dma((nd - 1,))),
+        ("g_recv", dma((nd - 1,))),
+        ("local", dma((16,))),
+    ]
+    return result
+
+
+def main_kernel(cfg, *refs):
+    nd, nm, frames, slow_frames, share, slots = cfg
+    out_names = [name for name, _, _ in outputs(cfg)]
+    names = list(ARGS) + ["out:" + n for n in out_names] + [n for n, _ in scratch(cfg)]
+    R = dict(zip(names, refs, strict=True))
     p = Place(nd, nm)
-    peers = [p.dev(p.x, p.c, p.off_a(i), p.b) for i in range(1, p.na)]
-    peers += [p.dev(p.x, p.c, p.a, p.off_b(i)) for i in range(1, p.nb)]
-    peers += [p.dev(p.off_x(i), p.c, p.a, p.b) for i in range(1, p.nx)]
-    peers += [p.dev(p.x, 1 - p.c, p.a, p.b)]
-    signal_all(peers)
-
+    devices = nd * nm
+    halves = POS // BLK
+    rows = up(slots + 15, 16)
+    tiles = rows // 16
+    slow_rows, fast_rows = slow_frames * POS, frames * POS
+    per_group = frames // GROUPS
+    group_rows = per_group * POS
+    keep = share == BLK
     me = p.dp * nm + p.mp
-    start = start_ref[me]
-    shift = lax.rem(start, 16)
-    shift_ref[...] = jnp.zeros_like(shift_ref)
-    shift_ref[16 : 16 + slots] = master_ref[...]
-    moved = shift_ref[pl.ds(16 - shift, rows), :]
+
+    peers = [(lax.rem(p.dp + i, nd), p.mp) for i in range(1, nd)]
+    near = [p.dev(p.x, p.c, p.off_a(i), p.b) for i in range(1, p.na)]
+    near += [p.dev(p.x, p.c, p.a, p.off_b(i)) for i in range(1, p.nb)]
+    signal_all(peers + near)
+
+    local_copies = []
+
+    def fetch(source, target):
+        copy = pltpu.make_async_copy(source, target, R["local"].at[len(local_copies)])
+        copy.start()
+        local_copies.append(copy)
+        return copy
+
+    get_owner = fetch(R["owners"], R["owner_v"])
+    get_master = fetch(R["master"], R["shift"].at[pl.ds(16, slots)])
+    get_fast = fetch(R["fast"], R["fast_v"])
+    get_slow = fetch(R["slow"], R["slow_v"])
+    get_fcot = fetch(R["fcot"], R["fcot_v"])
+    get_scot = fetch(R["scot"], R["scot_v"])
+    get_owner_s = fetch(R["owner"], R["owner_s"])
+
+    crop = R["crop"][0]
+    R["mask"][...] = position_mask(crop)
+    tall = crop.astype(f32)
+    area = tall * tall
+    xt_ref, xs_ref, fc_ref, sc_ref = R["xt"], R["xs"], R["fc"], R["sc"]
+    xt_ref[: 2 * POS] = jnp.zeros((2 * POS, BLK), bf16)
+    xt_ref[(frames + 2) * POS :] = jnp.zeros((2 * POS, BLK), bf16)
+
+    get_owner.wait()
+    spot = lax.broadcasted_iota(jnp.int32, (8, BLK), 0) * BLK
+    spot = spot + lax.broadcasted_iota(jnp.int32, (8, BLK), 1)
+    lowest = jnp.full((8, BLK), NBLK, jnp.int32)
+    number = jnp.zeros((8, BLK), jnp.int32)
+    for i in range(up(NBLK, 1024) // 1024):
+        block = spot + i * 1024
+        mine = R["owner_v"][i * 8 : (i + 1) * 8, :] == me
+        mine = mine & (block < NBLK)
+        lowest = jnp.minimum(lowest, jnp.where(mine, block, NBLK))
+        number = number + jnp.where(mine, 1, 0)
+    my_start, my_count = jnp.min(lowest), jnp.sum(number)
+    shift = lax.rem(my_start, 16)
+    get_master.wait()
+    moved = R["shift"][pl.ds(16 - shift, rows), :]
     row = lax.broadcasted_iota(jnp.int32, (rows, BLK), 0)
-    own = (row >= shift) & (row < shift + count_ref[me])
-    p_ref[me] = jnp.where(own, moved, 0.0).astype(bf16)
-
-    pl.semaphore_wait(pltpu.get_barrier_semaphore(), len(peers))
-
-    out = Sender(send_sems)
+    own = (row >= shift) & (row < shift + my_count)
+    p_ref = R["p"]
+
+    def p_slot(slot):
+        return p_ref.at[pl.ds(slot * tiles, tiles)]
+
+    p_slot(me)[...] = jnp.where(own, moved, 0.0).astype(bf16).reshape(tiles, 16, BLK)
+
+    pl.semaphore_wait(pltpu.get_barrier_semaphore(), len(peers) + len(near))
+    out = Sender(R["sends"])
 
     def view(x, c, a, b):
-        return p_ref.at[p.slot(x, c, a, b)]
+        return p_slot(p.slot(x, c, a, b))
 
     def pass_on(source, along_a=False, along_b=False, along_x=False, along_c=False):
-        piece, sem = view(*source), p_recv.at[p.slot(*source)]
+        piece, sem = view(*source), R["p_recv"].at[p.slot(*source)]
         if along_a:
             for i in range(1, p.na):
                 out.send(piece, sem, p.dev(p.x, p.c, p.off_a(i), p.b))
@@ -237,43 +407,107 @@
             out.send(piece, sem, p.dev(p.x, 1 - p.c, p.a, p.b))
 
     def take(source):
-        arrived(view(*source), p_recv.at[p.slot(*source)])
+        arrived(view(*source), R["p_recv"].at[p.slot(*source)])
 
     pass_on((p.x, p.c, p.a, p.b), along_a=True, along_b=True, along_x=True, along_c=True)
 
-    mask = position_mask(crop_ref[0])
-    xt_ref[: 2 * POS] = jnp.zeros((2 * POS, BLK), bf16)
-    xt_ref[(frames + 2) * POS :] = jnp.zeros((2 * POS, BLK), bf16)
-
-    def frame_view(r):
-        return xt_ref.at[pl.ds(pl.multiple_of((r + 2) * POS, POS), POS)]
-
-    frame_view(p.mp)[...] = (fast_ref[...].astype(f32).T * mask).astype(bf16)
-    fast_gather = Gather(p, frame_view, out, f_recv)
-    fast_gather.start()
-
-    if share == BLK:
-
-        def slow_view(r):
-            return xs_ref.at[:, pl.ds(pl.multiple_of(r * BLK, BLK), BLK)]
-
+    mask = R["mask"][...]
+
+    def frame_view(ref, skip):
+        return lambda r: ref.at[pl.ds(pl.multiple_of((r + skip) * POS, POS), POS)]
+
+    def own_frame(target, source):
+        target(p.mp)[...] = (source[...].astype(f32).T * mask).astype(bf16)
+
+    def lane_view(ref):
+        return lambda r: ref.at[:, pl.ds(pl.multiple_of(r * BLK, BLK), BLK)]
+
+    def natural_view(ref):
+        return lambda r: ref.at[pl.ds(pl.multiple_of(r * share, share), share)]
+
+    def own_slow(target, source):
+        stage = R["stage"]
+        stage[...] = source[...].astype(f32)
         for s in range(slow_frames):
-            piece = slow_ref[:, s * POS : (s + 1) * POS].astype(f32).T * mask
-            slow_view(p.mp)[s * POS : (s + 1) * POS, :] = piece.astype(bf16)
+            for h in range(halves):
+                part = stage[pl.ds(h * slow_frames + s, share, stride=halves * slow_frames), :]
+                at = slice(s * POS + h * BLK, s * POS + (h + 1) * BLK)
+                if keep:
+                    turned = part.T * mask[h * BLK : (h + 1) * BLK, :]
+                    target(p.mp)[at, :] = turned.astype(bf16)
+                else:
+                    R["piece"][:, at] = part.astype(bf16)
+        if not keep:
+            pltpu.sync_copy(R["piece"], target(p.mp))
+
+    def from_natural(natural, wide):
+        def block(i, _):
+            s, j = i // (C_SLOW // BLK), lax.rem(i, C_SLOW // BLK)
+            at_row = pl.ds(pl.multiple_of(s * POS, POS), POS)
+            at_lane = pl.ds(pl.multiple_of(j * BLK, BLK), BLK)
+            pltpu.sync_copy(natural.at[at_lane, at_row], R["turn"])
+            piece = R["turn"][...].astype(f32).T * R["mask"][...]
+            wide[at_row, at_lane] = piece.astype(bf16)
+            return 0
+
+        lax.fori_loop(0, slow_frames * (C_SLOW // BLK), block, 0)
+
+    x_view, fc_view = frame_view(xt_ref, 2), frame_view(fc_ref, 0)
+    if keep:
+        xs_view, sc_view = lane_view(xs_ref), lane_view(sc_ref)
     else:
-
-        def slow_view(r):
-            return natural_ref.at[pl.ds(pl.multiple_of(r * share, share), share)]
-
-        slow_view(p.mp)[...] = slow_ref[...]
-    slow_gather = Gather(p, slow_view, out, s_recv)
-    slow_gather.start()
+        xs_view, sc_view = natural_view(R["out:natural_x"]), natural_view(R["out:natural_c"])
+    x_gather = Gather(p, x_view, out, R["x_recv"])
+    xs_gather = Gather(p, xs_view, out, R["xs_recv"])
+    fc_gather = Gather(p, fc_view, out, R["fc_recv"])
+    sc_gather = Gather(p, sc_view, out, R["sc_recv"])
+    get_fast.wait()
+    own_frame(x_view, R["fast_v"])
+    x_gather.start()
+    get_slow.wait()
+    own_slow(xs_view, R["slow_v"])
+
+    get_owner_s.wait()
+    steps = [1 << i for i in reversed(range(max(1, (slots - 1).bit_length())))]
+    owner_s, run_device, run_start, run_count = (
+        R[n] for n in ("owner_s", "run_device", "run_start", "run_count")
+    )
+
+    def run(k, at):
+        device = owner_s[jnp.minimum(at, NBLK - 1)]
+        n = jnp.int32(1)
+        for step in steps:
+            more = n + step
+            last = at + more - 1
+            inside = owner_s[jnp.minimum(last, NBLK - 1)] == device
+            n = jnp.where((more <= slots) & (last < NBLK) & inside, more, n)
+        run_device[k] = device
+        run_start[k] = at
+        run_count[k] = n
+        return at + n
+
+    lax.fori_loop(0, devices, run, jnp.int32(0))
 
     for i in range(1, p.na):
         source = (p.x, p.c, p.off_a(p.na - i), p.b)
         take(source)
         pass_on(source, along_b=True, along_x=True, along_c=True)
-    fast_gather.relay()
+    x_gather.relay()
+    xs_gather.start()
+
+    def tile_of(k):
+        return run_device[k] * tiles - run_start[k] // 16
+
+    def table(k, found):
+        start, last = run_start[k], run_start[k] + run_count[k] - 1
+        final = jnp.minimum(spot * 16 + 15, NBLK - 1)
+        holds = (final >= start) & (final <= last)
+        tile = jnp.where(spot == start // 16, devices * tiles + k, spot + tile_of(k))
+        return jnp.where(holds, tile, found)
+
+    R["table_v"][...] = lax.fori_loop(0, devices, table, jnp.zeros((8, BLK), jnp.int32))
+    get_table = fetch(R["table_v"], R["table_s"])
+
     across = p.na * 3 // 4
     for i in range(p.na):
         for j in range(1, p.nb):
@@ -284,216 +518,106 @@
             source = (p.off_x(j), p.c, p.off_a(p.na - i), p.b)
             take(source)
             pass_on(source, along_b=i >= across, along_c=True)
-    slow_gather.relay()
+    get_fcot.wait()
+    own_frame(fc_view, R["fcot_v"])
+    get_scot.wait()
+    own_slow(sc_view, R["scot_v"])
     for i in range(p.na):
         for j in range(1, p.nb):
             for k in range(1, p.nx):
                 source = (p.off_x(k), p.c, p.off_a(p.na - i), p.off_b(j))
                 take(source)
                 pass_on(source, along_c=True)
+    sc_gather.start()
+    fc_gather.start()
+    xs_gather.relay()
     for i in range(p.na):
         for j in range(p.nb):
             for k in range(p.nx):
                 take((p.off_x(k), 1 - p.c, p.off_a(i), p.off_b(j)))
-    fast_gather.finish()
-    slow_gather.finish()
-    out.drain()
-    if share != BLK:
-        from_natural(natural_ref, xs_ref, mask, slow_frames)
-
-
-def from_natural(natural_ref, wide_ref, mask, slow_frames):
-    def block(i, _):
-        s, j = i // (C_SLOW // BLK), lax.rem(i, C_SLOW // BLK)
-        at_row = pl.ds(pl.multiple_of(s * POS, POS), POS)
-        at_lane = pl.ds(pl.multiple_of(j * BLK, BLK), BLK)
-        piece = natural_ref[at_lane, at_row].astype(f32).T * mask
-        wide_ref[at_row, at_lane] = piece.astype(bf16)
-        return 0
-
-    lax.fori_loop(0, slow_frames * (C_SLOW // BLK), block, 0)
-
-
-def call_gather(cfg, starts, counts, crop, master, fast, slow):
-    nd, nm, frames, slow_frames, share, slots = cfg
-    rows = up(slots + 15, 16)
-    params, arrays = gather_sizes(nd, nm)
-    smem = pl.BlockSpec(memory_space=pltpu.SMEM)
-    vmem = pl.BlockSpec(memory_space=pltpu.VMEM)
-    dma = pltpu.SemaphoreType.DMA
-    natural = (C_SLOW, slow_frames * POS) if share != BLK else (16, BLK)
-    return pl.pallas_call(
-        functools.partial(gather_kernel, cfg),
-        out_shape=(
-            jax.ShapeDtypeStruct((nd * nm, rows, BLK), bf16),
-            jax.ShapeDtypeStruct(((frames + 4) * POS, BLK), bf16),
-            jax.ShapeDtypeStruct((slow_frames * POS, C_SLOW), bf16),
-        ),
-        in_specs=[smem, smem, smem, vmem, vmem, vmem],
-        out_specs=(vmem, vmem, vmem),
-        scratch_shapes=[
-            pltpu.VMEM((rows + 16, BLK), f32),
-            pltpu.VMEM(natural, bf16),
-            dma((nd * nm,)),
-            dma((nm,)),
-            dma((nm,)),
-            dma((params + 2 * arrays,)),
-        ],
-        compiler_params=pltpu.CompilerParams(
-            collective_id=0, has_side_effects=True, vmem_limit_bytes=48 << 20
-        ),
-        name="gather",
-    )(starts, counts, crop, master, fast, slow)
-
-
-def lane_group():
-    return lax.broadcasted_iota(jnp.int32, (1, BLK), 1) // B_FAST
-
-
-def fold_lanes(v):
-    v = v + pltpu.roll(v, B_FAST, 1)
-    return v + pltpu.roll(v, 2 * B_FAST, 1)
-
-
-def weights_kernel(
-    cfg, start_ref, p_ref, lat_ref, s1_ref, s2_ref, s3_ref, f1_ref, f2_ref, f3_ref, vec_ref,
-    flat_ref, square_ref
-):
-    nd, nm, frames, slow_frames, share, slots = cfg
-    rows = up(slots + 15, 16)
-    chunk = 64
-
-    def clear(i, _):
-        flat_ref[pl.ds(pl.multiple_of(i * chunk, chunk), chunk), :] = jnp.zeros((chunk, BLK), f32)
-        return 0
-
-    lax.fori_loop(0, flat_ref.shape[0] // chunk, clear, 0)
-
-    def add(d, _):
-        base = pl.multiple_of(start_ref[d] // 16 * 16, 16)
-        flat_ref[pl.ds(base, rows), :] += p_ref[d].astype(f32)
-        return 0
-
-    lax.fori_loop(0, nd * nm, add, 0)
-
-    def matrix(out_ref, at, tall, blocks):
+    get_table.wait()
+
+    def tile_rows(t):
+        return pl.ds(pl.multiple_of(t * 16, 16), 16)
+
+    q_ref = R["q"]
+
+    def first_tile(k, before):
+        tile = p_ref[run_device[k] * tiles].astype(f32)
+        shared = lax.rem(run_start[k], 16) != 0
+        tile = tile + jnp.where(shared, before, 0.0)
+        q_ref[k] = tile.astype(bf16)
+        last = (run_start[k] + run_count[k] - 1) // 16
+        alone = last == run_start[k] // 16
+        return jnp.where(alone, tile, p_ref[tile_of(k) + last].astype(f32))
+
+    lax.fori_loop(0, devices, first_tile, jnp.zeros((16, BLK), f32))
+    flat_ref, table_s = R["flat"], R["table_s"]
+
+    def lay_out(first_block, end_block):
+        first, end = first_block // 16, up(end_block, 16) // 16
+
+        def one(t):
+            source = table_s[t // BLK, lax.rem(t, BLK)]
+            plain = p_ref[jnp.minimum(source, devices * tiles - 1)]
+            shared = q_ref[jnp.maximum(source - devices * tiles, 0)]
+            tile = jnp.where(source < devices * tiles, plain, shared)
+            flat_ref[tile_rows(t), :] = tile.astype(f32)
+
+        def eight(i, _):
+            for k in range(8):
+                one(first + i * 8 + k)
+            return 0
+
+        lax.fori_loop(0, (end - first) // 8, eight, 0)
+        for t in range(first + (end - first) // 8 * 8, end):
+            one(t)
+
+    def matrix(out_ref, at, height, blocks):
+        lay_out(at, at + height * blocks)
         for j in range(blocks):
-            for o in range(0, tall, 256):
+            for o in range(0, height, 256):
                 out_ref[o : o + 256, j * BLK : (j + 1) * BLK] = flat_ref[
                     pl.ds(at + o * blocks + j, 256, stride=blocks), :
                 ].astype(bf16)
 
-    matrix(lat_ref, AT_LAT, C_LAT, 5)
-    matrix(s1_ref, AT_S1, B_SLOW, 10)
-    matrix(s2_ref, AT_S2, B_SLOW, 6)
-    matrix(s3_ref, AT_S3, C_SLOW, 2)
-    for k in range(3):
-        tap = flat_ref[pl.ds(AT_F1 + k, B_FAST, stride=3), :].astype(bf16)
+    group = lane_group()
+    square_ref = R["square"]
+    lat_w, s1_w, s2_w, s3_w = R["lat_w"], R["s1_w"], R["s2_w"], R["s3_w"]
+    f1_w, f2_w, f3_w, vec_ref = R["f1_w"], R["f2_w"], R["f3_w"], R["vec"]
+
+    def spread_rows(at, height):
+        for r in range(GROUPS):
+            part = jnp.where(group == r, flat_ref[at : at + height // GROUPS, :], 0.0)
+            square_ref[pl.ds(r, height // GROUPS, stride=GROUPS), :] = fold_lanes(part)
+        return square_ref[:height, :]
+
+    def fast_weights():
+        lay_out(AT_F1, AT_LAT)
+        for k in range(3):
+            tap = flat_ref[pl.ds(AT_F1 + k, B_FAST, stride=3), :].astype(bf16)
+            for g in range(GROUPS):
+                f1_w[g * B_FAST : (g + 1) * B_FAST, k * BLK : (k + 1) * BLK] = tap
+        two = spread_rows(AT_F2, B_FAST)
         for g in range(GROUPS):
-            f1_ref[g * B_FAST : (g + 1) * B_FAST, k * BLK : (k + 1) * BLK] = tap
-    group = lane_group()
-
-    def spread(at, tall):
-        for r in range(GROUPS):
-            part = jnp.where(group == r, flat_ref[at : at + tall // GROUPS, :], 0.0)
-            square_ref[pl.ds(r, tall // GROUPS, stride=GROUPS), :] = fold_lanes(part)
-        return square_ref[:tall, :]
-
-    two = spread(AT_F2, B_FAST)
-    for g in range(GROUPS):
-        f2_ref[g * B_FAST : (g + 1) * B_FAST, :] = jnp.where(group == g, two, 0.0).astype(bf16)
-    f3_ref[...] = spread(AT_F3, C_FAST).astype(bf16)
+            f2_w[g * B_FAST : (g + 1) * B_FAST, :] = jnp.where(group == g, two, 0.0).astype(bf16)
+        f3_w[...] = spread_rows(AT_F3, C_FAST).astype(bf16)
+
+    matrix(lat_w, AT_LAT, C_LAT, 5)
+    lay_out(AT_VEC, NBLK)
     vec_ref[...] = flat_ref[AT_VEC : AT_VEC + 32, :]
 
-
-def call_weights(cfg, starts, gathered):
-    nd, nm, frames, slow_frames, share, slots = cfg
-    rows = up(slots + 15, 16)
-    smem = pl.BlockSpec(memory_space=pltpu.SMEM)
-    vmem = pl.BlockSpec(memory_space=pltpu.VMEM)
-    shapes = [
-        ((C_LAT, 5 * C_FAST), bf16),
-        ((B_SLOW, C_SLOW + C_LAT), bf16),
-        ((B_SLOW, 3 * B_SLOW), bf16),
-        ((C_SLOW, B_SLOW), bf16),
-        ((BLK, 3 * C_FAST), bf16),
-        ((BLK, BLK), bf16),
-        ((BLK, BLK), bf16),
-        ((32, BLK), f32),
-    ]
-    return pl.pallas_call(
-        functools.partial(weights_kernel, cfg),
-        out_shape=tuple(jax.ShapeDtypeStruct(s, t) for s, t in shapes),
-        in_specs=[smem, vmem],
-        out_specs=tuple(vmem for _ in shapes),
-        scratch_shapes=[
-            pltpu.VMEM((up(NBLK + rows, 64), BLK), f32),
-            pltpu.VMEM((BLK, BLK), f32),
-        ],
-        compiler_params=pltpu.CompilerParams(vmem_limit_bytes=48 << 20),
-        name="weights",
-    )(starts, gathered)
-
-
-EX_LAT, EX_S1, EX_S2, EX_B2, EX_B1, EX_BLAT = range(6)
-EX_F1, EX_F2, EX_F3, EX_BF3, EX_BF2, EX_BF1 = range(6, 12)
-EX_S3, EX_BS3 = 12, 13
-EXCHANGES = 14
-
-
-def main_kernel(
-    cfg, start_ref, crop_ref, xt_ref, xs_ref, lat_w, s1_w, s2_w, s3_w, f1_w, f2_w, f3_w, vec_ref,
-    fcot_ref, scot_ref,
-    fast_out, slow_out, fast_grad, slow_grad, grad_out,
-    mask_ref, fc_ref, sc_ref, natural_ref, zb, latb, s1b, s2b, dz, da1, da2, c1, c2, c3, e, e3,
-    a1p, a2p, h1p, h2p, d1p, d2p, ep, a3, e3f, square_ref, flat_ref, own3_ref, win_ref,
-    st_ref, st16_ref, f_recv, s_recv, gather_sems, ex_send, ex_recv, g_send, g_recv
-):
-    nd, nm, frames, slow_frames, share, slots = cfg
-    p = Place(nd, nm)
-    slow_rows, fast_rows = slow_frames * POS, frames * POS
-    per_group = frames // GROUPS
-    group_rows = per_group * POS
-    keep = share == BLK
-    da3, da3f = sc_ref, fc_ref
-
-    peers = [(lax.rem(p.dp + i, nd), p.mp) for i in range(1, nd)]
-    near = [p.dev(p.x, p.c, p.off_a(i), p.b) for i in range(1, p.na)]
-    near += [p.dev(p.x, p.c, p.a, p.off_b(i)) for i in range(1, p.nb)]
-    signal_all(peers + near)
-
-    crop = crop_ref[0]
-    mask_ref[...] = position_mask(crop)
-    tall = crop.astype(f32)
-    area = tall * tall
-
-    mask = mask_ref[...]
-
-    def frame_view(r):
-        return fc_ref.at[pl.ds(pl.multiple_of(r * POS, POS), POS)]
-
-    frame_view(p.mp)[...] = (fcot_ref[...].astype(f32).T * mask).astype(bf16)
-    if keep:
-
-        def slow_view(r):
-            return sc_ref.at[:, pl.ds(pl.multiple_of(r * BLK, BLK), BLK)]
-
-        for s in range(slow_frames):
-            piece = scot_ref[:, s * POS : (s + 1) * POS].astype(f32).T * mask
-            slow_view(p.mp)[s * POS : (s + 1) * POS, :] = piece.astype(bf16)
-    else:
-
-        def slow_view(r):
-            return natural_ref.at[pl.ds(pl.multiple_of(r * share, share), share)]
-
-        slow_view(p.mp)[...] = scot_ref[...]
-
-    pl.semaphore_wait(pltpu.get_barrier_semaphore(), len(peers) + len(near))
-    out = Sender(gather_sems)
-    slow_gather = Gather(p, slow_view, out, s_recv)
-    fast_gather = Gather(p, frame_view, out, f_recv)
-    fast_gather.start()
-    slow_gather.start()
+    x_gather.finish()
+    zb, latb, s1b, s2b, da1, da2 = (R[n] for n in ("zb", "latb", "s1b", "s2b", "da1", "da2"))
+    c1, c2, c3, e, e3 = (R[n] for n in ("c1", "c2", "c3", "e", "e3"))
+    a1p, a2p, h1p, h2p, d1p, d2p, ep, a3, e3f = (
+        R[n] for n in ("a1p", "a2p", "h1p", "h2p", "d1p", "d2p", "ep", "a3", "e3f")
+    )
+    mask_ref, own3_ref, win_ref, st_ref, st16_ref = (
+        R[n] for n in ("mask", "own3", "win", "st", "st16")
+    )
+    ex_send, ex_recv, g_send, g_recv = (R[n] for n in ("ex_send", "ex_recv", "g_send", "g_recv"))
+    da3, da3f, dz = sc_ref, fc_ref, s2b
 
     ex_copies = []
 
@@ -518,9 +642,10 @@
         buffer = stat(which)
         for i in range(1, nd):
             arrived(buffer.at[lax.rem(p.dp + nd - i, nd)], ex_recv.at[which, i - 1])
-        total = buffer[0]
+        ref, at = (st_ref, which) if which < 12 else (st16_ref, which - 12)
+        total = ref[at, 0]
         for i in range(1, nd):
-            total = total + buffer[i]
+            total = total + ref[at, i]
         return total
 
     def put(which, at, vector):
@@ -608,10 +733,28 @@
             at = AT_VEC + row + j
             flat_ref[at : at + 1, :] = vector[:, j * BLK : (j + 1) * BLK]
 
+    deliveries = []
+
+    def deliver(source, name):
+        copy = pltpu.make_async_copy(
+            source, R["out:" + name], R["local"].at[len(local_copies) + len(deliveries)]
+        )
+        copy.start()
+        deliveries.append(copy)
+
+    def put_frame(name, target, block):
+        for h in range(halves):
+            target[pl.ds(h, C_FAST, stride=halves), :] = block[h * BLK : (h + 1) * BLK, :].T
+        deliver(target, name)
+
+    def put_slow(target, s, block):
+        for h in range(halves):
+            target[pl.ds(s * halves + h, share, stride=slow_frames * halves), :] = to_channels(
+                block[h * BLK : (h + 1) * BLK, :]
+            )
+
     def frame(ref, s):
         return ref[s * POS : (s + 1) * POS, :]
-
-    group = lane_group()
 
     for s in range(slow_frames):
         window = jnp.concatenate([frame(xt_ref, 4 * s + k) for k in range(5)], 1)
@@ -621,6 +764,8 @@
     put(EX_LAT, 2, two)
     st_ref[EX_LAT, p.dp, 4:8, :] = jnp.full((4, BLK), area, f32)
     exchange(EX_LAT)
+
+    fast_weights()
 
     def first(j, _):
         total = jnp.zeros((POS, BLK), f32)
@@ -639,6 +784,11 @@
     put(EX_F1, 1, fold_lanes(two))
     st_ref[EX_F1, p.dp, 2:8, :] = jnp.full((6, BLK), area, f32)
     exchange(EX_F1)
+
+    matrix(s1_w, AT_S1, B_SLOW, 10)
+    xs_gather.finish()
+    if not keep:
+        from_natural(R["out:natural_x"], xs_ref)
 
     for s in range(slow_frames):
         c1[s * POS : (s + 1) * POS, :] = dot_nt(frame(xs_ref, s), s1_w[:, :C_SLOW])
@@ -659,6 +809,8 @@
     st_ref[EX_S1, p.dp, 4:8, :] = jnp.zeros((4, BLK), f32)
     exchange(EX_S1)
 
+    matrix(s2_w, AT_S2, B_SLOW, 6)
+
     packed = vec_ref[0:1, :]
 
     def spread(which):
@@ -677,7 +829,7 @@
     put(EX_F2, 1, fold_lanes(two))
     st_ref[EX_F2, p.dp, 2:8, :] = jnp.zeros((6, BLK), f32)
     exchange(EX_F2)
-    fast_gather.relay()
+    fc_gather.relay()
 
     total = exchanged(EX_S1)
     s1_norm = affine(row_of(total, 0, 2), row_of(total, 2, 2), slow_count, *vectors(V_S1))
@@ -692,6 +844,8 @@
     st_ref[EX_S2, p.dp, 4:8, :] = jnp.zeros((4, BLK), f32)
     exchange(EX_S2)
 
+    matrix(s3_w, AT_S3, C_SLOW, 2)
+
     f2_norm = affine(*exchanged_two(EX_F2), fast_count, spread(2), spread(3))
     activate(a2p, h2p, group_rows, BLK, f2_norm[2], f2_norm[3])
     for g in range(GROUPS):
@@ -707,7 +861,7 @@
     put(EX_F3, 1, two)
     st_ref[EX_F3, p.dp, 2:8, :] = jnp.zeros((6, BLK), f32)
     exchange(EX_F3)
-    slow_gather.relay()
+    sc_gather.relay()
 
     total = exchanged(EX_S2)
     s2_norm = affine(row_of(total, 0, 2), row_of(total, 2, 2), slow_count, *vectors(V_S2))
@@ -723,10 +877,10 @@
     exchange(EX_S3)
 
     f3_norm = affine(*exchanged_two(EX_F3), fast_count, *vectors(V_F3))
-    fast_gather.finish()
+    fc_gather.finish()
     own = a3[rows_at(p.mp, POS), :] * f3_norm[2] + f3_norm[3]
     own = own + xt_ref[rows_at(p.mp + 2, POS), :].astype(f32)
-    fast_out[...] = (gelu(own) * mask_ref[...]).T
+    put_frame("fast_out", R["out_fast"], gelu(own) * mask_ref[...])
 
     def fast_slopes(i, acc):
         mean, scale, grow, base = f3_norm
@@ -747,10 +901,10 @@
     put_vector(V_F3[0], two)
     put_vector(V_F3[1], one)
 
-    slow_gather.finish()
+    sc_gather.finish()
     out.drain()
     if not keep:
-        from_natural(natural_ref, sc_ref, mask_ref[...], slow_frames)
+        from_natural(R["out:natural_c"], sc_ref)
     total = exchanged(EX_S3)
     s3_norm = affine(row_of(total, 0, 8), row_of(total, 8, 8), slow_count8, *vectors(V_S3))
 
@@ -803,8 +957,9 @@
     for s in range(slow_frames):
         at = slice(s * POS, (s + 1) * POS)
         pre = c3[at, at_lane] * own_norm[2] + own_norm[3] + xs_ref[at, at_lane].astype(f32)
-        slow_out[:, at] = to_channels(gelu(pre) * mask_ref[...])
+        put_slow(R["out_slow"], s, gelu(pre) * mask_ref[...])
         own3_ref[at, :] = gelu_slope(pre) * sc_ref[at, at_lane].astype(f32)
+    deliver(R["out_slow"], "slow_out")
 
     q0, q1 = back_vectors(*exchanged_two(EX_BF3), fast_count, f3_norm)
     raw_grads(a3, e3f, da3f, fast_rows, BLK, f3_norm, q0, q1)
@@ -938,7 +1093,8 @@
     for s in range(slow_frames):
         at = slice(s * POS, (s + 1) * POS)
         value = own3_ref[at, :] + dot_nn(da1[at, :], s1_w[:, at_lane])
-        slow_grad[:, at] = to_channels(value * mask_ref[...])
+        put_slow(R["out_sgrad"], s, value * mask_ref[...])
+    deliver(R["out_sgrad"], "slow_grad")
 
     q0, q1 = back_vectors(*exchanged_two(EX_BF1), fast_count, f1_norm)
     raw_grads(a1p, ep, d1p, group_rows, BLK, f1_norm, q0, q1)
@@ -981,8 +1137,14 @@
     height = up(slots, 16)
     g_copies = []
 
+    def start_of(device):
+        def one(k, found):
+            return jnp.where(run_device[k] == device, run_start[k], found)
+
+        return lax.fori_loop(0, devices, one, jnp.int32(0))
+
     def window_of(device):
-        return flat_ref[pl.ds(start_ref[device], height), :]
+        return flat_ref[pl.ds(start_of(device), height), :]
 
     for i in range(1, nd):
         peer = lax.rem(p.dp + i, nd)
@@ -1008,86 +1170,64 @@
         left = jnp.where(there, dz[rows_at(at, POS), :], 0.0).astype(bf16)
         weight = lat_w[:, pl.ds(pl.multiple_of(tap * BLK, BLK), BLK)]
         near_grad = near_grad + dot_nn(left, weight)
-    fast_grad[...] = (near_grad * mask_ref[...]).T
-
-    total = window_of(p.dp * nm + p.mp)
+    put_frame("fast_grad", R["out_fgrad"], near_grad * mask_ref[...])
+
+    total = window_of(me)
     for i in range(1, nd):
         arrived(win_ref.at[1, i - 1], g_recv.at[i - 1])
         total = total + win_ref[1, i - 1].astype(f32)
-    grad_out[...] = total
+    R["out_grad"][...] = total
+    deliver(R["out_grad"], "grad")
     for copy in ex_copies + g_copies:
         copy.wait_send()
-
-
-def call_main(cfg, starts, crop, xt, xs, weights, fcot, scot):
-    nd, nm, frames, slow_frames, share, slots = cfg
-    height = up(slots, 16)
-    slow_rows, fast_rows = slow_frames * POS, frames * POS
-    group_rows = fast_rows // GROUPS
-    keep = share == BLK
+    for copy in deliveries:
+        copy.wait()
+
+
+def call_main(cfg, crop, owner, padded, master, fast, slow, fcot, scot):
     smem = pl.BlockSpec(memory_space=pltpu.SMEM)
-    vmem = pl.BlockSpec(memory_space=pltpu.VMEM)
-    dma = pltpu.SemaphoreType.DMA
-    out_shapes = (
-        (C_FAST, POS), (share, slow_rows), (C_FAST, POS), (share, slow_rows), (height, BLK)
-    )
-    scratch = [
-        ((POS, BLK), f32),
-        ((fast_rows, BLK), bf16),
-        ((slow_rows, C_SLOW), bf16),
-        ((16, BLK) if keep else (C_SLOW, slow_rows), bf16),
-    ]
-    scratch += [((slow_rows, 256), bf16)] * 7
-    scratch += [
-        ((slow_rows, 256), f32),
-        ((slow_rows, 256), f32),
-        ((slow_rows, C_SLOW), f32),
-        ((slow_rows, 256), f32),
-        ((slow_rows, C_SLOW) if keep else (8, BLK), f32),
-        ((group_rows, BLK), f32),
-        ((group_rows, BLK), f32),
-        ((group_rows, BLK), bf16),
-        ((group_rows, BLK), bf16),
-        ((group_rows, BLK), bf16),
-        ((group_rows, BLK), bf16),
-        ((group_rows, BLK), f32),
-        ((fast_rows, BLK), f32),
-        ((fast_rows, BLK), f32),
-        ((BLK, BLK), f32),
-        ((up(NBLK + height, 64), BLK), f32),
-        ((slow_rows, BLK), f32),
-        ((2, nd - 1, height, BLK), bf16),
-        ((12, nd, 8, BLK), f32),
-        ((2, nd, 16, BLK), f32),
-    ]
+    hbm = pl.BlockSpec(memory_space=pltpu.HBM)
+    outs = outputs(cfg)
     return pl.pallas_call(
         functools.partial(main_kernel, cfg),
-        out_shape=tuple(jax.ShapeDtypeStruct(s, f32) for s in out_shapes),
-        in_specs=[smem, smem] + [vmem] * 12,
-        out_specs=tuple(vmem for _ in out_shapes),
-        scratch_shapes=[pltpu.VMEM(s, t) for s, t in scratch]
-        + [
-            dma((nm,)),
-            dma((nm,)),
-            dma((2 * (nm - 1),)),
-            dma((EXCHANGES, nd - 1)),
-            dma((EXCHANGES, nd - 1)),
-            dma((nd - 1,)),
-            dma((nd - 1,)),
-        ],
+        out_shape=tuple(jax.ShapeDtypeStruct(s, t) for _, s, t in outs),
+        in_specs=[smem] + [hbm] * 7,
+        out_specs=tuple(hbm for _ in outs),
+        scratch_shapes=[s for _, s in scratch(cfg)],
         compiler_params=pltpu.CompilerParams(
-            collective_id=1, has_side_effects=True, vmem_limit_bytes=60 << 20
+            collective_id=0, has_side_effects=True, vmem_limit_bytes=62 << 20
         ),
         name="block",
-    )(starts, crop, xt, xs, *weights, fcot, scot)
-
-
-def adam_kernel(cfg, start_ref, count_ref, grad, master, one, two, w_out, one_out, two_out, low_out):
+    )(crop, owner, padded, master, fast, slow, fcot, scot)[:5]
+
+
+def adam_kernel(
+    cfg, owner_ref, grad, master, one, two, a_in, b_in, c_in, d_in,
+    w_out, one_out, two_out, low_out, a_out, b_out, c_out, d_out, sems
+):
     nd, nm, frames, slow_frames, share, slots = cfg
+    copies = [
+        pltpu.make_async_copy(source, target, sems.at[i])
+        for i, (source, target) in enumerate(
+            ((a_in, a_out), (b_in, b_out), (c_in, c_out), (d_in, d_out))
+        )
+    ]
+    for copy in copies:
+        copy.start()
     me = lax.axis_index("dp") * nm + lax.axis_index("mp")
+    spot = lax.broadcasted_iota(jnp.int32, (8, BLK), 0) * BLK
+    spot = spot + lax.broadcasted_iota(jnp.int32, (8, BLK), 1)
+    lowest = jnp.full((8, BLK), NBLK, jnp.int32)
+    number = jnp.zeros((8, BLK), jnp.int32)
+    for i in range(up(NBLK, 1024) // 1024):
+        block = spot + i * 1024
+        mine = (owner_ref[i * 8 : (i + 1) * 8, :] == me) & (block < NBLK)
+        lowest = jnp.minimum(lowest, jnp.where(mine, block, NBLK))
+        number = number + jnp.where(mine, 1, 0)
+    start, count = jnp.min(lowest), jnp.sum(number)
     row = lax.broadcasted_iota(jnp.int32, (slots, BLK), 0)
-    living = row < count_ref[me]
-    block = row + start_ref[me]
+    living = row < count
+    block = row + start
     rate = jnp.full((slots, BLK), 0.2, f32)
     for at, width in (
         (AT_VEC, B_SLOW),
@@ -1111,48 +1251,56 @@
     one_out[...] = jnp.where(living, first, 0.0)
     two_out[...] = jnp.where(living, second, 0.0)
     low_out[...] = weight.astype(bf16)
-
-
-def call_adam(cfg, starts, counts, grad, master, one, two):
+    for copy in copies:
+        copy.wait()
+
+
+def call_adam(cfg, owner, grad, master, one, two, passed):
     shape = master.shape
-    smem = pl.BlockSpec(memory_space=pltpu.SMEM)
     vmem = pl.BlockSpec(memory_space=pltpu.VMEM)
+    hbm = pl.BlockSpec(memory_space=pltpu.HBM)
     return pl.pallas_call(
         functools.partial(adam_kernel, cfg),
-        out_shape=tuple(jax.ShapeDtypeStruct(shape, t) for t in (f32, f32, f32, bf16)),
-        in_specs=[smem, smem] + [vmem] * 4,
-        out_specs=(vmem,) * 4,
+        out_shape=tuple(jax.ShapeDtypeStruct(shape, t) for t in (f32, f32, f32, bf16))
+        + tuple(jax.ShapeDtypeStruct(a.shape, a.dtype) for a in passed),
+        in_specs=[vmem] * 5 + [hbm] * 4,
+        out_specs=(vmem,) * 4 + (hbm,) * 4,
+        scratch_shapes=[pltpu.SemaphoreType.DMA((4,))],
         compiler_params=pltpu.CompilerParams(vmem_limit_bytes=32 << 20),
         name="adam",
-    )(starts, counts, grad, master, one, two)
+    )(owner, grad, master, one, two, *passed)
 
 
 def solution(mesh):
     nd, nm = mesh.shape["dp"], mesh.shape["mp"]
 
     def local(fast_in, slow_in, fast_cot, slow_cot, crop, owner, master, one, two):
-        cfg = (nd, nm, fast_in.shape[1] * nm, slow_in.shape[1], slow_in.shape[0], master.shape[0])
-        devices = jnp.arange(nd * nm, dtype=jnp.int32)[:, None]
-        mine = owner[None, :] == devices
-        spot = jnp.arange(NBLK, dtype=jnp.int32)[None, :]
-        starts = jnp.min(jnp.where(mine, spot, NBLK), 1)
-        counts = jnp.sum(mine.astype(jnp.int32), 1)
-        fast = fast_in.reshape(C_FAST, -1)
-        slow = slow_in.reshape(slow_in.shape[0], -1)
-        fcot = fast_cot.reshape(C_FAST, -1)
-        scot = slow_cot.reshape(slow_in.shape[0], -1)
-        gathered, xt, xs = call_gather(cfg, starts, counts, crop, master, fast, slow)
-        weights = call_weights(cfg, starts, gathered)
-        fast_out, slow_out, fast_grad, slow_grad, grad = call_main(
-            cfg, starts, crop, xt, xs, weights, fcot, scot
+        share, slow_frames = slow_in.shape[0], slow_in.shape[1]
+        cfg = (nd, nm, fast_in.shape[1] * nm, slow_frames, share, master.shape[0])
+
+        def halves(array):
+            split = array.reshape(share, slow_frames, POS // BLK, BLK)
+            return split.transpose(0, 2, 1, 3).reshape(-1, BLK)
+
+        padded = jnp.pad(owner, (0, up(NBLK, 1024) - NBLK)).reshape(-1, BLK)
+        *passed, grad = call_main(
+            cfg,
+            crop,
+            owner,
+            padded,
+            master,
+            fast_in.reshape(C_FAST, POS),
+            halves(slow_in),
+            fast_cot.reshape(C_FAST, POS),
+            halves(slow_cot),
         )
-        new = call_adam(cfg, starts, counts, grad, master, one, two)
+        new = call_adam(cfg, padded, grad, master, one, two, passed)
         return (
-            fast_out.reshape(fast_in.shape),
-            slow_out.reshape(slow_in.shape),
-            fast_grad.reshape(fast_in.shape),
-            slow_grad.reshape(slow_in.shape),
-            *new,
+            new[4].reshape(fast_in.shape),
+            new[5].reshape(slow_in.shape),
+            new[6].reshape(fast_in.shape),
+            new[7].reshape(slow_in.shape),
+            *new[:4],
         )
 
     return jax.shard_map(

time: 130 us -> 104 us (0.80); the launches traced: 129 us -> 104 us
  local copies, waits for them, and re-layouts: 21.9 us -> 6.08 us
  Pallas kernels: 104 us -> 96.6 us
    pallas_call x2 -> x0, Pallas kernels: 44.4 us -> none  [the longest x1 41.8 us: call_gather(): pl.pallas_call(functools.partial(gather_kernel, cfg), out_shape=(jax.Shap...]
    pallas_call x1, Pallas kernels: 58.1 us -> 94.8 us  [call_main(): pl.pallas_call(functools.partial(main_kernel, cfg), out_shape=tuple((jax....]
    unnamed x44 -> x18, local copies, waits for them, and re-layouts: 18 us -> 4.66 us
    reshape x2 -> x1, local copies, waits for them, and re-layouts: 3.91 us -> 1.42 us  [local(): padded = jnp.pad(owner, (0, up(NBLK, 1024) - NBLK)).reshape(-1, BLK)]
where the time goes in v2:
time: 104 us
  Pallas kernels  96.6 us (93%)
  local copies, waits for them, and re-layouts  6.08 us (6%)
  between operations  1.34 us (1%)
    pallas_call x1, Pallas kernels, call_main(): pl.pallas_call(functools.partial(main_kernel, cfg), out_shape=tuple((jax....  94.8 us
    unnamed x18, local copies, waits for them, and re-layouts  4.66 us

profile of v2, /device:TPU:25, one launch (start us, length us, event | category | flops | bytes accessed | tf_op | source)
XLA Modules:
  0.0 104.0 jit_solution(14986759853361963530)
XLA Ops:
  1.3 0.0 copy-start.5
  1.3 1.4 %pad_bitcast_fusion.refs_2_.owner_ref = s32[64,128]{1,0:T(8,128)} fusion(s32[7591]{0:T(1024)} %refs_1_.1), kind=kLoop, calls=%fused_computation | loop fusion | bytes 63132 | tf_op jit(solution)/shard_map/reshape | solution.py:1285
  2.7 0.0 copy-start
  2.7 0.0 copy-start.1
  2.7 0.0 copy-start.4
  2.7 94.8 %block.1 = (f32[256,128]{1,0:T(8,128)}, f32[512,128]{1,0:T(8,128)}, f32[256,128]{1,0:T(8,128)}, f32[512,128]{1,0:T(8,128)}, f32[480,128]{1,0:T(8,128)}) custom-call(s32[1]{0:T(128)S(6)} %copy.23.refs_0_, s32[7591]{0:T(1024)} %refs_1_.1, s32[64,128]{1,0:T(8,128)} %pad_bitcast_fusion.refs_2_.owner_ref, f32[476,128]{1,0:T(8,128)} %master.1, ...), custom_call_target="tpu_custom_call" | custom-call | tf_op jit(solution)/shard_map/block/pallas_call | solution.py:1191
  97.5 0.0 copy-done.5
  97.5 0.0 copy-done
  97.5 0.0 copy-done.1
  97.6 0.0 copy-done.4
  97.6 0.0 copy-start.2
  97.6 0.9 copy-done.2
  98.5 0.0 copy-start.3
  98.5 0.9 copy-done.3
  99.5 0.0 copy-start.6
  99.5 0.9 copy-done.6
  100.4 0.0 copy-start.7
  100.4 0.9 copy-done.7
  101.3 0.0 copy-start.8
  101.3 0.9 copy-done.8
  102.2 1.8 %adam.1 = (f32[476,128]{1,0:T(8,128)}, f32[476,128]{1,0:T(8,128)}, f32[476,128]{1,0:T(8,128)}, bf16[476,128]{1,0:T(8,128)(2,1)}, f32[256,128]{1,0:T(8,128)}, /*i...) custom-call(s32[64,128]{1,0:T(8,128)S(1)} %copy-done.1, f32[480,128]{1,0:T(8,128)S(1)} %copy-done.6, ...), custom_call_target="tpu_custom_call" | custom-call | tf_op jit(solution)/shard_map/adam/pallas_call | solution.py:1262
Async XLA Ops:
  1.3 96.2 %copy-start.5 = (f32[476,128]{1,0:T(8,128)S(1)}, f32[476,128]{1,0:T(8,128)}, u32[]{:S(2)}) copy-start(f32[476,128]{1,0:T(8,128)} %two.1) | copy-start | bytes 731140
  2.7 94.8 %copy-start = (f32[476,128]{1,0:T(8,128)S(1)}, f32[476,128]{1,0:T(8,128)}, u32[]{:S(2)}) copy-start(f32[476,128]{1,0:T(8,128)} %master.1) | copy-start | bytes 731140
  2.7 94.8 %copy-start.1 = (s32[64,128]{1,0:T(8,128)S(1)}, s32[64,128]{1,0:T(8,128)}, u32[]{:S(2)}) copy-start(s32[64,128]{1,0:T(8,128)} %pad_bitcast_fusion.refs_2_.owner_ref) | copy-start | bytes 98308
  2.7 94.8 %copy-start.4 = (f32[476,128]{1,0:T(8,128)S(1)}, f32[476,128]{1,0:T(8,128)}, u32[]{:S(2)}) copy-start(f32[476,128]{1,0:T(8,128)} %one.1) | copy-start | bytes 731140
  97.6 1.0 copy-start.2
  98.5 0.9 copy-start.3
  99.5 0.9 copy-start.6
  100.4 0.9 copy-start.7
  101.3 0.9 copy-start.8

commit v3 on v2

v3 whole, which is shorter than its diff:
```python
import functools
import math
import types

import jax
import jax.numpy as jnp
from jax import lax
from jax.experimental import pallas as pl
from jax.experimental.pallas import tpu as pltpu
from jax.sharding import PartitionSpec as P

C_FAST = 128
B_FAST = 32
C_SLOW = 1024
B_SLOW = 256
C_LAT = 256
TILE = 16
POS = TILE * TILE
BLK = 128
STEP = 10
NBLK = 7591

norm_eps = 1e-05
beta_first = 0.5
beta_second = 0.5
adam_eps = 1e-08
decay_rate = 0.05

MESH = pl.DeviceIdType.MESH
f32 = jnp.float32
bf16 = jnp.bfloat16
RC = 32
CH = 256
GROUPS = BLK // B_FAST
COLUMNS = 2
HALF = POS // COLUMNS
SLABS = C_SLOW // BLK

AT_F1 = 0
AT_F2 = AT_F1 + B_FAST * 3 * C_FAST // BLK
AT_F3 = AT_F2 + B_FAST * B_FAST // BLK
AT_LAT = AT_F3 + C_FAST * B_FAST // BLK
AT_S1 = AT_LAT + C_LAT * 5 * C_FAST // BLK
AT_S2 = AT_S1 + B_SLOW * (C_SLOW + C_LAT) // BLK
AT_S3 = AT_S2 + B_SLOW * 3 * B_SLOW // BLK
AT_VEC = AT_S3 + C_SLOW * B_SLOW // BLK
V_F3 = (1, 2, 1)
V_LAT = (3, 5, 2)
V_S1 = (7, 9, 2)
V_S2 = (11, 13, 2)
V_S3 = (15, 23, 8)


def up(n, m):
    return (n + m - 1) // m * m


def dot_nt(a, b):
    return lax.dot_general(a, b, (((1,), (1,)), ((), ())), preferred_element_type=f32)


def dot_tn(a, b):
    return lax.dot_general(a, b, (((0,), (0,)), ((), ())), preferred_element_type=f32)


def dot_nn(a, b):
    return lax.dot_general(a, b, (((1,), (0,)), ((), ())), preferred_element_type=f32)


G0 = math.sqrt(2.0 / math.pi)
G1 = 0.044715


def gelu(x):
    t = jnp.tanh(x * (G0 + (G0 * G1) * (x * x)))
    return 0.5 * x * (1.0 + t)


def gelu_slope(x):
    xx = x * x
    t = jnp.tanh(x * (G0 + (G0 * G1) * xx))
    return 0.5 * (1.0 + t) + (0.5 * x) * (1.0 - t * t) * (G0 + (3.0 * G0 * G1) * xx)


def position_mask(crop):
    spot = lax.broadcasted_iota(jnp.int32, (POS, BLK), 0)
    inside = (spot // TILE < crop) & (lax.rem(spot, TILE) < crop)
    return jnp.where(inside, 1.0, 0.0).astype(f32)


def lane_group():
    return lax.broadcasted_iota(jnp.int32, (1, BLK), 1) // B_FAST


def fold_lanes(v):
    v = v + pltpu.roll(v, B_FAST, 1)
    return v + pltpu.roll(v, 2 * B_FAST, 1)


def remote(source, target, send_sem, recv_sem, device):
    pltpu.make_async_remote_copy(
        src_ref=source,
        dst_ref=target,
        send_sem=send_sem,
        recv_sem=recv_sem,
        device_id=device,
        device_id_type=MESH,
    ).start()


def arrived(view, sem):
    pltpu.make_async_copy(view, view, sem).wait()


class Place:
    def __init__(self, nd, nm):
        self.nd, self.nm = nd, nm
        self.nx = nd // 2
        self.nb = COLUMNS
        self.na = nm // self.nb
        self.dp = lax.axis_index("dp")
        self.mp = lax.axis_index("mp")
        self.x, self.c = self.dp // 2, lax.rem(self.dp, 2)
        self.a, self.b = self.mp // self.nb, lax.rem(self.mp, self.nb)

    def off_a(self, i):
        return lax.rem(self.a + i, self.na)

    def off_b(self, i):
        return lax.rem(self.b + i, self.nb)

    def off_x(self, i):
        return lax.rem(self.x + i, self.nx)

    def dev(self, x, c, a, b):
        return (x * 2 + c, a * self.nb + b)

    def slot(self, x, c, a, b):
        return (x * 2 + c) * self.nm + a * self.nb + b


class Gather:
    def __init__(self, place, slabs, other, skip, send, near, far):
        self.p, self.slabs, self.other, self.skip = place, slabs, other, skip
        self.sems = send, near, far

    def view(self, rank):
        return self.slabs.at[rank + self.skip]

    def along(self, rank):
        p, (send, near, far) = self.p, self.sems
        for i in range(1, p.na):
            device = (p.dp, p.off_a(i) * p.nb + p.b)
            remote(self.view(rank), self.view(rank), send, far, device)

    def start(self):
        p, (send, near, far) = self.p, self.sems
        remote(self.other, self.view(p.mp), send, near, (p.dp, p.a * p.nb + p.off_b(1)))
        self.along(p.mp)

    def relay(self):
        p, (send, near, far) = self.p, self.sems
        rank = p.a * p.nb + p.off_b(1)
        arrived(self.view(rank), near)
        self.along(rank)

    def finish(self):
        arrived(self.slabs.at[pl.ds(0, (self.p.na - 1) * self.p.nb)], self.sems[2])

    def drain(self):
        arrived(self.slabs.at[pl.ds(0, self.p.nm - 1)], self.sems[0])


EX_LAT, EX_S1, EX_S2, EX_B2, EX_B1, EX_BLAT = range(6)
EX_F1, EX_F2, EX_F3, EX_BF3, EX_BF2, EX_BF1 = range(6, 12)
EX_S3, EX_BS3 = 12, 13
EXCHANGES = 14

FAST_OUT, SLOW_OUT, FAST_GRAD, SLOW_GRAD = range(4)
SENT, MINE, GOT = range(3)


def outputs(cfg):
    nd, nm, frames, slow_frames, share, slots = cfg
    halves = POS // BLK
    fast, slow = (C_FAST * halves, BLK), (share * slow_frames * halves, BLK)
    result = [(fast, f32), (slow, f32), (fast, f32), (slow, f32), ((up(slots, 16), BLK), f32)]
    if share != BLK:
        result += [((nm, share, slow_frames * HALF), bf16)] * 2
    return result


def scratch(cfg):
    nd, nm, frames, slow_frames, share, slots = cfg
    devices, group = nd * nm, nd * COLUMNS
    rows = up(slots + 15, 16)
    height = up(slots, 16)
    halves = POS // BLK
    slow_rows, fast_rows = slow_frames * HALF, frames * HALF
    group_rows = fast_rows // GROUPS
    windows = group // 2
    vmem, smem, dma = pltpu.VMEM, pltpu.SMEM, pltpu.SemaphoreType.DMA
    piece = (slow_rows, BLK) if share == BLK else (share, slow_rows)
    result = dict(
        owner_v=vmem((up(NBLK, 1024) // BLK, BLK), jnp.int32),
        owner_s=smem((NBLK,), jnp.int32),
        run_device=smem((devices,), jnp.int32),
        run_start=smem((devices,), jnp.int32),
        run_count=smem((devices,), jnp.int32),
        table_v=vmem((8, BLK), jnp.int32),
        table_s=smem((8, BLK), jnp.int32),
        shift=vmem((rows + 16, BLK), f32),
        p=vmem((devices * (rows // 16), 16, BLK), bf16),
        q=vmem((devices, 16, BLK), bf16),
        fast_v=vmem((C_FAST, POS), bf16),
        slow_v=vmem((share * slow_frames * halves, BLK), bf16),
        fcot_v=vmem((C_FAST, POS), bf16),
        scot_v=vmem((share * slow_frames * halves, BLK), bf16),
        stage=vmem((share * slow_frames * halves, BLK), f32),
        turned=vmem((POS, BLK), f32),
        x_other=vmem((HALF, BLK), bf16),
        fc_other=vmem((HALF, BLK), bf16),
        xs_other=vmem(piece, bf16),
        sc_other=vmem(piece, bf16),
        xt=vmem((frames + 4, HALF, BLK), bf16),
        xs=vmem((SLABS, slow_rows, BLK), bf16),
        fc=vmem((frames, HALF, BLK), bf16),
        sc=vmem((SLABS, slow_rows, BLK), bf16),
        wide=vmem((slow_rows, 5 * C_FAST), bf16),
        lat_w=vmem((C_LAT, 5 * C_FAST), bf16),
        s1_w=vmem((B_SLOW, C_SLOW + C_LAT), bf16),
        s2_w=vmem((B_SLOW, 3 * B_SLOW), bf16),
        s3_w=vmem((C_SLOW, B_SLOW), bf16),
        f1_w=vmem((BLK, 3 * C_FAST), bf16),
        f2_w=vmem((BLK, BLK), bf16),
        f3_w=vmem((BLK, BLK), bf16),
        vec=vmem((32, BLK), f32),
        mask_all=vmem((POS, BLK), f32),
        mask=vmem((HALF, BLK), f32),
    )
    if share != BLK:
        result.update(
            piece=vmem(piece, bf16),
            turn=vmem((BLK, HALF), bf16),
        )
    result.update(
        zb=vmem((slow_rows, 256), bf16),
        latb=vmem((slow_rows, 256), bf16),
        s2b=vmem((slow_rows, 256), bf16),
        dz=vmem((slow_rows, 256), bf16),
        da1=vmem((slow_rows, 256), bf16),
    )
    result.update(
        two_in=vmem(((slow_frames + 2) * HALF, 256), bf16),
        two_back=vmem(((slow_frames + 2) * HALF, 256), bf16),
        c1=vmem((slow_rows, 256), f32),
        c2=vmem((slow_rows, 256), f32),
        c3=vmem((slow_rows, C_SLOW), f32),
        e=vmem((slow_rows, 256), f32),
        e3=vmem((slow_rows, C_SLOW), f32),
        da3=vmem((slow_rows, C_SLOW), bf16),
        a1p=vmem((group_rows, BLK), f32),
        a2p=vmem((group_rows, BLK), f32),
        h1p=vmem((group_rows, BLK), bf16),
        h2p=vmem((group_rows, BLK), bf16),
        d1p=vmem((group_rows, BLK), bf16),
        d2p=vmem((group_rows, BLK), bf16),
        ep=vmem((group_rows, BLK), f32),
        a3=vmem((fast_rows, BLK), f32),
        e3f=vmem((fast_rows, BLK), f32),
        da3f=vmem((fast_rows, BLK), bf16),
        square=vmem((BLK, BLK), f32),
        flat=vmem((up(NBLK + height, 64), BLK), f32),
        own3=vmem((COLUMNS, slow_rows, BLK), f32),
        sib_out=vmem((windows, height, BLK), bf16),
        sib_in=vmem((windows, height, BLK), bf16),
        far_out=vmem((windows, height, BLK), bf16),
        far_in=vmem((windows, height, BLK), bf16),
        st=vmem((12, group, 8, BLK), f32),
        st16=vmem((2, group, 16, BLK), f32),
    )
    result.update(
        fast_out_box=vmem((3, HALF, BLK), f32),
        slow_out_box=vmem((3, slow_rows, BLK), f32),
        fast_grad_box=vmem((3, HALF, BLK), f32),
        slow_grad_box=vmem((3, slow_rows, BLK), f32),
        fast_out_end=vmem((C_FAST * halves, BLK), f32),
        slow_out_end=vmem((share * slow_frames * halves, BLK), f32),
        fast_grad_end=vmem((C_FAST * halves, BLK), f32),
        slow_grad_end=vmem((share * slow_frames * halves, BLK), f32),
        end_grad=vmem((height, BLK), f32),
        p_send=dma(()),
        p_recv=dma((devices,)),
        gather_sems=dma((4, 3)),
        ex_send=dma((EXCHANGES,)),
        ex_recv=dma((EXCHANGES,)),
        box_send=dma((4,)),
        box_recv=dma((4,)),
        sum_sems=dma((4,)),
        local=dma((16,)),
    )
    return result


def main_kernel(cfg, *refs):
    nd, nm, frames, slow_frames, share, slots = cfg
    n_out = len(outputs(cfg))
    args, results, held = refs[:8], refs[8 : 8 + n_out], refs[8 + n_out :]
    crop_in, owner_in, owners_in, master_in, fast_in, slow_in, fcot_in, scot_in = args
    R = types.SimpleNamespace(**dict(zip(scratch(cfg), held, strict=True)))
    p = Place(nd, nm)
    devices = nd * nm
    halves = POS // BLK
    rows = up(slots + 15, 16)
    tiles = rows // 16
    slow_rows, fast_rows = slow_frames * HALF, frames * HALF
    per_group = frames // GROUPS
    group_rows = per_group * HALF
    slabs = share == BLK
    me = p.dp * nm + p.mp
    partner = p.a * p.nb + p.off_b(1)

    members = nd * p.nb
    member = p.dp * p.nb + p.b
    group_peers = [
        (lax.rem(p.dp + i, nd), p.a * p.nb + p.off_b(k))
        for i in range(nd)
        for k in range(p.nb)
        if i or k
    ]
    near = [p.dev(p.x, p.c, p.off_a(i), p.b) for i in range(1, p.na)]
    barrier = pltpu.get_barrier_semaphore()
    for device in group_peers + near:
        pl.semaphore_signal(barrier, inc=1, device_id=device, device_id_type=MESH)

    local_copies = []

    def fetch(source, target):
        copy = pltpu.make_async_copy(source, target, R.local.at[len(local_copies)])
        copy.start()
        local_copies.append(copy)
        return copy

    get_owner = fetch(owners_in, R.owner_v)
    get_master = fetch(master_in, R.shift.at[pl.ds(16, slots)])
    get_fast = fetch(fast_in, R.fast_v)
    get_slow = fetch(slow_in, R.slow_v)
    get_owner_s = fetch(owner_in, R.owner_s)
    get_fcot = fetch(fcot_in, R.fcot_v)
    get_scot = fetch(scot_in, R.scot_v)

    crop = crop_in[0]
    R.mask_all[...] = position_mask(crop)
    R.mask[...] = R.mask_all[pl.ds(pl.multiple_of(p.b * HALF, HALF), HALF), :]
    tall = crop.astype(f32)
    area = tall * tall * (1.0 / COLUMNS)
    xt_ref, xs_ref, fc_ref, sc_ref = R.xt, R.xs, R.fc, R.sc
    for f in (0, 1, frames + 2, frames + 3):
        xt_ref[f] = jnp.zeros((HALF, BLK), bf16)
    two_in, two_back = R.two_in, R.two_back
    for ref in (two_in, two_back):
        ref[:HALF] = jnp.zeros((HALF, 256), bf16)
        ref[(slow_frames + 1) * HALF :] = jnp.zeros((HALF, 256), bf16)

    get_owner.wait()
    spot = lax.broadcasted_iota(jnp.int32, (8, BLK), 0) * BLK
    spot = spot + lax.broadcasted_iota(jnp.int32, (8, BLK), 1)
    lowest = jnp.full((8, BLK), NBLK, jnp.int32)
    number = jnp.zeros((8, BLK), jnp.int32)
    for i in range(up(NBLK, 1024) // 1024):
        block = spot + i * 1024
        mine = R.owner_v[i * 8 : (i + 1) * 8, :] == me
        mine = mine & (block < NBLK)
        lowest = jnp.minimum(lowest, jnp.where(mine, block, NBLK))
        number = number + jnp.where(mine, 1, 0)
    my_start, my_count = jnp.min(lowest), jnp.sum(number)
    shift = lax.rem(my_start, 16)
    get_master.wait()
    moved = R.shift[pl.ds(16 - shift, rows), :]
    row = lax.broadcasted_iota(jnp.int32, (rows, BLK), 0)
    own = (row >= shift) & (row < shift + my_count)
    p_ref = R.p

    def p_slot(slot):
        return p_ref.at[pl.ds(slot * tiles, tiles)]

    p_slot(me)[...] = jnp.where(own, moved, 0.0).astype(bf16).reshape(tiles, 16, BLK)

    pl.semaphore_wait(barrier, len(group_peers) + len(near))
    p_sends = []

    def view(x, c, a, b):
        return p_slot(p.slot(x, c, a, b))

    def pass_on(source, along_a=False, along_b=False, along_x=False, along_c=False):
        piece, sem = view(*source), R.p_recv.at[p.slot(*source)]
        to = []
        if along_a:
            to += [p.dev(p.x, p.c, p.off_a(i), p.b) for i in range(1, p.na)]
        if along_x:
            to += [p.dev(p.off_x(i), p.c, p.a, p.b) for i in range(1, p.nx)]
        if along_b:
            to += [p.dev(p.x, p.c, p.a, p.off_b(1))]
        if along_c:
            to += [p.dev(p.x, 1 - p.c, p.a, p.b)]
        for device in to:
            remote(piece, piece, R.p_send, sem, device)
            p_sends.append(device)

    def take(source):
        arrived(view(*source), R.p_recv.at[p.slot(*source)])

    pass_on((p.x, p.c, p.a, p.b), along_a=True, along_b=True, along_x=True, along_c=True)

    turned_ref = R.turned

    def half_of(b):
        return pl.ds(pl.multiple_of(b * HALF, HALF), HALF)

    def own_frame(slot, other, source):
        turned_ref[...] = source[...].astype(f32).T * R.mask_all[...]
        slot[...] = turned_ref[half_of(p.b), :].astype(bf16)
        other[...] = turned_ref[half_of(p.off_b(1)), :].astype(bf16)

    def own_slow(slot, other, source):
        stage = R.stage
        stage[...] = source[...].astype(f32)
        for s in range(slow_frames):
            at = slice(s * HALF, (s + 1) * HALF)
            for h in range(halves):
                part = stage[pl.ds(h * slow_frames + s, share, stride=halves * slow_frames), :]
                if slabs:
                    here = slice(h * BLK, (h + 1) * BLK)
                    turned_ref[here, :] = part.T * R.mask_all[here, :]
                else:
                    turned_ref[h * share : (h + 1) * share, :] = part
            if slabs:
                slot[at, :] = turned_ref[half_of(p.b), :].astype(bf16)
                other[at, :] = turned_ref[half_of(p.off_b(1)), :].astype(bf16)
            else:
                for ref, b in ((R.piece, p.b), (other, p.off_b(1))):
                    mine = pl.ds(pl.multiple_of(b * share, share), share)
                    ref[:, at] = turned_ref[mine, :].astype(bf16)
        if not slabs:
            pltpu.sync_copy(R.piece, slot)

    def from_natural(natural, wide):
        ranks = BLK // share

        def block(i, _):
            s, j = i // SLABS, lax.rem(i, SLABS)
            at_row = pl.ds(pl.multiple_of(s * HALF, HALF), HALF)
            for k in range(ranks):
                pltpu.sync_copy(
                    natural.at[j * ranks + k, :, at_row],
                    R.turn.at[pl.ds(k * share, share)],
                )
            piece = R.turn[...].astype(f32).T * R.mask[...]
            wide[j, at_row, :] = piece.astype(bf16)
            return 0

        lax.fori_loop(0, slow_frames * SLABS, block, 0)

    def gather(which, array, other, skip=0):
        sems = [R.gather_sems.at[which, i] for i in range(3)]
        return Gather(p, array, other, skip, *sems)

    x_gather = gather(0, xt_ref, R.x_other, 2)
    fc_gather = gather(1, fc_ref, R.fc_other)
    xs_gather = gather(2, xs_ref if slabs else results[5], R.xs_other)
    sc_gather = gather(3, sc_ref if slabs else results[6], R.sc_other)
    get_fast.wait()
    own_frame(x_gather.view(p.mp), R.x_other, R.fast_v)
    x_gather.start()
    get_slow.wait()
    own_slow(xs_gather.view(p.mp), R.xs_other, R.slow_v)

    get_owner_s.wait()
    steps = [1 << i for i in reversed(range(max(1, (slots - 1).bit_length())))]
    owner_s, run_device, run_start, run_count = (R.owner_s, R.run_device, R.run_start, R.run_count)

    def run(k, at):
        device = owner_s[jnp.minimum(at, NBLK - 1)]
        n = jnp.int32(1)
        for step in steps:
            more = n + step
            last = at + more - 1
            inside = owner_s[jnp.minimum(last, NBLK - 1)] == device
            n = jnp.where((more <= slots) & (last < NBLK) & inside, more, n)
        run_device[k] = device
        run_start[k] = at
        run_count[k] = n
        return at + n

    lax.fori_loop(0, devices, run, jnp.int32(0))

    for i in range(1, p.na):
        source = (p.x, p.c, p.off_a(p.na - i), p.b)
        take(source)
        pass_on(source, along_b=True, along_x=True, along_c=True)
    x_gather.relay()
    xs_gather.start()

    def tile_of(k):
        return run_device[k] * tiles - run_start[k] // 16

    def table(k, found):
        start, last = run_start[k], run_start[k] + run_count[k] - 1
        final = jnp.minimum(spot * 16 + 15, NBLK - 1)
        holds = (final >= start) & (final <= last)
        tile = jnp.where(spot == start // 16, devices * tiles + k, spot + tile_of(k))
        return jnp.where(holds, tile, found)

    R.table_v[...] = lax.fori_loop(0, devices, table, jnp.zeros((8, BLK), jnp.int32))
    get_table = fetch(R.table_v, R.table_s)

    across = p.na // 2
    for i in range(p.na):
        source = (p.x, p.c, p.off_a(p.na - i), p.off_b(1))
        take(source)
        pass_on(source, along_x=i < across, along_c=True)
        for j in range(1, p.nx):
            source = (p.off_x(j), p.c, p.off_a(p.na - i), p.b)
            take(source)
            pass_on(source, along_b=i >= across, along_c=True)
    xs_gather.relay()
    get_fcot.wait()
    own_frame(fc_gather.view(p.mp), R.fc_other, R.fcot_v)
    get_scot.wait()
    own_slow(sc_gather.view(p.mp), R.sc_other, R.scot_v)
    for i in range(p.na):
        for k in range(1, p.nx):
            source = (p.off_x(k), p.c, p.off_a(p.na - i), p.off_b(1))
            take(source)
            pass_on(source, along_c=True)
    fc_gather.start()
    sc_gather.start()
    for i in range(p.na):
        for j in range(p.nb):
            for k in range(p.nx):
                take((p.off_x(k), 1 - p.c, p.off_a(i), p.off_b(j)))
    get_table.wait()

    def tile_rows(t):
        return pl.ds(pl.multiple_of(t * 16, 16), 16)

    q_ref = R.q

    def first_tile(k, before):
        tile = p_ref[run_device[k] * tiles].astype(f32)
        shared = lax.rem(run_start[k], 16) != 0
        tile = tile + jnp.where(shared, before, 0.0)
        q_ref[k] = tile.astype(bf16)
        last = (run_start[k] + run_count[k] - 1) // 16
        alone = last == run_start[k] // 16
        return jnp.where(alone, tile, p_ref[tile_of(k) + last].astype(f32))

    lax.fori_loop(0, devices, first_tile, jnp.zeros((16, BLK), f32))
    flat_ref, table_s = R.flat, R.table_s

    def lay_out(first_block, end_block):
        first, end = first_block // 16, up(end_block, 16) // 16

        def one(t):
            source = table_s[t // BLK, lax.rem(t, BLK)]
            plain = p_ref[jnp.minimum(source, devices * tiles - 1)]
            shared = q_ref[jnp.maximum(source - devices * tiles, 0)]
            tile = jnp.where(source < devices * tiles, plain, shared)
            flat_ref[tile_rows(t), :] = tile.astype(f32)

        def eight(i, _):
            for k in range(8):
                one(first + i * 8 + k)
            return 0

        lax.fori_loop(0, (end - first) // 8, eight, 0)
        for t in range(first + (end - first) // 8 * 8, end):
            one(t)

    def matrix(out_ref, at, height, blocks):
        lay_out(at, at + height * blocks)
        for j in range(blocks):
            for o in range(0, height, 256):
                out_ref[o : o + 256, j * BLK : (j + 1) * BLK] = flat_ref[
                    pl.ds(at + o * blocks + j, 256, stride=blocks), :
                ].astype(bf16)

    group = lane_group()
    square_ref = R.square
    lat_w, s1_w, s2_w, s3_w = R.lat_w, R.s1_w, R.s2_w, R.s3_w
    f1_w, f2_w, f3_w, vec_ref = R.f1_w, R.f2_w, R.f3_w, R.vec

    def spread_rows(at, height):
        for r in range(GROUPS):
            part = jnp.where(group == r, flat_ref[at : at + height // GROUPS, :], 0.0)
            square_ref[pl.ds(r, height // GROUPS, stride=GROUPS), :] = fold_lanes(part)
        return square_ref[:height, :]

    def fast_weights():
        lay_out(AT_F1, AT_LAT)
        for k in range(3):
            tap = flat_ref[pl.ds(AT_F1 + k, B_FAST, stride=3), :].astype(bf16)
            for g in range(GROUPS):
                f1_w[g * B_FAST : (g + 1) * B_FAST, k * BLK : (k + 1) * BLK] = tap
        two = spread_rows(AT_F2, B_FAST)
        for g in range(GROUPS):
            f2_w[g * B_FAST : (g + 1) * B_FAST, :] = jnp.where(group == g, two, 0.0).astype(bf16)
        f3_w[...] = spread_rows(AT_F3, C_FAST).astype(bf16)

    matrix(lat_w, AT_LAT, C_LAT, 5)
    lay_out(AT_VEC, NBLK)
    vec_ref[...] = flat_ref[AT_VEC : AT_VEC + 32, :]
    x_gather.finish()

    zb, latb, s2b, dz, da1, wide_ref = (R.zb, R.latb, R.s2b, R.dz, R.da1, R.wide)
    c1, c2, c3, e, e3, da3 = (R.c1, R.c2, R.c3, R.e, R.e3, R.da3)
    a1p, a2p, h1p, h2p, d1p, d2p, ep, a3, e3f, da3f = (R.a1p, R.a2p, R.h1p, R.h2p, R.d1p, R.d2p, R.ep, R.a3, R.e3f, R.da3f)
    mask_ref, own3_ref, st_ref, st16_ref = (R.mask, R.own3, R.st, R.st16)
    s1b = two_in.at[pl.ds(HALF, slow_rows)]
    da2 = two_back.at[pl.ds(HALF, slow_rows)]

    def stat(which):
        return (st_ref, which) if which < 12 else (st16_ref, which - 12)

    def exchange(which):
        ref, at = stat(which)
        own = ref.at[at, member]
        for device in group_peers:
            remote(own, own, R.ex_send.at[which], R.ex_recv.at[which], device)

    def exchanged(which):
        ref, at = stat(which)
        arrived(ref.at[at, pl.ds(0, members - 1)], R.ex_recv.at[which])
        total = ref[at, 0]
        for i in range(1, members):
            total = total + ref[at, i]
        return total

    def put(which, at, vector):
        ref, index = stat(which)
        for j in range(vector.shape[1] // BLK):
            ref[index, member, at + j : at + j + 1, :] = vector[:, j * BLK : (j + 1) * BLK]

    def fill(which, at, value):
        ref, index = stat(which)
        ref[index, member, at:8, :] = jnp.full((8 - at, BLK), value, f32)

    def row_of(block, at, n):
        return jnp.concatenate([block[at + j : at + j + 1, :] for j in range(n)], 1)

    def vectors(place):
        g, b, n = place
        return row_of(vec_ref[...], g, n), row_of(vec_ref[...], b, n)

    def rows_at(i, size):
        return pl.ds(pl.multiple_of(i * size, size), size)

    def mask_at(i, width):
        part = mask_ref[pl.ds(pl.multiple_of(lax.rem(i * RC, HALF), RC), RC), :]
        return jnp.concatenate([part] * (width // BLK), 1) if width > BLK else part

    def eights(v):
        return jnp.sum(v.reshape(v.shape[0] // 8, 8, v.shape[1]), 0)

    def total_row(v):
        return jnp.sum(v, 0, keepdims=True)

    def affine(sums, squares, count, gain, bias):
        mean = sums / count
        scale = lax.rsqrt(squares / count - mean * mean + norm_eps)
        grow = gain * scale
        return mean, scale, grow, bias - mean * grow

    def sums_of(ref, n_rows, width):
        def body(i, acc):
            v = ref[rows_at(i, RC), :].astype(f32)
            return acc[0] + eights(v), acc[1] + eights(v * v)

        zero = jnp.zeros((8, width), f32)
        one, two = lax.fori_loop(0, n_rows // RC, body, (zero, zero))
        return total_row(one), total_row(two)

    def activate(src, dst, n_rows, width, grow, base):
        def body(i, _):
            at = rows_at(i, RC)
            pre = src[at, :].astype(f32) * grow + base
            dst[at, :] = (gelu(pre) * mask_at(i, width)).astype(bf16)
            return 0

        lax.fori_loop(0, n_rows // RC, body, 0)

    def slopes(src, incoming, n_rows, width, norm):
        mean, scale, grow, base = norm

        def body(i, acc):
            at = rows_at(i, RC)
            a = src[at, :].astype(f32)
            d = gelu_slope(a * grow + base) * incoming[at, :] * mask_at(i, width)
            incoming[at, :] = d
            return acc[0] + eights(d), acc[1] + eights(d * ((a - mean) * scale))

        zero = jnp.zeros((8, width), f32)
        one, two = lax.fori_loop(0, n_rows // RC, body, (zero, zero))
        return total_row(one), total_row(two)

    def back_vectors(bias_sum, gain_sum, count, norm):
        mean, scale, grow, base = norm
        k1 = grow * gain_sum / count
        return grow * bias_sum / count - k1 * (mean * scale), k1 * scale

    def raw_grads(src, pres, dst, n_rows, width, norm, q0, q1):
        grow = norm[2]

        def body(i, _):
            at = rows_at(i, RC)
            a = src[at, :].astype(f32)
            da = grow * pres[at, :] - mask_at(i, width) * (q0 + a * q1)
            dst[at, :] = da.astype(bf16)
            return 0

        lax.fori_loop(0, n_rows // RC, body, 0)

    def put_vector(row, vector):
        for j in range(vector.shape[1] // BLK):
            at = AT_VEC + row + j
            flat_ref[at : at + 1, :] = vector[:, j * BLK : (j + 1) * BLK]

    def put_pair(which, one, two, place=None):
        put(which, 0, one)
        put(which, one.shape[1] // BLK, two)
        if place is not None:
            put_vector(place[0], two)
            put_vector(place[1], one)

    slow_chunks = [slice(i, i + CH) for i in range(0, slow_rows, CH)]
    group_chunks = [slice(i, i + CH) for i in range(0, group_rows, CH)]

    def all_slabs(ref, at):
        return jnp.concatenate([ref[j, at, :] for j in range(SLABS)], 1)

    boxes = (
        (R.fast_out_box, R.fast_out_end),
        (R.slow_out_box, R.slow_out_end),
        (R.fast_grad_box, R.fast_grad_end),
        (R.slow_grad_box, R.slow_grad_end),
    )

    def box(which, kind):
        return boxes[which][0].at[kind]

    def hand_over(which):
        box_sems = R.box_send.at[which], R.box_recv.at[which]
        remote(box(which, SENT), box(which, GOT), *box_sems, (p.dp, partner))

    deliveries = []

    def deliver(source, which):
        sem = R.local.at[len(local_copies) + len(deliveries)]
        copy = pltpu.make_async_copy(source, results[which], sem)
        copy.start()
        deliveries.append(copy)

    def to_channels(block):
        turned = block.T
        if slabs:
            return turned
        lane_shift = lax.rem(p.mp * share, BLK)
        return sum(
            jnp.where(lane_shift == k * share, turned[k * share : (k + 1) * share, :], 0.0)
            for k in range(BLK // share)
        )

    def complete(which):
        ref, end = boxes[which]
        arrived(box(which, GOT), R.box_recv.at[which])
        fast = which in (FAST_OUT, FAST_GRAD)
        n = 1 if fast else slow_frames
        for s in range(n):
            at = slice(s * HALF, (s + 1) * HALF)
            for h in range(halves):
                block = jnp.where(p.b == h, ref[MINE, at, :], ref[GOT, at, :])
                block = block.T if fast else to_channels(block)
                end[pl.ds(s * halves + h, block.shape[0], stride=n * halves), :] = block
        deliver(end, which)

    for s in range(slow_frames):
        for k in range(5):
            wide_ref[s * HALF : (s + 1) * HALF, k * BLK : (k + 1) * BLK] = xt_ref[4 * s + k]
    for at in slow_chunks:
        zb[at, :] = dot_nt(wide_ref[at, :], lat_w[...]).astype(bf16)
    put_pair(EX_LAT, *sums_of(zb, slow_rows, C_LAT))
    fill(EX_LAT, 4, area)
    exchange(EX_LAT)

    fast_weights()

    def fast_rows_of(ref, first_frame, at):
        f = first_frame + at.start // HALF
        return jnp.concatenate([ref[f + i] for i in range(CH // HALF)], 0)

    for at in group_chunks:
        total = jnp.zeros((CH, BLK), f32)
        for g in range(GROUPS):
            window = jnp.concatenate(
                [fast_rows_of(xt_ref, g * per_group + 1 + k, at) for k in range(3)], 1
            )
            total = total + jnp.where(group == g, dot_nt(window, f1_w[...]), 0.0)
        a1p[at, :] = total

    def put_folded(which, one, two):
        put(which, 0, fold_lanes(one))
        put(which, 1, fold_lanes(two))

    put_folded(EX_F1, *sums_of(a1p, group_rows, BLK))
    fill(EX_F1, 2, area)
    exchange(EX_F1)
    fc_gather.relay()
    sc_gather.relay()

    matrix(s1_w, AT_S1, B_SLOW, 10)
    xs_gather.finish()
    if not slabs:
        from_natural(results[5], xs_ref)

    for at in slow_chunks:
        c1[at, :] = dot_nt(all_slabs(xs_ref, at), s1_w[:, :C_SLOW])

    total = exchanged(EX_LAT)
    area_all = total[4:5, :]
    slow_count = jnp.concatenate([area_all * float(slow_frames)] * 2, 1)
    slow_count8 = jnp.concatenate([slow_count] * 4, 1)
    fast_count = area_all * float(frames)
    lat_norm = affine(row_of(total, 0, 2), row_of(total, 2, 2), slow_count, *vectors(V_LAT))
    activate(zb, latb, slow_rows, C_LAT, lat_norm[2], lat_norm[3])
    for at in slow_chunks:
        c1[at, :] = c1[at, :] + dot_nt(latb[at, :], s1_w[:, C_SLOW:])
    put_pair(EX_S1, *sums_of(c1, slow_rows, B_SLOW))
    fill(EX_S1, 4, 0.0)
    exchange(EX_S1)

    matrix(s2_w, AT_S2, B_SLOW, 6)

    packed = vec_ref[0:1, :]

    def spread(which):
        return fold_lanes(jnp.where(group == which, packed, 0.0))

    def exchanged_two(which):
        total = exchanged(which)
        return total[0:1, :], total[1:2, :]

    f1_norm = affine(*exchanged_two(EX_F1), fast_count, spread(0), spread(1))
    activate(a1p, h1p, group_rows, BLK, f1_norm[2], f1_norm[3])
    for at in group_chunks:
        a2p[at, :] = dot_nt(h1p[at, :], f2_w[...])
    put_folded(EX_F2, *sums_of(a2p, group_rows, BLK))
    fill(EX_F2, 2, 0.0)
    exchange(EX_F2)

    total = exchanged(EX_S1)
    s1_norm = affine(row_of(total, 0, 2), row_of(total, 2, 2), slow_count, *vectors(V_S1))
    activate(c1, s1b, slow_rows, B_SLOW, s1_norm[2], s1_norm[3])

    def shifted(ref, at, k):
        return ref[at.start + k * HALF : at.stop + k * HALF, :]

    for at in slow_chunks:
        window = jnp.concatenate([shifted(two_in, at, k) for k in range(3)], 1)
        c2[at, :] = dot_nt(window, s2_w[...])
    put_pair(EX_S2, *sums_of(c2, slow_rows, B_SLOW))
    fill(EX_S2, 4, 0.0)
    exchange(EX_S2)

    matrix(s3_w, AT_S3, C_SLOW, 2)

    f2_norm = affine(*exchanged_two(EX_F2), fast_count, spread(2), spread(3))
    activate(a2p, h2p, group_rows, BLK, f2_norm[2], f2_norm[3])
    for g in range(GROUPS):
        for at in group_chunks:
            part = jnp.where(group == g, h2p[at, :], 0.0).astype(bf16)
            here = slice(g * group_rows + at.start, g * group_rows + at.stop)
            a3[here, :] = dot_nt(part, f3_w[...])
    put_pair(EX_F3, *sums_of(a3, fast_rows, BLK))
    fill(EX_F3, 2, 0.0)
    exchange(EX_F3)

    total = exchanged(EX_S2)
    s2_norm = affine(row_of(total, 0, 2), row_of(total, 2, 2), slow_count, *vectors(V_S2))
    activate(c2, s2b, slow_rows, B_SLOW, s2_norm[2], s2_norm[3])
    quarter = C_SLOW // 4
    quarters = [slice(n * quarter, (n + 1) * quarter) for n in range(4)]
    for n, lanes in enumerate(quarters):
        for at in slow_chunks:
            c3[at, lanes] = dot_nt(s2b[at, :], s3_w[lanes, :])
        one, two = sums_of(c3.at[:, lanes], slow_rows, quarter)
        put(EX_S3, 2 * n, one)
        put(EX_S3, 8 + 2 * n, two)
    exchange(EX_S3)

    f3_norm = affine(*exchanged_two(EX_F3), fast_count, *vectors(V_F3))
    for rank, kind in ((partner, SENT), (p.mp, MINE)):
        pre = a3[rows_at(rank, HALF), :] * f3_norm[2] + f3_norm[3]
        pre = pre + xt_ref[rank + 2].astype(f32)
        R.fast_out_box[kind] = gelu(pre) * mask_ref[...]
    hand_over(FAST_OUT)
    fc_gather.finish()

    def fast_slopes(i, acc):
        mean, scale, grow, base = f3_norm
        at = rows_at(i, RC)
        f, here = i // (HALF // RC), rows_at(lax.rem(i, HALF // RC), RC)
        a = a3[at, :]
        x = xt_ref[f + 2, here, :].astype(f32)
        d = gelu_slope(a * grow + base + x) * fc_ref[f, here, :].astype(f32)
        e3f[at, :] = d
        return acc[0] + eights(d), acc[1] + eights(d * ((a - mean) * scale))

    zero = jnp.zeros((8, BLK), f32)
    one, two = lax.fori_loop(0, fast_rows // RC, fast_slopes, (zero, zero))
    put_pair(EX_BF3, total_row(one), total_row(two), V_F3)
    fill(EX_BF3, 2, 0.0)
    exchange(EX_BF3)

    sc_gather.finish()
    if not slabs:
        from_natural(results[6], sc_ref)
    total = exchanged(EX_S3)
    s3_norm = affine(row_of(total, 0, 8), row_of(total, 8, 8), slow_count8, *vectors(V_S3))

    def pair_of(ref, n, at):
        return jnp.concatenate([ref[2 * n, at, :], ref[2 * n + 1, at, :]], 1).astype(f32)

    for n, lanes in enumerate(quarters):
        norm = [v[:, lanes] for v in s3_norm]

        def slow_slopes(i, acc, n=n, lanes=lanes, norm=norm):
            at = rows_at(i, RC)
            a = c3[at, lanes]
            pre = a * norm[2] + norm[3] + pair_of(xs_ref, n, at)
            d = gelu_slope(pre) * pair_of(sc_ref, n, at)
            e3[at, lanes] = d
            return acc[0] + eights(d), acc[1] + eights(d * ((a - norm[0]) * norm[1]))

        zero = jnp.zeros((8, quarter), f32)
        one, two = lax.fori_loop(0, slow_rows // RC, slow_slopes, (zero, zero))
        one, two = total_row(one), total_row(two)
        put(EX_BS3, 2 * n, one)
        put(EX_BS3, 8 + 2 * n, two)
        put_vector(V_S3[0] + 2 * n, two)
        put_vector(V_S3[1] + 2 * n, one)
    exchange(EX_BS3)

    places = []
    for kind, rank in enumerate((partner, p.mp)):
        slab = rank * share // BLK
        lanes = pl.ds(pl.multiple_of(slab * BLK, BLK), BLK)
        places.append((kind, lanes))
        norm = [
            sum(jnp.where(slab == k, v[:, k * BLK : (k + 1) * BLK], 0.0) for k in range(SLABS))
            for v in s3_norm
        ]
        for s in range(slow_frames):
            at = slice(s * HALF, (s + 1) * HALF)
            pre = c3[at, lanes] * norm[2] + norm[3] + xs_ref[slab, at, :].astype(f32)
            R.slow_out_box[kind, at, :] = gelu(pre) * mask_ref[...]
            own3_ref[kind, at, :] = e3[at, lanes]
        if kind == SENT:
            hand_over(SLOW_OUT)

    q0, q1 = back_vectors(*exchanged_two(EX_BF3), fast_count, f3_norm)
    raw_grads(a3, e3f, da3f, fast_rows, BLK, f3_norm, q0, q1)
    for at in group_chunks:
        total = jnp.zeros((CH, BLK), f32)
        for g in range(GROUPS):
            here = slice(g * group_rows + at.start, g * group_rows + at.stop)
            total = total + jnp.where(group == g, dot_nn(da3f[here, :], f3_w[...]), 0.0)
        ep[at, :] = total
    one, two = slopes(a2p, ep, group_rows, BLK, f2_norm)
    put_folded(EX_BF2, one, two)
    fill(EX_BF2, 2, 0.0)
    exchange(EX_BF2)
    vec_two = jnp.where(group == 2, fold_lanes(two), 0.0)
    vec_two = vec_two + jnp.where(group == 3, fold_lanes(one), 0.0)
    complete(FAST_OUT)

    total = exchanged(EX_BS3)
    q0, q1 = back_vectors(row_of(total, 0, 8), row_of(total, 8, 8), slow_count8, s3_norm)
    for lanes in quarters:
        norm = [v[:, lanes] for v in s3_norm]
        raw_grads(
            c3.at[:, lanes], e3.at[:, lanes], da3.at[:, lanes], slow_rows, quarter, norm,
            q0[:, lanes], q1[:, lanes]
        )
    for at in slow_chunks:
        e[at, :] = dot_nn(da3[at, :], s3_w[...])
    put_pair(EX_B2, *slopes(c2, e, slow_rows, B_SLOW, s2_norm), V_S2)
    fill(EX_B2, 4, 0.0)
    exchange(EX_B2)

    def to_flat(at, blocks, offset, lane, value):
        for j in range(value.shape[1] // BLK):
            here = pl.ds(at + offset * blocks + lane + j, value.shape[0], stride=blocks)
            flat_ref[here, :] = value[:, j * BLK : (j + 1) * BLK]

    for n, lanes in enumerate(quarters):
        to_flat(AT_S3, 2, n * quarter, 0, dot_tn(da3[:, lanes], s2b[...]))

    q0, q1 = back_vectors(*exchanged_two(EX_BF2), fast_count, f2_norm)
    raw_grads(a2p, ep, d2p, group_rows, BLK, f2_norm, q0, q1)
    for at in group_chunks:
        ep[at, :] = dot_nn(d2p[at, :], f2_w[...])
    one, two = slopes(a1p, ep, group_rows, BLK, f1_norm)
    put_folded(EX_BF1, one, two)
    fill(EX_BF1, 2, 0.0)
    exchange(EX_BF1)
    vec_one = jnp.where(group == 0, fold_lanes(two), 0.0)
    vec_one = vec_one + jnp.where(group == 1, fold_lanes(one), 0.0)
    put_vector(0, vec_one + vec_two)

    total = exchanged(EX_B2)
    q0, q1 = back_vectors(row_of(total, 0, 2), row_of(total, 2, 2), slow_count, s2_norm)
    raw_grads(c2, e, da2, slow_rows, B_SLOW, s2_norm, q0, q1)
    for at in slow_chunks:
        e[at, :] = functools.reduce(
            lambda u, v: u + v,
            [
                dot_nn(shifted(two_back, at, 2 - k), s2_w[:, k * B_SLOW : (k + 1) * B_SLOW])
                for k in range(3)
            ],
        )
    put_pair(EX_B1, *slopes(c1, e, slow_rows, B_SLOW, s1_norm), V_S1)
    fill(EX_B1, 4, 0.0)
    exchange(EX_B1)

    everything = slice(0, slow_rows)
    for k in range(3):
        part = dot_tn(two_back[HALF : HALF + slow_rows, :], shifted(two_in, everything, k))
        to_flat(AT_S2, 6, 0, 2 * k, part)

    total = jnp.zeros((BLK, BLK), f32)
    for g in range(GROUPS):
        at = slice(g * group_rows, (g + 1) * group_rows)
        total = total + jnp.where(group == g, dot_tn(da3f[at, :], h2p[...]), 0.0)

    def to_blocks(value, at):
        n = value.shape[0] // GROUPS
        square_ref[: value.shape[0], :] = fold_lanes(value)
        flat_ref[at : at + n, :] = sum(
            jnp.where(group == r, square_ref[pl.ds(r, n, stride=GROUPS), :], 0.0)
            for r in range(GROUPS)
        )

    to_blocks(total, AT_F3)
    square = dot_tn(d2p[...], h1p[...])
    to_blocks(
        sum(
            jnp.where(group == g, square[g * B_FAST : (g + 1) * B_FAST, :], 0.0)
            for g in range(GROUPS)
        ),
        AT_F2,
    )
    complete(SLOW_OUT)

    total = exchanged(EX_B1)
    q0, q1 = back_vectors(row_of(total, 0, 2), row_of(total, 2, 2), slow_count, s1_norm)
    raw_grads(c1, e, da1, slow_rows, B_SLOW, s1_norm, q0, q1)
    for at in slow_chunks:
        e[at, :] = dot_nn(da1[at, :], s1_w[:, C_SLOW:])
    put_pair(EX_BLAT, *slopes(zb, e, slow_rows, C_LAT, lat_norm), V_LAT)
    fill(EX_BLAT, 4, 0.0)
    exchange(EX_BLAT)

    for kind, lanes in places:
        for s in range(slow_frames):
            at = slice(s * HALF, (s + 1) * HALF)
            value = own3_ref[kind, at, :] + dot_nn(da1[at, :], s1_w[:, lanes])
            R.slow_grad_box[kind, at, :] = value * mask_ref[...]
        if kind == SENT:
            hand_over(SLOW_GRAD)

    q0, q1 = back_vectors(*exchanged_two(EX_BF1), fast_count, f1_norm)
    raw_grads(a1p, ep, d1p, group_rows, BLK, f1_norm, q0, q1)
    for k in range(3):
        tap = jnp.zeros((B_FAST, BLK), f32)
        for g in range(GROUPS):
            first = g * per_group + k + 1
            right = jnp.concatenate([xt_ref[first + i] for i in range(per_group)], 0)
            part = dot_tn(d1p[...], right)
            tap = tap + part[g * B_FAST : (g + 1) * B_FAST, :]
        to_flat(AT_F1, 3, 0, k, tap)

    for n in range(4):
        right = jnp.concatenate([xs_ref[2 * n], xs_ref[2 * n + 1]], 1)
        to_flat(AT_S1, 10, 0, 2 * n, dot_tn(da1[...], right))
    to_flat(AT_S1, 10, 0, 8, dot_tn(da1[...], latb[...]))

    def frame_grad(rank):
        grad = e3f[rows_at(rank, HALF), :]
        for k in range(3):
            f = rank - k + 1
            there = (f >= 0) & (f < frames)
            g, j = f // per_group, lax.rem(f, per_group)
            g, j = jnp.where(there, g, 0), jnp.where(there, j, 0)
            left = jnp.where((group == g) & there, d1p[rows_at(j, HALF), :], 0.0).astype(bf16)
            grad = grad + dot_nn(left, f1_w[:, k * BLK : (k + 1) * BLK])
        return grad

    def lateral_grad(rank):
        later, s = lax.rem(rank + 2, 4), (rank + 2) // 4
        grad = jnp.zeros((HALF, BLK), f32)
        for tap, at, there in (
            (later, s, s < slow_frames),
            (later + 4, s - 1, (later == 0) & (s > 0)),
        ):
            tap, at = jnp.where(there, tap, 0), jnp.where(there, at, 0)
            left = jnp.where(there, dz[rows_at(at, HALF), :], 0.0).astype(bf16)
            weight = lat_w[:, pl.ds(pl.multiple_of(tap * BLK, BLK), BLK)]
            grad = grad + dot_nn(left, weight)
        return grad

    R.fast_grad_box[SENT] = frame_grad(partner)
    R.fast_grad_box[MINE] = frame_grad(p.mp)

    total = exchanged(EX_BLAT)
    q0, q1 = back_vectors(row_of(total, 0, 2), row_of(total, 2, 2), slow_count, lat_norm)
    raw_grads(zb, e, dz, slow_rows, C_LAT, lat_norm, q0, q1)
    to_flat(AT_LAT, 5, 0, 0, dot_tn(dz[...], wide_ref[...]))

    height = up(slots, 16)
    sib_out, sib_in, far_out, far_in = (R.sib_out, R.sib_in, R.far_out, R.far_in)
    sib_send, sib_recv, far_send, far_recv = (R.sum_sems.at[i] for i in range(4))
    targets = [(i, j) for i in range(p.nx) for j in range(p.nb)]

    def start_of(device):
        def one(k, found):
            return jnp.where(run_device[k] == device, run_start[k], found)

        return lax.fori_loop(0, devices, one, jnp.int32(0))

    def window_of(c, target):
        x, b = p.off_x(target[0]), p.off_b(target[1])
        return flat_ref[pl.ds(start_of(p.slot(x, c, p.a, b)), height), :]

    for o, target in enumerate(targets):
        sib_out[o] = window_of(1 - p.c, target).astype(bf16)
    remote(sib_out, sib_in, sib_send, sib_recv, p.dev(p.x, 1 - p.c, p.a, p.b))

    for rank, kind in ((partner, SENT), (p.mp, MINE)):
        grad = R.fast_grad_box[kind] + lateral_grad(rank)
        R.fast_grad_box[kind] = grad * mask_ref[...]
    hand_over(FAST_GRAD)

    arrived(sib_in, sib_recv)
    for o, target in enumerate(targets[1:], 1):
        far_out[o] = (window_of(p.c, target) + sib_in[o].astype(f32)).astype(bf16)
        device = p.dev(p.off_x(target[0]), p.c, p.a, p.off_b(target[1]))
        remote(far_out.at[o], far_in.at[o], far_send, far_recv, device)
    complete(SLOW_GRAD)
    complete(FAST_GRAD)
    total = window_of(p.c, targets[0]) + sib_in[0].astype(f32)
    arrived(far_in.at[pl.ds(1, len(targets) - 1)], far_recv)
    for o in range(1, len(targets)):
        total = total + far_in[o].astype(f32)
    R.end_grad[...] = total
    deliver(R.end_grad, 4)

    sent = len(p_sends)
    while sent:
        n = min(sent, devices)
        arrived(p_ref.at[pl.ds(0, n * tiles)], R.p_send)
        sent -= n
    for each in (x_gather, xs_gather, fc_gather, sc_gather):
        each.drain()
    for which in range(EXCHANGES):
        ref, at = stat(which)
        arrived(ref.at[at, pl.ds(0, members - 1)], R.ex_send.at[which])
    for which in range(len(boxes)):
        arrived(box(which, SENT), R.box_send.at[which])
    arrived(sib_out, sib_send)
    arrived(far_out.at[pl.ds(1, len(targets) - 1)], far_send)
    for copy in deliveries:
        copy.wait()


def call_main(cfg, crop, owner, padded, master, fast, slow, fcot, scot):
    smem = pl.BlockSpec(memory_space=pltpu.SMEM)
    hbm = pl.BlockSpec(memory_space=pltpu.HBM)
    outs = outputs(cfg)
    return pl.pallas_call(
        functools.partial(main_kernel, cfg),
        out_shape=tuple(jax.ShapeDtypeStruct(s, t) for s, t in outs),
        in_specs=[smem] + [hbm] * 7,
        out_specs=tuple(hbm for _ in outs),
        scratch_shapes=list(scratch(cfg).values()),
        compiler_params=pltpu.CompilerParams(
            collective_id=0, has_side_effects=True, vmem_limit_bytes=62 << 20
        ),
        name="block",
    )(crop, owner, padded, master, fast, slow, fcot, scot)[:5]


def adam_kernel(cfg, *refs):
    nd, nm, frames, slow_frames, share, slots = cfg
    inputs, results, (sems, *held) = refs[:9], refs[9:17], refs[17:]
    owner_ref, grad, master, one, two = held[:5]
    w_out, one_out, two_out, low_out = held[9:]
    fetches = [
        pltpu.make_async_copy(source, target, sems.at[i])
        for i, (source, target) in enumerate(zip(inputs, held[:9], strict=True))
    ]
    for copy in fetches:
        copy.start()
    stores = [
        pltpu.make_async_copy(source, target, sems.at[9 + i])
        for i, (source, target) in enumerate(zip(held[9:] + held[5:9], results, strict=True))
    ]
    me = lax.axis_index("dp") * nm + lax.axis_index("mp")
    spot = lax.broadcasted_iota(jnp.int32, (8, BLK), 0) * BLK
    spot = spot + lax.broadcasted_iota(jnp.int32, (8, BLK), 1)
    lowest = jnp.full((8, BLK), NBLK, jnp.int32)
    number = jnp.zeros((8, BLK), jnp.int32)
    fetches[0].wait()
    for i in range(up(NBLK, 1024) // 1024):
        block = spot + i * 1024
        mine = (owner_ref[i * 8 : (i + 1) * 8, :] == me) & (block < NBLK)
        lowest = jnp.minimum(lowest, jnp.where(mine, block, NBLK))
        number = number + jnp.where(mine, 1, 0)
    start, count = jnp.min(lowest), jnp.sum(number)
    row = lax.broadcasted_iota(jnp.int32, (slots, BLK), 0)
    living = row < count
    block = row + start
    rate = jnp.full((slots, BLK), 0.2, f32)
    for at, width in (
        (AT_VEC, B_SLOW),
        (AT_S3, 3 * B_SLOW),
        (AT_S2, C_SLOW + C_LAT),
        (AT_S1, 5 * C_FAST),
        (AT_LAT, B_FAST),
        (AT_F2, 3 * C_FAST),
    ):
        rate = jnp.where(block < at, 0.5 / math.sqrt(width), rate)
    decay = jnp.where(block < AT_VEC, decay_rate, 0.0)
    for copy in fetches[5:]:
        copy.wait()
    for copy in stores[4:]:
        copy.start()
    for copy in fetches[1:5]:
        copy.wait()
    g = grad[:slots, :]
    first = beta_first * one[...] + (1.0 - beta_first) * g
    second = beta_second * two[...] + (1.0 - beta_second) * g * g
    lift_one = 1.0 - beta_first**STEP
    lift_two = 1.0 - beta_second**STEP
    update = first / lift_one / (jnp.sqrt(second / lift_two) + adam_eps)
    weight = master[...]
    weight = jnp.where(living, weight - rate * (update + decay * weight), 0.0)
    w_out[...] = weight
    one_out[...] = jnp.where(living, first, 0.0)
    two_out[...] = jnp.where(living, second, 0.0)
    low_out[...] = weight.astype(bf16)
    for copy in stores[:4]:
        copy.start()
    for copy in stores:
        copy.wait()


def call_adam(cfg, owner, grad, master, one, two, passed):
    arrays = (owner, grad, master, one, two, *passed)
    hbm = pl.BlockSpec(memory_space=pltpu.HBM)
    new = [jax.ShapeDtypeStruct(master.shape, t) for t in (f32, f32, f32, bf16)]
    results = new + [jax.ShapeDtypeStruct(a.shape, a.dtype) for a in passed]
    held = [pltpu.VMEM(a.shape, a.dtype) for a in (*arrays, *new)]
    return pl.pallas_call(
        functools.partial(adam_kernel, cfg),
        out_shape=tuple(results),
        in_specs=[hbm] * len(arrays),
        out_specs=(hbm,) * len(results),
        scratch_shapes=[pltpu.SemaphoreType.DMA((len(arrays) + len(results),)), *held],
        compiler_params=pltpu.CompilerParams(vmem_limit_bytes=62 << 20),
        name="adam",
    )(*arrays)


def solution(mesh):
    nd, nm = mesh.shape["dp"], mesh.shape["mp"]

    def local(fast_in, slow_in, fast_cot, slow_cot, crop, owner, master, one, two):
        share, slow_frames = slow_in.shape[0], slow_in.shape[1]
        cfg = (nd, nm, fast_in.shape[1] * nm, slow_frames, share, master.shape[0])

        def halves(array):
            split = array.reshape(share, slow_frames, POS // BLK, BLK)
            return split.transpose(0, 2, 1, 3).reshape(-1, BLK)

        padded = jnp.pad(owner, (0, up(NBLK, 1024) - NBLK)).reshape(-1, BLK)
        *passed, grad = call_main(
            cfg,
            crop,
            owner,
            padded,
            master,
            fast_in.reshape(C_FAST, POS),
            halves(slow_in),
            fast_cot.reshape(C_FAST, POS),
            halves(slow_cot),
        )
        new = call_adam(cfg, padded, grad, master, one, two, passed)
        return (
            new[4].reshape(fast_in.shape),
            new[5].reshape(slow_in.shape),
            new[6].reshape(fast_in.shape),
            new[7].reshape(slow_in.shape),
            *new[:4],
        )

    return jax.shard_map(
        local,
        mesh=mesh,
        in_specs=(
            P(None, "mp", "dp", None),
            P("mp", None, "dp", None),
            P(None, "mp", "dp", None),
            P("mp", None, "dp", None),
            P("dp"),
            P(),
            P(("dp", "mp"), None),
            P(("dp", "mp"), None),
            P(("dp", "mp"), None),
        ),
        out_specs=(
            P(None, "mp", "dp", None),
            P("mp", None, "dp", None),
            P(None, "mp", "dp", None),
            P("mp", None, "dp", None),
            P(("dp", "mp"), None),
            P(("dp", "mp"), None),
            P(("dp", "mp"), None),
            P(("dp", "mp"), None),
        ),
        check_vma=False,
    )
```

time: 104 us -> 88.2 us (0.85)
  Pallas kernels: 96.6 us -> 85.3 us
  local copies, waits for them, and re-layouts: 6.08 us -> 1.38 us
    pallas_call x1, Pallas kernels: 94.8 us -> 82.5 us  [call_main(): pl.pallas_call(functools.partial(main_kernel, cfg), out_shape=tuple((jax....]
    unnamed x18 -> x0, local copies, waits for them, and re-layouts: 4.66 us -> none
    pallas_call x1, Pallas kernels: 1.81 us -> 2.87 us  [call_adam(): pl.pallas_call(functools.partial(adam_kernel, cfg), out_shape=tuple(resul...]
where the time goes in v3:
time: 88.2 us; the launch traced here: 88 us
  Pallas kernels  85.3 us (97%)
  local copies, waits for them, and re-layouts  1.38 us (2%)
  between operations  1.29 us (1%)
    pallas_call x1, Pallas kernels, call_main(): pl.pallas_call(functools.partial(main_kernel, cfg), out_shape=tuple((jax....  82.5 us
    pallas_call x1, Pallas kernels, call_adam(): pl.pallas_call(functools.partial(adam_kernel, cfg), out_shape=tuple(resul...  2.87 us

profile of v3, /device:TPU:25, one launch (start us, length us, event | category | flops | bytes accessed | tf_op | source)
XLA Modules:
  0.0 88.0 jit_solution(6179532919985989100)
XLA Ops:
  1.3 1.4 %pad_bitcast_fusion.refs_2_.refs_0_ = s32[64,128]{1,0:T(8,128)} fusion(s32[7591]{0:T(1024)} %refs_1_.1), kind=kLoop, calls=%fused_computation | loop fusion | bytes 63132 | tf_op jit(solution)/shard_map/reshape | solution.py:1295
  2.7 82.5 %block.1 = (f32[256,128]{1,0:T(8,128)}, f32[512,128]{1,0:T(8,128)}, f32[256,128]{1,0:T(8,128)}, f32[512,128]{1,0:T(8,128)}, f32[480,128]{1,0:T(8,128)}) custom-call(s32[1]{0:T(128)S(6)} %copy.23.refs_0_, s32[7591]{0:T(1024)} %refs_1_.1, s32[64,128]{1,0:T(8,128)} %pad_bitcast_fusion.refs_2_.refs_0_, f32[476,128]{1,0:T(8,128)} %refs_2_.1, ...), custom_call_target="tpu_custom_call" | custom-call | tf_op jit(solution)/shard_map/block/pallas_call | solution.py:1189
  85.1 2.9 %adam.1 = (f32[476,128]{1,0:T(8,128)}, f32[476,128]{1,0:T(8,128)}, f32[476,128]{1,0:T(8,128)}, bf16[476,128]{1,0:T(8,128)(2,1)}, f32[256,128]{1,0:T(8,128)}, /*i...) custom-call(s32[64,128]{1,0:T(8,128)} %pad_bitcast_fusion.refs_2_.refs_0_, ...), custom_call_target="tpu_custom_call" | custom-call | tf_op jit(solution)/shard_map/adam/pallas_call | solution.py:1273

commit v4 on v3

--- a/solution.py
+++ b/solution.py
@@ -185,6 +185,7 @@
     halves = POS // BLK
     fast, slow = (C_FAST * halves, BLK), (share * slow_frames * halves, BLK)
     result = [(fast, f32), (slow, f32), (fast, f32), (slow, f32), ((up(slots, 16), BLK), f32)]
+    result += [((8, BLK), jnp.int32)]
     if share != BLK:
         result += [((nm, share, slow_frames * HALF), bf16)] * 2
     return result
@@ -202,11 +203,13 @@
     vmem, smem, dma = pltpu.VMEM, pltpu.SMEM, pltpu.SemaphoreType.DMA
     piece = (slow_rows, BLK) if share == BLK else (share, slow_rows)
     result = dict(
-        owner_v=vmem((up(NBLK, 1024) // BLK, BLK), jnp.int32),
+        owner_v=vmem((NBLK,), jnp.int32),
         owner_s=smem((NBLK,), jnp.int32),
         run_device=smem((devices,), jnp.int32),
         run_start=smem((devices,), jnp.int32),
         run_count=smem((devices,), jnp.int32),
+        win_start=smem((group,), jnp.int32),
+        info=vmem((8, BLK), jnp.int32),
         table_v=vmem((8, BLK), jnp.int32),
         table_s=smem((8, BLK), jnp.int32),
         shift=vmem((rows + 16, BLK), f32),
@@ -271,7 +274,6 @@
         da3f=vmem((fast_rows, BLK), bf16),
         square=vmem((BLK, BLK), f32),
         flat=vmem((up(NBLK + height, 64), BLK), f32),
-        own3=vmem((COLUMNS, slow_rows, BLK), f32),
         sib_out=vmem((windows, height, BLK), bf16),
         sib_in=vmem((windows, height, BLK), bf16),
         far_out=vmem((windows, height, BLK), bf16),
@@ -290,13 +292,15 @@
         slow_grad_end=vmem((share * slow_frames * halves, BLK), f32),
         end_grad=vmem((height, BLK), f32),
         p_send=dma(()),
-        p_recv=dma((devices,)),
+        p_recv=dma((devices // 2,)),
+        p_sibling=dma(()),
         gather_sems=dma((4, 3)),
-        ex_send=dma((EXCHANGES,)),
+        ex_send=dma(()),
         ex_recv=dma((EXCHANGES,)),
-        box_send=dma((4,)),
+        box_send=dma(()),
         box_recv=dma((4,)),
-        sum_sems=dma((4,)),
+        sum_sems=dma((3,)),
+        sib_recv=dma((windows,)),
         local=dma((16,)),
     )
     return result
@@ -305,8 +309,8 @@
 def main_kernel(cfg, *refs):
     nd, nm, frames, slow_frames, share, slots = cfg
     n_out = len(outputs(cfg))
-    args, results, held = refs[:8], refs[8 : 8 + n_out], refs[8 + n_out :]
-    crop_in, owner_in, owners_in, master_in, fast_in, slow_in, fcot_in, scot_in = args
+    args, results, held = refs[:7], refs[7 : 7 + n_out], refs[7 + n_out :]
+    crop_in, owner_in, master_in, fast_in, slow_in, fcot_in, scot_in = args
     R = types.SimpleNamespace(**dict(zip(scratch(cfg), held, strict=True)))
     p = Place(nd, nm)
     devices = nd * nm
@@ -323,10 +327,11 @@
     members = nd * p.nb
     member = p.dp * p.nb + p.b
     group_peers = [
-        (lax.rem(p.dp + i, nd), p.a * p.nb + p.off_b(k))
-        for i in range(nd)
-        for k in range(p.nb)
-        if i or k
+        p.dev(p.off_x(i), lax.rem(p.c + k, 2), p.a, p.off_b(j))
+        for i in reversed(range(p.nx))
+        for j in reversed(range(p.nb))
+        for k in range(2)
+        if i or j or k
     ]
     near = [p.dev(p.x, p.c, p.off_a(i), p.b) for i in range(1, p.na)]
     barrier = pltpu.get_barrier_semaphore()
@@ -341,11 +346,11 @@
         local_copies.append(copy)
         return copy
 
-    get_owner = fetch(owners_in, R.owner_v)
+    get_owner = fetch(owner_in, R.owner_v)
+    get_owner_s = fetch(owner_in, R.owner_s)
     get_master = fetch(master_in, R.shift.at[pl.ds(16, slots)])
     get_fast = fetch(fast_in, R.fast_v)
     get_slow = fetch(slow_in, R.slow_v)
-    get_owner_s = fetch(owner_in, R.owner_s)
     get_fcot = fetch(fcot_in, R.fcot_v)
     get_scot = fetch(scot_in, R.scot_v)
 
@@ -367,13 +372,27 @@
     spot = spot + lax.broadcasted_iota(jnp.int32, (8, BLK), 1)
     lowest = jnp.full((8, BLK), NBLK, jnp.int32)
     number = jnp.zeros((8, BLK), jnp.int32)
-    for i in range(up(NBLK, 1024) // 1024):
-        block = spot + i * 1024
-        mine = R.owner_v[i * 8 : (i + 1) * 8, :] == me
-        mine = mine & (block < NBLK)
-        lowest = jnp.minimum(lowest, jnp.where(mine, block, NBLK))
+    whole = NBLK // 1024 * 1024
+    for i in range(0, whole, 1024):
+        mine = R.owner_v[pl.ds(i, 1024)].reshape(8, BLK) == me
+        lowest = jnp.minimum(lowest, jnp.where(mine, spot + i, NBLK))
         number = number + jnp.where(mine, 1, 0)
-    my_start, my_count = jnp.min(lowest), jnp.sum(number)
+    for i in range(whole, NBLK // BLK * BLK, BLK):
+        mine = R.owner_v[pl.ds(i, BLK)].reshape(1, BLK) == me
+        mine = mine & (spot < BLK)
+        lowest = jnp.minimum(lowest, jnp.where(mine, spot + i, NBLK))
+        number = number + jnp.where(mine, 1, 0)
+    get_owner_s.wait()
+
+    def last_ones(i, found):
+        first, n = found
+        mine = R.owner_s[i] == me
+        return jnp.where(mine, jnp.minimum(first, i), first), n + jnp.where(mine, 1, 0)
+
+    found = jnp.min(lowest), jnp.sum(number)
+    my_start, my_count = lax.fori_loop(NBLK // BLK * BLK, NBLK, last_ones, found)
+    line = lax.broadcasted_iota(jnp.int32, (8, BLK), 0)
+    R.info[...] = jnp.where(line == 0, my_start, my_count)
     shift = lax.rem(my_start, 16)
     get_master.wait()
     moved = R.shift[pl.ds(16 - shift, rows), :]
@@ -392,25 +411,32 @@
     def view(x, c, a, b):
         return p_slot(p.slot(x, c, a, b))
 
-    def pass_on(source, along_a=False, along_b=False, along_x=False, along_c=False):
-        piece, sem = view(*source), R.p_recv.at[p.slot(*source)]
+    def came(source):
+        x, c, a, b = source
+        return R.p_recv.at[x * nm + a * p.nb + b]
+
+    def pass_on(source, along_a=(), along_b=False, along_x=False, along_c=False):
+        piece, sem = view(*source), came(source)
         to = []
-        if along_a:
-            to += [p.dev(p.x, p.c, p.off_a(i), p.b) for i in range(1, p.na)]
+        for i in along_a:
+            to += [p.dev(p.x, p.c, p.off_a(i), p.b)]
         if along_x:
             to += [p.dev(p.off_x(i), p.c, p.a, p.b) for i in range(1, p.nx)]
         if along_b:
             to += [p.dev(p.x, p.c, p.a, p.off_b(1))]
-        if along_c:
-            to += [p.dev(p.x, 1 - p.c, p.a, p.b)]
         for device in to:
             remote(piece, piece, R.p_send, sem, device)
             p_sends.append(device)
+        if along_c:
+            device = p.dev(p.x, 1 - p.c, p.a, p.b)
+            remote(piece, piece, R.p_send, R.p_sibling, device)
+            p_sends.append(device)
 
     def take(source):
-        arrived(view(*source), R.p_recv.at[p.slot(*source)])
-
-    pass_on((p.x, p.c, p.a, p.b), along_a=True, along_b=True, along_x=True, along_c=True)
+        arrived(view(*source), came(source))
+
+    here = (p.x, p.c, p.a, p.b)
+    pass_on(here, along_a=range(1, p.na), along_b=True, along_x=True, along_c=True)
 
     turned_ref = R.turned
 
@@ -467,15 +493,14 @@
 
     x_gather = gather(0, xt_ref, R.x_other, 2)
     fc_gather = gather(1, fc_ref, R.fc_other)
-    xs_gather = gather(2, xs_ref if slabs else results[5], R.xs_other)
-    sc_gather = gather(3, sc_ref if slabs else results[6], R.sc_other)
+    xs_gather = gather(2, xs_ref if slabs else results[6], R.xs_other)
+    sc_gather = gather(3, sc_ref if slabs else results[7], R.sc_other)
     get_fast.wait()
     own_frame(x_gather.view(p.mp), R.x_other, R.fast_v)
     x_gather.start()
     get_slow.wait()
     own_slow(xs_gather.view(p.mp), R.xs_other, R.slow_v)
 
-    get_owner_s.wait()
     steps = [1 << i for i in reversed(range(max(1, (slots - 1).bit_length())))]
     owner_s, run_device, run_start, run_count = (R.owner_s, R.run_device, R.run_start, R.run_count)
 
@@ -493,6 +518,15 @@
         return at + n
 
     lax.fori_loop(0, devices, run, jnp.int32(0))
+
+    targets = [(i, j) for i in range(p.nx) for j in range(p.nb)]
+    owners = [p.slot(p.off_x(i), c, p.a, p.off_b(j)) for c in (p.c, 1 - p.c) for i, j in targets]
+
+    def find(k, found):
+        return [jnp.where(run_device[k] == d, run_start[k], at) for d, at in zip(owners, found)]
+
+    for i, at in enumerate(lax.fori_loop(0, devices, find, [jnp.int32(0)] * len(owners))):
+        R.win_start[i] = at
 
     for i in range(1, p.na):
         source = (p.x, p.c, p.off_a(p.na - i), p.b)
@@ -533,12 +567,8 @@
             source = (p.off_x(k), p.c, p.off_a(p.na - i), p.off_b(1))
             take(source)
             pass_on(source, along_c=True)
-    fc_gather.start()
     sc_gather.start()
-    for i in range(p.na):
-        for j in range(p.nb):
-            for k in range(p.nx):
-                take((p.off_x(k), 1 - p.c, p.off_a(i), p.off_b(j)))
+    arrived(p_ref.at[pl.ds(0, devices // 2 * tiles)], R.p_sibling)
     get_table.wait()
 
     def tile_rows(t):
@@ -615,7 +645,7 @@
     zb, latb, s2b, dz, da1, wide_ref = (R.zb, R.latb, R.s2b, R.dz, R.da1, R.wide)
     c1, c2, c3, e, e3, da3 = (R.c1, R.c2, R.c3, R.e, R.e3, R.da3)
     a1p, a2p, h1p, h2p, d1p, d2p, ep, a3, e3f, da3f = (R.a1p, R.a2p, R.h1p, R.h2p, R.d1p, R.d2p, R.ep, R.a3, R.e3f, R.da3f)
-    mask_ref, own3_ref, st_ref, st16_ref = (R.mask, R.own3, R.st, R.st16)
+    mask_ref, st_ref, st16_ref = R.mask, R.st, R.st16
     s1b = two_in.at[pl.ds(HALF, slow_rows)]
     da2 = two_back.at[pl.ds(HALF, slow_rows)]
 
@@ -626,7 +656,7 @@
         ref, at = stat(which)
         own = ref.at[at, member]
         for device in group_peers:
-            remote(own, own, R.ex_send.at[which], R.ex_recv.at[which], device)
+            remote(own, own, R.ex_send, R.ex_recv.at[which], device)
 
     def exchanged(which):
         ref, at = stat(which)
@@ -671,13 +701,16 @@
         grow = gain * scale
         return mean, scale, grow, bias - mean * grow
 
+    def loop(n, body, start):
+        return lax.fori_loop(0, n, body, start, unroll=n if n <= 8 else 4)
+
     def sums_of(ref, n_rows, width):
         def body(i, acc):
             v = ref[rows_at(i, RC), :].astype(f32)
             return acc[0] + eights(v), acc[1] + eights(v * v)
 
         zero = jnp.zeros((8, width), f32)
-        one, two = lax.fori_loop(0, n_rows // RC, body, (zero, zero))
+        one, two = loop(n_rows // RC, body, (zero, zero))
         return total_row(one), total_row(two)
 
     def activate(src, dst, n_rows, width, grow, base):
@@ -687,7 +720,7 @@
             dst[at, :] = (gelu(pre) * mask_at(i, width)).astype(bf16)
             return 0
 
-        lax.fori_loop(0, n_rows // RC, body, 0)
+        loop(n_rows // RC, body, 0)
 
     def slopes(src, incoming, n_rows, width, norm):
         mean, scale, grow, base = norm
@@ -700,7 +733,7 @@
             return acc[0] + eights(d), acc[1] + eights(d * ((a - mean) * scale))
 
         zero = jnp.zeros((8, width), f32)
-        one, two = lax.fori_loop(0, n_rows // RC, body, (zero, zero))
+        one, two = loop(n_rows // RC, body, (zero, zero))
         return total_row(one), total_row(two)
 
     def back_vectors(bias_sum, gain_sum, count, norm):
@@ -718,7 +751,7 @@
             dst[at, :] = da.astype(bf16)
             return 0
 
-        lax.fori_loop(0, n_rows // RC, body, 0)
+        loop(n_rows // RC, body, 0)
 
     def put_vector(row, vector):
         for j in range(vector.shape[1] // BLK):
@@ -749,7 +782,7 @@
         return boxes[which][0].at[kind]
 
     def hand_over(which):
-        box_sems = R.box_send.at[which], R.box_recv.at[which]
+        box_sems = R.box_send, R.box_recv.at[which]
         remote(box(which, SENT), box(which, GOT), *box_sems, (p.dp, partner))
 
     deliveries = []
@@ -814,13 +847,13 @@
     put_folded(EX_F1, *sums_of(a1p, group_rows, BLK))
     fill(EX_F1, 2, area)
     exchange(EX_F1)
-    fc_gather.relay()
     sc_gather.relay()
+    fc_gather.start()
 
     matrix(s1_w, AT_S1, B_SLOW, 10)
     xs_gather.finish()
     if not slabs:
-        from_natural(results[5], xs_ref)
+        from_natural(results[6], xs_ref)
 
     for at in slow_chunks:
         c1[at, :] = dot_nt(all_slabs(xs_ref, at), s1_w[:, :C_SLOW])
@@ -839,6 +872,8 @@
     exchange(EX_S1)
 
     matrix(s2_w, AT_S2, B_SLOW, 6)
+    fc_gather.relay()
+    matrix(s3_w, AT_S3, C_SLOW, 2)
 
     packed = vec_ref[0:1, :]
 
@@ -870,8 +905,6 @@
     put_pair(EX_S2, *sums_of(c2, slow_rows, B_SLOW))
     fill(EX_S2, 4, 0.0)
     exchange(EX_S2)
-
-    matrix(s3_w, AT_S3, C_SLOW, 2)
 
     f2_norm = affine(*exchanged_two(EX_F2), fast_count, spread(2), spread(3))
     activate(a2p, h2p, group_rows, BLK, f2_norm[2], f2_norm[3])
@@ -903,6 +936,35 @@
         pre = pre + xt_ref[rank + 2].astype(f32)
         R.fast_out_box[kind] = gelu(pre) * mask_ref[...]
     hand_over(FAST_OUT)
+    sc_gather.finish()
+    if not slabs:
+        from_natural(results[7], sc_ref)
+    total = exchanged(EX_S3)
+    s3_norm = affine(row_of(total, 0, 8), row_of(total, 8, 8), slow_count8, *vectors(V_S3))
+
+    def pair_of(ref, n, at):
+        return jnp.concatenate([ref[2 * n, at, :], ref[2 * n + 1, at, :]], 1).astype(f32)
+
+    for n, lanes in enumerate(quarters):
+        norm = [v[:, lanes] for v in s3_norm]
+
+        def slow_slopes(i, acc, n=n, lanes=lanes, norm=norm):
+            at = rows_at(i, RC)
+            a = c3[at, lanes]
+            pre = a * norm[2] + norm[3] + pair_of(xs_ref, n, at)
+            d = gelu_slope(pre) * pair_of(sc_ref, n, at)
+            e3[at, lanes] = d
+            return acc[0] + eights(d), acc[1] + eights(d * ((a - norm[0]) * norm[1]))
+
+        zero = jnp.zeros((8, quarter), f32)
+        one, two = loop(slow_rows // RC, slow_slopes, (zero, zero))
+        one, two = total_row(one), total_row(two)
+        put(EX_BS3, 2 * n, one)
+        put(EX_BS3, 8 + 2 * n, two)
+        put_vector(V_S3[0] + 2 * n, two)
+        put_vector(V_S3[1] + 2 * n, one)
+    exchange(EX_BS3)
+
     fc_gather.finish()
 
     def fast_slopes(i, acc):
@@ -916,56 +978,49 @@
         return acc[0] + eights(d), acc[1] + eights(d * ((a - mean) * scale))
 
     zero = jnp.zeros((8, BLK), f32)
-    one, two = lax.fori_loop(0, fast_rows // RC, fast_slopes, (zero, zero))
+    one, two = loop(fast_rows // RC, fast_slopes, (zero, zero))
     put_pair(EX_BF3, total_row(one), total_row(two), V_F3)
     fill(EX_BF3, 2, 0.0)
     exchange(EX_BF3)
 
-    sc_gather.finish()
-    if not slabs:
-        from_natural(results[6], sc_ref)
-    total = exchanged(EX_S3)
-    s3_norm = affine(row_of(total, 0, 8), row_of(total, 8, 8), slow_count8, *vectors(V_S3))
-
-    def pair_of(ref, n, at):
-        return jnp.concatenate([ref[2 * n, at, :], ref[2 * n + 1, at, :]], 1).astype(f32)
-
-    for n, lanes in enumerate(quarters):
-        norm = [v[:, lanes] for v in s3_norm]
-
-        def slow_slopes(i, acc, n=n, lanes=lanes, norm=norm):
-            at = rows_at(i, RC)
-            a = c3[at, lanes]
-            pre = a * norm[2] + norm[3] + pair_of(xs_ref, n, at)
-            d = gelu_slope(pre) * pair_of(sc_ref, n, at)
-            e3[at, lanes] = d
-            return acc[0] + eights(d), acc[1] + eights(d * ((a - norm[0]) * norm[1]))
-
-        zero = jnp.zeros((8, quarter), f32)
-        one, two = lax.fori_loop(0, slow_rows // RC, slow_slopes, (zero, zero))
-        one, two = total_row(one), total_row(two)
-        put(EX_BS3, 2 * n, one)
-        put(EX_BS3, 8 + 2 * n, two)
-        put_vector(V_S3[0] + 2 * n, two)
-        put_vector(V_S3[1] + 2 * n, one)
-    exchange(EX_BS3)
-
-    places = []
-    for kind, rank in enumerate((partner, p.mp)):
+    def slow_place(rank):
         slab = rank * share // BLK
-        lanes = pl.ds(pl.multiple_of(slab * BLK, BLK), BLK)
-        places.append((kind, lanes))
-        norm = [
+        return slab, pl.ds(pl.multiple_of(slab * BLK, BLK), BLK)
+
+    def slow_result(kind, rank):
+        slab, lanes = slow_place(rank)
+        grow, base = (
             sum(jnp.where(slab == k, v[:, k * BLK : (k + 1) * BLK], 0.0) for k in range(SLABS))
-            for v in s3_norm
-        ]
+            for v in s3_norm[2:]
+        )
         for s in range(slow_frames):
             at = slice(s * HALF, (s + 1) * HALF)
-            pre = c3[at, lanes] * norm[2] + norm[3] + xs_ref[slab, at, :].astype(f32)
+            pre = c3[at, lanes] * grow + base + xs_ref[slab, at, :].astype(f32)
             R.slow_out_box[kind, at, :] = gelu(pre) * mask_ref[...]
-            own3_ref[kind, at, :] = e3[at, lanes]
-        if kind == SENT:
-            hand_over(SLOW_OUT)
+
+    def slow_input_grad(kind, rank):
+        slab, lanes = slow_place(rank)
+        for s in range(slow_frames):
+            at = slice(s * HALF, (s + 1) * HALF)
+            value = e3[at, lanes] + dot_nn(da1[at, :], s1_w[:, lanes])
+            R.slow_grad_box[kind, at, :] = value * mask_ref[...]
+
+    slow_result(SENT, partner)
+    hand_over(SLOW_OUT)
+
+    total = exchanged(EX_BS3)
+    q0, q1 = back_vectors(row_of(total, 0, 8), row_of(total, 8, 8), slow_count8, s3_norm)
+    for lanes in quarters:
+        norm = [v[:, lanes] for v in s3_norm]
+        raw_grads(
+            c3.at[:, lanes], e3.at[:, lanes], da3.at[:, lanes], slow_rows, quarter, norm,
+            q0[:, lanes], q1[:, lanes]
+        )
+    for at in slow_chunks:
+        e[at, :] = dot_nn(da3[at, :], s3_w[...])
+    put_pair(EX_B2, *slopes(c2, e, slow_rows, B_SLOW, s2_norm), V_S2)
+    fill(EX_B2, 4, 0.0)
+    exchange(EX_B2)
 
     q0, q1 = back_vectors(*exchanged_two(EX_BF3), fast_count, f3_norm)
     raw_grads(a3, e3f, da3f, fast_rows, BLK, f3_norm, q0, q1)
@@ -981,21 +1036,6 @@
     exchange(EX_BF2)
     vec_two = jnp.where(group == 2, fold_lanes(two), 0.0)
     vec_two = vec_two + jnp.where(group == 3, fold_lanes(one), 0.0)
-    complete(FAST_OUT)
-
-    total = exchanged(EX_BS3)
-    q0, q1 = back_vectors(row_of(total, 0, 8), row_of(total, 8, 8), slow_count8, s3_norm)
-    for lanes in quarters:
-        norm = [v[:, lanes] for v in s3_norm]
-        raw_grads(
-            c3.at[:, lanes], e3.at[:, lanes], da3.at[:, lanes], slow_rows, quarter, norm,
-            q0[:, lanes], q1[:, lanes]
-        )
-    for at in slow_chunks:
-        e[at, :] = dot_nn(da3[at, :], s3_w[...])
-    put_pair(EX_B2, *slopes(c2, e, slow_rows, B_SLOW, s2_norm), V_S2)
-    fill(EX_B2, 4, 0.0)
-    exchange(EX_B2)
 
     def to_flat(at, blocks, offset, lane, value):
         for j in range(value.shape[1] // BLK):
@@ -1004,18 +1044,6 @@
 
     for n, lanes in enumerate(quarters):
         to_flat(AT_S3, 2, n * quarter, 0, dot_tn(da3[:, lanes], s2b[...]))
-
-    q0, q1 = back_vectors(*exchanged_two(EX_BF2), fast_count, f2_norm)
-    raw_grads(a2p, ep, d2p, group_rows, BLK, f2_norm, q0, q1)
-    for at in group_chunks:
-        ep[at, :] = dot_nn(d2p[at, :], f2_w[...])
-    one, two = slopes(a1p, ep, group_rows, BLK, f1_norm)
-    put_folded(EX_BF1, one, two)
-    fill(EX_BF1, 2, 0.0)
-    exchange(EX_BF1)
-    vec_one = jnp.where(group == 0, fold_lanes(two), 0.0)
-    vec_one = vec_one + jnp.where(group == 1, fold_lanes(one), 0.0)
-    put_vector(0, vec_one + vec_two)
 
     total = exchanged(EX_B2)
     q0, q1 = back_vectors(row_of(total, 0, 2), row_of(total, 2, 2), slow_count, s2_norm)
@@ -1032,6 +1060,18 @@
     fill(EX_B1, 4, 0.0)
     exchange(EX_B1)
 
+    q0, q1 = back_vectors(*exchanged_two(EX_BF2), fast_count, f2_norm)
+    raw_grads(a2p, ep, d2p, group_rows, BLK, f2_norm, q0, q1)
+    for at in group_chunks:
+        ep[at, :] = dot_nn(d2p[at, :], f2_w[...])
+    one, two = slopes(a1p, ep, group_rows, BLK, f1_norm)
+    put_folded(EX_BF1, one, two)
+    fill(EX_BF1, 2, 0.0)
+    exchange(EX_BF1)
+    vec_one = jnp.where(group == 0, fold_lanes(two), 0.0)
+    vec_one = vec_one + jnp.where(group == 1, fold_lanes(one), 0.0)
+    put_vector(0, vec_one + vec_two)
+
     everything = slice(0, slow_rows)
     for k in range(3):
         part = dot_tn(two_back[HALF : HALF + slow_rows, :], shifted(two_in, everything, k))
@@ -1059,7 +1099,6 @@
         ),
         AT_F2,
     )
-    complete(SLOW_OUT)
 
     total = exchanged(EX_B1)
     q0, q1 = back_vectors(row_of(total, 0, 2), row_of(total, 2, 2), slow_count, s1_norm)
@@ -1069,14 +1108,6 @@
     put_pair(EX_BLAT, *slopes(zb, e, slow_rows, C_LAT, lat_norm), V_LAT)
     fill(EX_BLAT, 4, 0.0)
     exchange(EX_BLAT)
-
-    for kind, lanes in places:
-        for s in range(slow_frames):
-            at = slice(s * HALF, (s + 1) * HALF)
-            value = own3_ref[kind, at, :] + dot_nn(da1[at, :], s1_w[:, lanes])
-            R.slow_grad_box[kind, at, :] = value * mask_ref[...]
-        if kind == SENT:
-            hand_over(SLOW_GRAD)
 
     q0, q1 = back_vectors(*exchanged_two(EX_BF1), fast_count, f1_norm)
     raw_grads(a1p, ep, d1p, group_rows, BLK, f1_norm, q0, q1)
@@ -1118,8 +1149,8 @@
             grad = grad + dot_nn(left, weight)
         return grad
 
-    R.fast_grad_box[SENT] = frame_grad(partner)
-    R.fast_grad_box[MINE] = frame_grad(p.mp)
+    slow_input_grad(SENT, partner)
+    hand_over(SLOW_GRAD)
 
     total = exchanged(EX_BLAT)
     q0, q1 = back_vectors(row_of(total, 0, 2), row_of(total, 2, 2), slow_count, lat_norm)
@@ -1128,41 +1159,45 @@
 
     height = up(slots, 16)
     sib_out, sib_in, far_out, far_in = (R.sib_out, R.sib_in, R.far_out, R.far_in)
-    sib_send, sib_recv, far_send, far_recv = (R.sum_sems.at[i] for i in range(4))
-    targets = [(i, j) for i in range(p.nx) for j in range(p.nb)]
-
-    def start_of(device):
-        def one(k, found):
-            return jnp.where(run_device[k] == device, run_start[k], found)
-
-        return lax.fori_loop(0, devices, one, jnp.int32(0))
-
-    def window_of(c, target):
-        x, b = p.off_x(target[0]), p.off_b(target[1])
-        return flat_ref[pl.ds(start_of(p.slot(x, c, p.a, b)), height), :]
-
-    for o, target in enumerate(targets):
-        sib_out[o] = window_of(1 - p.c, target).astype(bf16)
-    remote(sib_out, sib_in, sib_send, sib_recv, p.dev(p.x, 1 - p.c, p.a, p.b))
-
-    for rank, kind in ((partner, SENT), (p.mp, MINE)):
-        grad = R.fast_grad_box[kind] + lateral_grad(rank)
-        R.fast_grad_box[kind] = grad * mask_ref[...]
+    sib_send, far_send, far_recv = (R.sum_sems.at[i] for i in range(3))
+    sib_recv = R.sib_recv
+
+    def window_of(c, o):
+        return flat_ref[pl.ds(R.win_start[c * len(targets) + o], height), :]
+
+    order = [*range(1, len(targets)), 0]
+    for o in order:
+        sib_out[o] = window_of(1, o).astype(bf16)
+        sibling = p.dev(p.x, 1 - p.c, p.a, p.b)
+        remote(sib_out.at[o], sib_in.at[o], sib_send, sib_recv.at[o], sibling)
+
+    def fast_input_grad(kind, rank):
+        R.fast_grad_box[kind] = (frame_grad(rank) + lateral_grad(rank)) * mask_ref[...]
+
+    fast_input_grad(SENT, partner)
     hand_over(FAST_GRAD)
-
-    arrived(sib_in, sib_recv)
-    for o, target in enumerate(targets[1:], 1):
-        far_out[o] = (window_of(p.c, target) + sib_in[o].astype(f32)).astype(bf16)
-        device = p.dev(p.off_x(target[0]), p.c, p.a, p.off_b(target[1]))
-        remote(far_out.at[o], far_in.at[o], far_send, far_recv, device)
+    for o in order:
+        arrived(sib_in.at[o], sib_recv.at[o])
+        both = window_of(0, o) + sib_in[o].astype(f32)
+        if o:
+            far_out[o] = both.astype(bf16)
+            x, b = p.off_x(targets[o][0]), p.off_b(targets[o][1])
+            remote(far_out.at[o], far_in.at[o], far_send, far_recv, p.dev(x, p.c, p.a, b))
+        else:
+            total = both
+    complete(FAST_OUT)
+    slow_result(MINE, p.mp)
+    complete(SLOW_OUT)
+    slow_input_grad(MINE, p.mp)
     complete(SLOW_GRAD)
+    fast_input_grad(MINE, p.mp)
     complete(FAST_GRAD)
-    total = window_of(p.c, targets[0]) + sib_in[0].astype(f32)
     arrived(far_in.at[pl.ds(1, len(targets) - 1)], far_recv)
     for o in range(1, len(targets)):
         total = total + far_in[o].astype(f32)
     R.end_grad[...] = total
     deliver(R.end_grad, 4)
+    deliver(R.info, 5)
 
     sent = len(p_sends)
     while sent:
@@ -1171,38 +1206,35 @@
         sent -= n
     for each in (x_gather, xs_gather, fc_gather, sc_gather):
         each.drain()
-    for which in range(EXCHANGES):
-        ref, at = stat(which)
-        arrived(ref.at[at, pl.ds(0, members - 1)], R.ex_send.at[which])
-    for which in range(len(boxes)):
-        arrived(box(which, SENT), R.box_send.at[which])
+    arrived(flat_ref.at[pl.ds(0, (members - 1) * (12 * 8 + 2 * 16))], R.ex_send)
+    arrived(flat_ref.at[pl.ds(0, 2 * HALF + 2 * slow_rows)], R.box_send)
     arrived(sib_out, sib_send)
     arrived(far_out.at[pl.ds(1, len(targets) - 1)], far_send)
     for copy in deliveries:
         copy.wait()
 
 
-def call_main(cfg, crop, owner, padded, master, fast, slow, fcot, scot):
+def call_main(cfg, crop, owner, master, fast, slow, fcot, scot):
     smem = pl.BlockSpec(memory_space=pltpu.SMEM)
     hbm = pl.BlockSpec(memory_space=pltpu.HBM)
     outs = outputs(cfg)
     return pl.pallas_call(
         functools.partial(main_kernel, cfg),
         out_shape=tuple(jax.ShapeDtypeStruct(s, t) for s, t in outs),
-        in_specs=[smem] + [hbm] * 7,
+        in_specs=[smem] + [hbm] * 6,
         out_specs=tuple(hbm for _ in outs),
         scratch_shapes=list(scratch(cfg).values()),
         compiler_params=pltpu.CompilerParams(
             collective_id=0, has_side_effects=True, vmem_limit_bytes=62 << 20
         ),
         name="block",
-    )(crop, owner, padded, master, fast, slow, fcot, scot)[:5]
+    )(crop, owner, master, fast, slow, fcot, scot)[:6]
 
 
 def adam_kernel(cfg, *refs):
     nd, nm, frames, slow_frames, share, slots = cfg
     inputs, results, (sems, *held) = refs[:9], refs[9:17], refs[17:]
-    owner_ref, grad, master, one, two = held[:5]
+    run, grad, master, one, two = held[:5]
     w_out, one_out, two_out, low_out = held[9:]
     fetches = [
         pltpu.make_async_copy(source, target, sems.at[i])
@@ -1214,18 +1246,8 @@
         pltpu.make_async_copy(source, target, sems.at[9 + i])
         for i, (source, target) in enumerate(zip(held[9:] + held[5:9], results, strict=True))
     ]
-    me = lax.axis_index("dp") * nm + lax.axis_index("mp")
-    spot = lax.broadcasted_iota(jnp.int32, (8, BLK), 0) * BLK
-    spot = spot + lax.broadcasted_iota(jnp.int32, (8, BLK), 1)
-    lowest = jnp.full((8, BLK), NBLK, jnp.int32)
-    number = jnp.zeros((8, BLK), jnp.int32)
     fetches[0].wait()
-    for i in range(up(NBLK, 1024) // 1024):
-        block = spot + i * 1024
-        mine = (owner_ref[i * 8 : (i + 1) * 8, :] == me) & (block < NBLK)
-        lowest = jnp.minimum(lowest, jnp.where(mine, block, NBLK))
-        number = number + jnp.where(mine, 1, 0)
-    start, count = jnp.min(lowest), jnp.sum(number)
+    start, count = run[0:1, :], run[1:2, :]
     row = lax.broadcasted_iota(jnp.int32, (slots, BLK), 0)
     living = row < count
     block = row + start
@@ -1264,8 +1286,8 @@
         copy.wait()
 
 
-def call_adam(cfg, owner, grad, master, one, two, passed):
-    arrays = (owner, grad, master, one, two, *passed)
+def call_adam(cfg, run, grad, master, one, two, passed):
+    arrays = (run, grad, master, one, two, *passed)
     hbm = pl.BlockSpec(memory_space=pltpu.HBM)
     new = [jax.ShapeDtypeStruct(master.shape, t) for t in (f32, f32, f32, bf16)]
     results = new + [jax.ShapeDtypeStruct(a.shape, a.dtype) for a in passed]
@@ -1292,19 +1314,17 @@
             split = array.reshape(share, slow_frames, POS // BLK, BLK)
             return split.transpose(0, 2, 1, 3).reshape(-1, BLK)
 
-        padded = jnp.pad(owner, (0, up(NBLK, 1024) - NBLK)).reshape(-1, BLK)
-        *passed, grad = call_main(
+        *passed, grad, run = call_main(
             cfg,
             crop,
             owner,
-            padded,
             master,
             fast_in.reshape(C_FAST, POS),
             halves(slow_in),
             fast_cot.reshape(C_FAST, POS),
             halves(slow_cot),
         )
-        new = call_adam(cfg, padded, grad, master, one, two, passed)
+        new = call_adam(cfg, run, grad, master, one, two, passed)
         return (
             new[4].reshape(fast_in.shape),
             new[5].reshape(slow_in.shape),

time: 88.2 us -> 81.1 us (0.920)
  Pallas kernels: 85.3 us -> 79.6 us
  local copies, waits for them, and re-layouts: 1.38 us -> 0 us
    pallas_call x1, Pallas kernels: 82.5 us -> 76.7 us  [call_main(): pl.pallas_call(functools.partial(main_kernel, cfg), out_shape=tuple((jax....]
    reshape x1 -> x0, local copies, waits for them, and re-layouts: 1.38 us -> none  [local(): padded = jnp.pad(owner, (0, up(NBLK, 1024) - NBLK)).reshape(-1, BLK)]
where the time goes in v4:
time: 81.1 us; the launch traced here: 80.9 us
  Pallas kernels  79.6 us (98%)
  between operations  1.29 us (2%)
    pallas_call x1, Pallas kernels, call_main(): pl.pallas_call(functools.partial(main_kernel, cfg), out_shape=tuple((jax....  76.7 us
    pallas_call x1, Pallas kernels, call_adam(): pl.pallas_call(functools.partial(adam_kernel, cfg), out_shape=tuple(resul...  2.86 us

profile of v4, /device:TPU:25, one launch (start us, length us, event | category | flops | bytes accessed | tf_op | source)
XLA Modules:
  0.0 80.9 jit_solution(14291961200974803463)
XLA Ops:
  1.3 76.7 %block.1 = (f32[256,128]{1,0:T(8,128)}, f32[512,128]{1,0:T(8,128)}, f32[256,128]{1,0:T(8,128)}, f32[512,128]{1,0:T(8,128)}, f32[480,128]{1,0:T(8,128)}, /*index=5*/s32[8,128]{1,0:T(8,128)}) custom-call(s32[1]{0:T(128)S(6)} %copy.23.refs_0_, s32[7591]{0:T(1024)} %refs_1_.1, f32[476,128]{1,0:T(8,128)} %refs_2_.3, bf16[128,256]{1,0:T(8,128)(2,1)} %bitcast.18, ...), custom_call_target="tpu_custom_call" | custom-call | tf_op jit(solution)/shard_map/block/pallas_call | solution.py:1221
  78.0 2.9 %adam.1 = (f32[476,128]{1,0:T(8,128)}, f32[476,128]{1,0:T(8,128)}, f32[476,128]{1,0:T(8,128)}, bf16[476,128]{1,0:T(8,128)(2,1)}, f32[256,128]{1,0:T(8,128)}, /*i...) custom-call(s32[8,128]{1,0:T(8,128)} %get-tuple-element.22.refs_0_, ...), custom_call_target="tpu_custom_call" | custom-call | tf_op jit(solution)/shard_map/adam/pallas_call | solution.py:1295

commit v5 on v4

--- a/solution.py
+++ b/solution.py
@@ -185,7 +185,7 @@
     halves = POS // BLK
     fast, slow = (C_FAST * halves, BLK), (share * slow_frames * halves, BLK)
     result = [(fast, f32), (slow, f32), (fast, f32), (slow, f32), ((up(slots, 16), BLK), f32)]
-    result += [((8, BLK), jnp.int32)]
+    result += [((8, BLK), jnp.int32)] + [((slots, BLK), f32)] * 3
     if share != BLK:
         result += [((nm, share, slow_frames * HALF), bf16)] * 2
     return result
@@ -209,7 +209,6 @@
         run_start=smem((devices,), jnp.int32),
         run_count=smem((devices,), jnp.int32),
         win_start=smem((group,), jnp.int32),
-        info=vmem((8, BLK), jnp.int32),
         table_v=vmem((8, BLK), jnp.int32),
         table_s=smem((8, BLK), jnp.int32),
         shift=vmem((rows + 16, BLK), f32),
@@ -286,11 +285,6 @@
         slow_out_box=vmem((3, slow_rows, BLK), f32),
         fast_grad_box=vmem((3, HALF, BLK), f32),
         slow_grad_box=vmem((3, slow_rows, BLK), f32),
-        fast_out_end=vmem((C_FAST * halves, BLK), f32),
-        slow_out_end=vmem((share * slow_frames * halves, BLK), f32),
-        fast_grad_end=vmem((C_FAST * halves, BLK), f32),
-        slow_grad_end=vmem((share * slow_frames * halves, BLK), f32),
-        end_grad=vmem((height, BLK), f32),
         p_send=dma(()),
         p_recv=dma((devices // 2,)),
         p_sibling=dma(()),
@@ -309,8 +303,8 @@
 def main_kernel(cfg, *refs):
     nd, nm, frames, slow_frames, share, slots = cfg
     n_out = len(outputs(cfg))
-    args, results, held = refs[:7], refs[7 : 7 + n_out], refs[7 + n_out :]
-    crop_in, owner_in, master_in, fast_in, slow_in, fcot_in, scot_in = args
+    args, results, held = refs[:9], refs[9 : 9 + n_out], refs[9 + n_out :]
+    crop_in, owner_in, master_in, first_in, second_in, fast_in, slow_in, fcot_in, scot_in = args
     R = types.SimpleNamespace(**dict(zip(scratch(cfg), held, strict=True)))
     p = Place(nd, nm)
     devices = nd * nm
@@ -353,6 +347,7 @@
     get_slow = fetch(slow_in, R.slow_v)
     get_fcot = fetch(fcot_in, R.fcot_v)
     get_scot = fetch(scot_in, R.scot_v)
+    kept = [fetch(a, results[6 + i]) for i, a in enumerate((master_in, first_in, second_in))]
 
     crop = crop_in[0]
     R.mask_all[...] = position_mask(crop)
@@ -392,7 +387,7 @@
     found = jnp.min(lowest), jnp.sum(number)
     my_start, my_count = lax.fori_loop(NBLK // BLK * BLK, NBLK, last_ones, found)
     line = lax.broadcasted_iota(jnp.int32, (8, BLK), 0)
-    R.info[...] = jnp.where(line == 0, my_start, my_count)
+    results[5][...] = jnp.where(line == 0, my_start, my_count)
     shift = lax.rem(my_start, 16)
     get_master.wait()
     moved = R.shift[pl.ds(16 - shift, rows), :]
@@ -493,8 +488,8 @@
 
     x_gather = gather(0, xt_ref, R.x_other, 2)
     fc_gather = gather(1, fc_ref, R.fc_other)
-    xs_gather = gather(2, xs_ref if slabs else results[6], R.xs_other)
-    sc_gather = gather(3, sc_ref if slabs else results[7], R.sc_other)
+    xs_gather = gather(2, xs_ref if slabs else results[9], R.xs_other)
+    sc_gather = gather(3, sc_ref if slabs else results[10], R.sc_other)
     get_fast.wait()
     own_frame(x_gather.view(p.mp), R.x_other, R.fast_v)
     x_gather.start()
@@ -570,6 +565,7 @@
     sc_gather.start()
     arrived(p_ref.at[pl.ds(0, devices // 2 * tiles)], R.p_sibling)
     get_table.wait()
+    sc_gather.relay()
 
     def tile_rows(t):
         return pl.ds(pl.multiple_of(t * 16, 16), 16)
@@ -772,10 +768,10 @@
         return jnp.concatenate([ref[j, at, :] for j in range(SLABS)], 1)
 
     boxes = (
-        (R.fast_out_box, R.fast_out_end),
-        (R.slow_out_box, R.slow_out_end),
-        (R.fast_grad_box, R.fast_grad_end),
-        (R.slow_grad_box, R.slow_grad_end),
+        (R.fast_out_box, results[0]),
+        (R.slow_out_box, results[1]),
+        (R.fast_grad_box, results[2]),
+        (R.slow_grad_box, results[3]),
     )
 
     def box(which, kind):
@@ -784,14 +780,6 @@
     def hand_over(which):
         box_sems = R.box_send, R.box_recv.at[which]
         remote(box(which, SENT), box(which, GOT), *box_sems, (p.dp, partner))
-
-    deliveries = []
-
-    def deliver(source, which):
-        sem = R.local.at[len(local_copies) + len(deliveries)]
-        copy = pltpu.make_async_copy(source, results[which], sem)
-        copy.start()
-        deliveries.append(copy)
 
     def to_channels(block):
         turned = block.T
@@ -814,7 +802,6 @@
                 block = jnp.where(p.b == h, ref[MINE, at, :], ref[GOT, at, :])
                 block = block.T if fast else to_channels(block)
                 end[pl.ds(s * halves + h, block.shape[0], stride=n * halves), :] = block
-        deliver(end, which)
 
     for s in range(slow_frames):
         for k in range(5):
@@ -847,13 +834,11 @@
     put_folded(EX_F1, *sums_of(a1p, group_rows, BLK))
     fill(EX_F1, 2, area)
     exchange(EX_F1)
-    sc_gather.relay()
-    fc_gather.start()
 
     matrix(s1_w, AT_S1, B_SLOW, 10)
     xs_gather.finish()
     if not slabs:
-        from_natural(results[6], xs_ref)
+        from_natural(results[9], xs_ref)
 
     for at in slow_chunks:
         c1[at, :] = dot_nt(all_slabs(xs_ref, at), s1_w[:, :C_SLOW])
@@ -872,7 +857,7 @@
     exchange(EX_S1)
 
     matrix(s2_w, AT_S2, B_SLOW, 6)
-    fc_gather.relay()
+    fc_gather.start()
     matrix(s3_w, AT_S3, C_SLOW, 2)
 
     packed = vec_ref[0:1, :]
@@ -905,6 +890,8 @@
     put_pair(EX_S2, *sums_of(c2, slow_rows, B_SLOW))
     fill(EX_S2, 4, 0.0)
     exchange(EX_S2)
+
+    fc_gather.relay()
 
     f2_norm = affine(*exchanged_two(EX_F2), fast_count, spread(2), spread(3))
     activate(a2p, h2p, group_rows, BLK, f2_norm[2], f2_norm[3])
@@ -938,7 +925,7 @@
     hand_over(FAST_OUT)
     sc_gather.finish()
     if not slabs:
-        from_natural(results[7], sc_ref)
+        from_natural(results[10], sc_ref)
     total = exchanged(EX_S3)
     s3_norm = affine(row_of(total, 0, 8), row_of(total, 8, 8), slow_count8, *vectors(V_S3))
 
@@ -1195,58 +1182,52 @@
     arrived(far_in.at[pl.ds(1, len(targets) - 1)], far_recv)
     for o in range(1, len(targets)):
         total = total + far_in[o].astype(f32)
-    R.end_grad[...] = total
-    deliver(R.end_grad, 4)
-    deliver(R.info, 5)
+    results[4][...] = total
 
     sent = len(p_sends)
     while sent:
         n = min(sent, devices)
         arrived(p_ref.at[pl.ds(0, n * tiles)], R.p_send)
         sent -= n
+    for copy in kept:
+        copy.wait()
     for each in (x_gather, xs_gather, fc_gather, sc_gather):
         each.drain()
     arrived(flat_ref.at[pl.ds(0, (members - 1) * (12 * 8 + 2 * 16))], R.ex_send)
     arrived(flat_ref.at[pl.ds(0, 2 * HALF + 2 * slow_rows)], R.box_send)
     arrived(sib_out, sib_send)
     arrived(far_out.at[pl.ds(1, len(targets) - 1)], far_send)
-    for copy in deliveries:
-        copy.wait()
-
-
-def call_main(cfg, crop, owner, master, fast, slow, fcot, scot):
+
+
+def call_main(cfg, *args):
     smem = pl.BlockSpec(memory_space=pltpu.SMEM)
     hbm = pl.BlockSpec(memory_space=pltpu.HBM)
+    vmem = pl.BlockSpec(memory_space=pltpu.VMEM)
     outs = outputs(cfg)
     return pl.pallas_call(
         functools.partial(main_kernel, cfg),
-        out_shape=tuple(jax.ShapeDtypeStruct(s, t) for s, t in outs),
-        in_specs=[smem] + [hbm] * 6,
-        out_specs=tuple(hbm for _ in outs),
+        out_shape=tuple((pltpu.VMEM if i < 9 else jax.ShapeDtypeStruct)(s, t) for i, (s, t) in enumerate(outs)),
+        in_specs=[smem] + [hbm] * 8,
+        out_specs=(vmem,) * 9 + (hbm,) * (len(outs) - 9),
         scratch_shapes=list(scratch(cfg).values()),
         compiler_params=pltpu.CompilerParams(
-            collective_id=0, has_side_effects=True, vmem_limit_bytes=62 << 20
+            collective_id=0, has_side_effects=True, vmem_limit_bytes=56 << 20
         ),
         name="block",
-    )(crop, owner, master, fast, slow, fcot, scot)[:6]
+    )(*args)[:9]
 
 
 def adam_kernel(cfg, *refs):
     nd, nm, frames, slow_frames, share, slots = cfg
-    inputs, results, (sems, *held) = refs[:9], refs[9:17], refs[17:]
-    run, grad, master, one, two = held[:5]
-    w_out, one_out, two_out, low_out = held[9:]
-    fetches = [
+    inputs, results, sems, held = refs[:9], refs[9:17], refs[17], refs[18:]
+    run, grad, master, one, two = inputs[:5]
+    w_out, one_out, two_out, low_out = held
+    stores = [
         pltpu.make_async_copy(source, target, sems.at[i])
-        for i, (source, target) in enumerate(zip(inputs, held[:9], strict=True))
+        for i, (source, target) in enumerate(zip(held + inputs[5:], results, strict=True))
     ]
-    for copy in fetches:
+    for copy in stores[4:]:
         copy.start()
-    stores = [
-        pltpu.make_async_copy(source, target, sems.at[9 + i])
-        for i, (source, target) in enumerate(zip(held[9:] + held[5:9], results, strict=True))
-    ]
-    fetches[0].wait()
     start, count = run[0:1, :], run[1:2, :]
     row = lax.broadcasted_iota(jnp.int32, (slots, BLK), 0)
     living = row < count
@@ -1262,12 +1243,6 @@
     ):
         rate = jnp.where(block < at, 0.5 / math.sqrt(width), rate)
     decay = jnp.where(block < AT_VEC, decay_rate, 0.0)
-    for copy in fetches[5:]:
-        copy.wait()
-    for copy in stores[4:]:
-        copy.start()
-    for copy in fetches[1:5]:
-        copy.wait()
     g = grad[:slots, :]
     first = beta_first * one[...] + (1.0 - beta_first) * g
     second = beta_second * two[...] + (1.0 - beta_second) * g * g
@@ -1289,16 +1264,19 @@
 def call_adam(cfg, run, grad, master, one, two, passed):
     arrays = (run, grad, master, one, two, *passed)
     hbm = pl.BlockSpec(memory_space=pltpu.HBM)
+    vmem = pl.BlockSpec(memory_space=pltpu.VMEM)
     new = [jax.ShapeDtypeStruct(master.shape, t) for t in (f32, f32, f32, bf16)]
     results = new + [jax.ShapeDtypeStruct(a.shape, a.dtype) for a in passed]
-    held = [pltpu.VMEM(a.shape, a.dtype) for a in (*arrays, *new)]
     return pl.pallas_call(
         functools.partial(adam_kernel, cfg),
         out_shape=tuple(results),
-        in_specs=[hbm] * len(arrays),
+        in_specs=[vmem] * len(arrays),
         out_specs=(hbm,) * len(results),
-        scratch_shapes=[pltpu.SemaphoreType.DMA((len(arrays) + len(results),)), *held],
-        compiler_params=pltpu.CompilerParams(vmem_limit_bytes=62 << 20),
+        scratch_shapes=[
+            pltpu.SemaphoreType.DMA((len(results),)),
+            *[pltpu.VMEM(a.shape, a.dtype) for a in new],
+        ],
+        compiler_params=pltpu.CompilerParams(vmem_limit_bytes=16 << 20),
         name="adam",
     )(*arrays)
 
@@ -1314,11 +1292,13 @@
             split = array.reshape(share, slow_frames, POS // BLK, BLK)
             return split.transpose(0, 2, 1, 3).reshape(-1, BLK)
 
-        *passed, grad, run = call_main(
+        *passed, grad, run, master, one, two = call_main(
             cfg,
             crop,
             owner,
             master,
+            one,
+            two,
             fast_in.reshape(C_FAST, POS),
             halves(slow_in),
             fast_cot.reshape(C_FAST, POS),

time: 81.1 us -> 78 us (0.962)
  Pallas kernels: 79.6 us -> 76.1 us
    pallas_call x1, Pallas kernels: 76.7 us -> 74.7 us  [call_main(): pl.pallas_call(functools.partial(main_kernel, cfg), out_shape=tuple(((plt...]
    pallas_call x1, Pallas kernels: 2.86 us -> 1.39 us  [call_adam(): pl.pallas_call(functools.partial(adam_kernel, cfg), out_shape=tuple(resul...]
where the time goes in v5:
time: 78 us; the launch traced here: 77.4 us
  Pallas kernels  76.1 us (98%)
  between operations  1.29 us (2%)
    pallas_call x1, Pallas kernels, call_main(): pl.pallas_call(functools.partial(main_kernel, cfg), out_shape=tuple(((plt...  74.7 us

profile of v5, /device:TPU:25, one launch (start us, length us, event | category | flops | bytes accessed | tf_op | source)
XLA Modules:
  0.0 77.4 jit_solution(2574428553830201130)
XLA Ops:
  1.3 74.7 %block.1 = (f32[256,128]{1,0:T(8,128)S(1)}, f32[512,128]{1,0:T(8,128)S(1)}, f32[256,128]{1,0:T(8,128)S(1)}, f32[512,128]{1,0:T(8,128)S(1)}, f32[480,128]{1,0:T(8...) custom-call(s32[1]{0:T(128)S(6)} %copy.23.refs_0_, ...), custom_call_target="tpu_custom_call" | custom-call | tf_op jit(solution)/shard_map/block/pallas_call | solution.py:1207
  76.0 1.4 %adam.1 = (f32[476,128]{1,0:T(8,128)}, f32[476,128]{1,0:T(8,128)}, f32[476,128]{1,0:T(8,128)}, bf16[476,128]{1,0:T(8,128)(2,1)}, f32[256,128]{1,0:T(8,128)}, /*i...) custom-call(s32[8,128]{1,0:T(8,128)S(1)} %get-tuple-element.25.refs_0_, ...), custom_call_target="tpu_custom_call" | custom-call | tf_op jit(solution)/shard_map/adam/pallas_call | solution.py:1270

commit v6 on v5

--- a/solution.py
+++ b/solution.py
@@ -164,11 +164,62 @@
         arrived(self.view(rank), near)
         self.along(rank)
 
+    def pass_on(self, i):
+        pass
+
     def finish(self):
         arrived(self.slabs.at[pl.ds(0, (self.p.na - 1) * self.p.nb)], self.sems[2])
 
     def drain(self):
         arrived(self.slabs.at[pl.ds(0, self.p.nm - 1)], self.sems[0])
+
+
+class TreeGather(Gather):
+    def __init__(self, place, slabs, other, skip, send, near, mate, *more):
+        super().__init__(place, slabs, other, skip, send, near, mate)
+        self.cross, self.relayed = more[:2], more[2]
+        a = place.a
+        self.inner = (a == 1) | (a == 2)
+        self.mate = a + 1 - 2 * lax.rem(a, 2)
+        self.over_there = 2 - a // 2
+        self.other_half = 2 - a // 2 * 2
+
+    def along(self, rank, i=0):
+        p, piece = self.p, self.view(rank)
+        for a, recv in ((self.mate, self.sems[2]), (self.over_there, self.cross[i])):
+            remote(piece, piece, self.sems[0], recv, (p.dp, a * p.nb + p.b))
+
+    def relay(self):
+        p = self.p
+        rank = p.a * p.nb + p.off_b(1)
+        arrived(self.view(rank), self.sems[1])
+        self.along(rank, 1)
+
+    def pass_on(self, i):
+        p = self.p
+
+        @pl.when(self.inner)
+        def _():
+            arrived(self.slabs.at[pl.ds(0, 2)], self.cross[i])
+            for k in range(2):
+                piece = self.view((self.other_half + k) * p.nb + p.off_b(i))
+                to = (p.dp, self.mate * p.nb + p.b)
+                remote(piece, piece, self.relayed, self.cross[i], to)
+
+    def finish(self):
+        arrived(self.slabs.at[pl.ds(0, self.p.nb)], self.sems[2])
+
+        @pl.when(~self.inner)
+        def _():
+            for cross in self.cross:
+                arrived(self.slabs.at[pl.ds(0, 2)], cross)
+
+    def drain(self):
+        arrived(self.slabs.at[pl.ds(0, 1 + 2 * self.p.nb)], self.sems[0])
+
+        @pl.when(self.inner)
+        def _():
+            arrived(self.slabs.at[pl.ds(0, 2 * self.p.nb)], self.relayed)
 
 
 EX_LAT, EX_S1, EX_S2, EX_B2, EX_B1, EX_BLAT = range(6)
@@ -288,7 +339,7 @@
         p_send=dma(()),
         p_recv=dma((devices // 2,)),
         p_sibling=dma(()),
-        gather_sems=dma((4, 3)),
+        gather_sems=dma((4, 6)),
         ex_send=dma(()),
         ex_recv=dma((EXCHANGES,)),
         box_send=dma(()),
@@ -482,14 +533,15 @@
 
         lax.fori_loop(0, slow_frames * SLABS, block, 0)
 
-    def gather(which, array, other, skip=0):
-        sems = [R.gather_sems.at[which, i] for i in range(3)]
-        return Gather(p, array, other, skip, *sems)
-
-    x_gather = gather(0, xt_ref, R.x_other, 2)
-    fc_gather = gather(1, fc_ref, R.fc_other)
-    xs_gather = gather(2, xs_ref if slabs else results[9], R.xs_other)
-    sc_gather = gather(3, sc_ref if slabs else results[10], R.sc_other)
+    def gather(kind, which, array, other, skip=0):
+        sems = [R.gather_sems.at[which, i] for i in range(3 if kind is Gather else 6)]
+        return kind(p, array, other, skip, *sems)
+
+    tree = TreeGather if p.na == 4 else Gather
+    x_gather = gather(tree, 0, xt_ref, R.x_other, 2)
+    fc_gather = gather(Gather, 1, fc_ref, R.fc_other)
+    xs_gather = gather(Gather, 2, xs_ref if slabs else results[9], R.xs_other)
+    sc_gather = gather(Gather, 3, sc_ref if slabs else results[10], R.sc_other)
     get_fast.wait()
     own_frame(x_gather.view(p.mp), R.x_other, R.fast_v)
     x_gather.start()
@@ -542,6 +594,8 @@
 
     R.table_v[...] = lax.fori_loop(0, devices, table, jnp.zeros((8, BLK), jnp.int32))
     get_table = fetch(R.table_v, R.table_s)
+    x_gather.pass_on(0)
+    x_gather.pass_on(1)
 
     across = p.na // 2
     for i in range(p.na):

time: 78 us -> 76.6 us (0.982)
  Pallas kernels: 76.1 us -> 74.7 us
    pallas_call x1, Pallas kernels: 74.7 us -> 73.3 us  [call_main(): pl.pallas_call(functools.partial(main_kernel, cfg), out_shape=tuple(((plt...]
where the time goes in v6:
time: 76.6 us; the launch traced here: 76 us
  Pallas kernels  74.7 us (98%)
  between operations  1.29 us (2%)
    pallas_call x1, Pallas kernels, call_main(): pl.pallas_call(functools.partial(main_kernel, cfg), out_shape=tuple(((plt...  73.3 us

profile of v6, /device:TPU:25, one launch (start us, length us, event | category | flops | bytes accessed | tf_op | source)
XLA Modules:
  0.0 76.0 jit_solution(17987379589178546400)
XLA Ops:
  1.3 73.3 %block.1 = (f32[256,128]{1,0:T(8,128)S(1)}, f32[512,128]{1,0:T(8,128)S(1)}, f32[256,128]{1,0:T(8,128)S(1)}, f32[512,128]{1,0:T(8,128)S(1)}, f32[480,128]{1,0:T(8...) custom-call(s32[1]{0:T(128)S(6)} %copy.23.refs_0_, ...), custom_call_target="tpu_custom_call" | custom-call | tf_op jit(solution)/shard_map/block/pallas_call | solution.py:1261
  74.6 1.4 %adam.1 = (f32[476,128]{1,0:T(8,128)}, f32[476,128]{1,0:T(8,128)}, f32[476,128]{1,0:T(8,128)}, bf16[476,128]{1,0:T(8,128)(2,1)}, f32[256,128]{1,0:T(8,128)}, /*i...) custom-call(s32[8,128]{1,0:T(8,128)S(1)} %get-tuple-element.25.refs_0_, ...), custom_call_target="tpu_custom_call" | custom-call | tf_op jit(solution)/shard_map/adam/pallas_call | solution.py:1324

commit v7 on v6

--- a/solution.py
+++ b/solution.py
@@ -611,12 +611,12 @@
     own_frame(fc_gather.view(p.mp), R.fc_other, R.fcot_v)
     get_scot.wait()
     own_slow(sc_gather.view(p.mp), R.sc_other, R.scot_v)
+    sc_gather.start()
     for i in range(p.na):
         for k in range(1, p.nx):
             source = (p.off_x(k), p.c, p.off_a(p.na - i), p.off_b(1))
             take(source)
             pass_on(source, along_c=True)
-    sc_gather.start()
     arrived(p_ref.at[pl.ds(0, devices // 2 * tiles)], R.p_sibling)
     get_table.wait()
     sc_gather.relay()

time: 76.6 us -> 75.3 us (0.983)
  Pallas kernels: 74.7 us -> 72.8 us
    pallas_call x1, Pallas kernels: 73.3 us -> 71.4 us  [call_main(): pl.pallas_call(functools.partial(main_kernel, cfg), out_shape=tuple(((plt...]
where the time goes in v7:
time: 75.3 us; the launch traced here: 74.1 us
  Pallas kernels  72.8 us (97%)
  between operations  1.29 us (2%)
    pallas_call x1, Pallas kernels, call_main(): pl.pallas_call(functools.partial(main_kernel, cfg), out_shape=tuple(((plt...  71.4 us

profile of v7, /device:TPU:25, one launch (start us, length us, event | category | flops | bytes accessed | tf_op | source)
XLA Modules:
  0.0 74.1 jit_solution(6930712884243090542)
XLA Ops:
  1.3 71.4 %block.1 = (f32[256,128]{1,0:T(8,128)S(1)}, f32[512,128]{1,0:T(8,128)S(1)}, f32[256,128]{1,0:T(8,128)S(1)}, f32[512,128]{1,0:T(8,128)S(1)}, f32[480,128]{1,0:T(8...) custom-call(s32[1]{0:T(128)S(6)} %copy.23.refs_0_, ...), custom_call_target="tpu_custom_call" | custom-call | tf_op jit(solution)/shard_map/block/pallas_call | solution.py:1261
  72.7 1.4 %adam.1 = (f32[476,128]{1,0:T(8,128)}, f32[476,128]{1,0:T(8,128)}, f32[476,128]{1,0:T(8,128)}, bf16[476,128]{1,0:T(8,128)(2,1)}, f32[256,128]{1,0:T(8,128)}, /*i...) custom-call(s32[8,128]{1,0:T(8,128)S(1)} %get-tuple-element.25.refs_0_, ...), custom_call_target="tpu_custom_call" | custom-call | tf_op jit(solution)/shard_map/adam/pallas_call | solution.py:1324

commit v8 on v7

--- a/solution.py
+++ b/solution.py
@@ -29,7 +29,7 @@
 MESH = pl.DeviceIdType.MESH
 f32 = jnp.float32
 bf16 = jnp.bfloat16
-RC = 32
+RC = 64
 CH = 256
 GROUPS = BLK // B_FAST
 COLUMNS = 2
@@ -339,14 +339,14 @@
         p_send=dma(()),
         p_recv=dma((devices // 2,)),
         p_sibling=dma(()),
-        gather_sems=dma((4, 6)),
+        gather_sems=dma((15,)),
         ex_send=dma(()),
         ex_recv=dma((EXCHANGES,)),
         box_send=dma(()),
         box_recv=dma((4,)),
         sum_sems=dma((3,)),
         sib_recv=dma((windows,)),
-        local=dma((16,)),
+        local=dma((11,)),
     )
     return result
 
@@ -534,7 +534,8 @@
         lax.fori_loop(0, slow_frames * SLABS, block, 0)
 
     def gather(kind, which, array, other, skip=0):
-        sems = [R.gather_sems.at[which, i] for i in range(3 if kind is Gather else 6)]
+        first = which * 3 + 3 if which else 0
+        sems = [R.gather_sems.at[first + i] for i in range(3 if kind is Gather else 6)]
         return kind(p, array, other, skip, *sems)
 
     tree = TreeGather if p.na == 4 else Gather
@@ -1206,7 +1207,7 @@
     def window_of(c, o):
         return flat_ref[pl.ds(R.win_start[c * len(targets) + o], height), :]
 
-    order = [*range(1, len(targets)), 0]
+    order = [*reversed(range(len(targets)))]
     for o in order:
         sib_out[o] = window_of(1, o).astype(bf16)
         sibling = p.dev(p.x, 1 - p.c, p.a, p.b)

time: 75.3 us -> 75.1 us (level)
  no operation moved by 1% of the time
where the time goes in v8:
time: 75.1 us; the launch traced here: 73.7 us
  Pallas kernels  72.4 us (96%)
  between operations  1.29 us (2%)
    pallas_call x1, Pallas kernels, call_main(): pl.pallas_call(functools.partial(main_kernel, cfg), out_shape=tuple(((plt...  71 us

profile of v8, /device:TPU:25, one launch (start us, length us, event | category | flops | bytes accessed | tf_op | source)
XLA Modules:
  0.0 73.7 jit_solution(9692647523120027621)
XLA Ops:
  1.3 71.0 %block.1 = (f32[256,128]{1,0:T(8,128)S(1)}, f32[512,128]{1,0:T(8,128)S(1)}, f32[256,128]{1,0:T(8,128)S(1)}, f32[512,128]{1,0:T(8,128)S(1)}, f32[480,128]{1,0:T(8...) custom-call(s32[1]{0:T(128)S(6)} %copy.23.refs_0_, ...), custom_call_target="tpu_custom_call" | custom-call | tf_op jit(solution)/shard_map/block/pallas_call | solution.py:1262
  72.3 1.4 %adam.1 = (f32[476,128]{1,0:T(8,128)}, f32[476,128]{1,0:T(8,128)}, f32[476,128]{1,0:T(8,128)}, bf16[476,128]{1,0:T(8,128)(2,1)}, f32[256,128]{1,0:T(8,128)}, /*i...) custom-call(s32[8,128]{1,0:T(8,128)S(1)} %get-tuple-element.25.refs_0_, ...), custom_call_target="tpu_custom_call" | custom-call | tf_op jit(solution)/shard_map/adam/pallas_call | solution.py:1325
